TPU v7x, 32 devices: a whole 2x2x4 slice. The times are simulated.
32 devices in a mesh: blk: 4 (over y, x), wide: 8 (over z, core).
Axes of the slice: x: 2, y: 2, z: 4, core: 2. Of those that a mesh axis runs over, the one named last changes fastest.
Arguments:
- upstream: bfloat16 [3072, 7168], P('wide'), may hold values from -8 to 8
- gate_pre: bfloat16 [3072, 1024], P('wide', 'blk'), may hold values from -6 to 6
- up_pre: bfloat16 [3072, 1024], P('wide', 'blk'), may hold values from -8 to 8
- down_weight: bfloat16 [7168, 2, 1024], P(None, None, 'blk'), may hold values from -0.1875 to 0.1875
- block_expert: int32 [24], P('wide'), may hold values from 0 to 1
- row_token: int32 [3072], P('wide'), may hold values from 0 to 383, as said below
- gate_prob: float32 [3072], P('wide'), may hold values from 0.05 to 0.8
Outputs:
- down_grad: float32 [7168, 2, 1024], P('wide', None, 'blk')
- grad_rms: float32 [2], replicated
- prob_grad: float32 [3072], P('wide')
- gate_grad: bfloat16 [3072, 1024], P('wide', 'blk')
- up_grad: bfloat16 [3072, 1024], P('wide', 'blk')
Inputs may be any that keep to these rules, and one draw needn't show every extreme that they name: Within each index of wide, row_token is a permutation of the 384 tokens held there: every token has exactly one routed row in the window.
All inputs are finite; a program needn't handle non-finite values.
Results may differ from a plain program's by a relative error of at most 0.0029.
Values sent between devices are 32-bit elements; how exact they have to be, the bound alone decides.
No kernel may reach another device: no remote copies, remote signals or barrier semaphores. Data moves between devices by JAX's collectives and lax.ppermute only.
A program may use at most 128 MiB of HBM per device.

v0:
```python
import jax
import jax.numpy as jnp
from jax import lax
from jax.sharding import PartitionSpec as P

D = 7168
FFW = 1024
EXPERTS = 2
BLOCK = 128


def body(upstream, gate_pre, up_pre, down_weight, block_expert, row_token, gate_prob):
    routed = upstream[row_token]
    row_count = routed.shape[0]
    block_count = row_count // BLOCK
    width = routed.shape[1]
    hidden_share = gate_pre.shape[1]
    gate_value = gate_pre.astype(jnp.float32)
    up_value = up_pre.astype(jnp.float32)
    sigmoid_gate = jax.nn.sigmoid(gate_value)
    active = gate_value * sigmoid_gate
    hidden = active * up_value
    weighted = (hidden * gate_prob[:, None]).astype(jnp.bfloat16)
    routed_blocks = routed.reshape(block_count, BLOCK, width)
    weighted_blocks = weighted.reshape(block_count, BLOCK, hidden_share)

    def project(block_item):
        rows_block, expert_id = block_item
        weights = lax.dynamic_index_in_dim(down_weight, expert_id, 1, keepdims=False)
        return jnp.dot(rows_block, weights, preferred_element_type=jnp.float32)

    projected = lax.map(project, (routed_blocks, block_expert)).reshape(row_count, hidden_share)
    scaled = gate_prob[:, None] * projected
    up_grad = (scaled * active).astype(jnp.bfloat16)
    gate_grad = (
        scaled * up_value * sigmoid_gate * (1.0 + gate_value * (1.0 - sigmoid_gate))
    ).astype(jnp.bfloat16)
    partial_value = jnp.sum(hidden * projected, axis=1)
    prob_grad = lax.psum(partial_value, "blk")
    row_share = width // lax.axis_size("wide")

    def select_columns(amount):
        return routed.reshape(block_count, BLOCK, amount)

    def block_product(columns, block_index):
        column_block = lax.dynamic_index_in_dim(columns, block_index, 0, keepdims=False)
        weighted_block = lax.dynamic_index_in_dim(weighted_blocks, block_index, 0, keepdims=False)
        return jnp.dot(column_block.T, weighted_block, preferred_element_type=jnp.float32)

    pieces = []
    for expert in range(EXPERTS):

        def one_expert(first, amount, expert=expert):
            columns = select_columns(amount)

            def add_block(block_index, running):
                expert_id = lax.dynamic_index_in_dim(block_expert, block_index, 0, keepdims=False)

                def with_block(running_sum):
                    return running_sum + block_product(columns, block_index)

                def without_block(running_sum):
                    return running_sum

                return lax.cond(expert_id == expert, with_block, without_block, running)

            start_value = jnp.zeros((amount, hidden_share), jnp.float32)
            return lax.fori_loop(0, block_count, add_block, start_value)

        pieces.append(
            lax.psum_scatter(
                one_expert(jnp.int32(0), lax.axis_size("wide") * row_share),
                "wide",
                scatter_dimension=0,
                tiled=True,
            )
        )
    down_grad = jnp.stack(pieces, axis=1)
    squares = jnp.sum(down_grad * down_grad, axis=(0, 2))
    total_sum = lax.psum(squares, ("blk", "wide"))
    grad_rms = jnp.sqrt(total_sum / float(D * FFW))
    return (down_grad, grad_rms, prob_grad, gate_grad, up_grad)


def solution(mesh):
    in_specs = (
        P("wide", None),
        P("wide", "blk"),
        P("wide", "blk"),
        P(None, None, "blk"),
        P("wide"),
        P("wide"),
        P("wide"),
    )
    out_specs = (P("wide", None, "blk"), P(), P("wide"), P("wide", "blk"), P("wide", "blk"))
    return jax.shard_map(body, mesh=mesh, in_specs=in_specs, out_specs=out_specs, check_vma=False)
```

profile of v0, /device:TPU:0, one launch (start us, length us, event | category | flops | bytes accessed | tf_op | source)
XLA Modules:
  0.0 293.2 jit_solution(3440205396377253287)
XLA Ops:
  7.2 0.0 reduce-scatter.3.cloned.1.call-start
  7.2 0.7 compare_select_fusion
  7.9 7.0 %copy.12 = bf16[7168,2,256]{2,0,1:T(8,128)(2,1)} copy(bf16[7168,2,256]{2,1,0:T(2,128)(2,1)} %param.20) | data formatting | bytes 14680064 | tf_op jit(solution)/shard_map/while | solution.py:32
  14.9 0.0 copy-start.3
  14.9 16.5 %gather_fusion = bf16[384,7168]{1,0:T(8,128)(2,1)} fusion(bf16[384,7168]{1,0:T(8,128)(2,1)} %param.17, s32[1024]{0:T(1024)S(1)} %pad_clamp_fusion), kind=kCustom, calls=%fused_computation | custom fusion | bytes 11011584 | tf_op jit(solution)/shard_map/gather | solution.py:13
  31.4 0.0 copy-done.3
  31.4 0.0 copy-start
  31.4 0.0 copy-start.1
  31.4 0.0 copy-start.2
  31.4 17.4 %while.44 = (s32[]{:T(128)}, f32[3,128,256]{2,1,0:T(8,128)S(1)}, bf16[3,128,7168]{2,1,0:T(8,128)(2,1)}, s32[3]{0:T(128)S(1)}, bf16[7168,2,256]{2,0,1:T(8,128)(2,1)}, /*index=5*/s32[]{:T(128)}, s32[]{:T(128)}, s32[]{:T(128)}) while((s32[]{:T(128)}, f32[3,128,256]{2,1,0:T(8,128)S(1)}, bf16[3,128,7168]{2,1,0:T(8,128)(2,1)}, s32[3]{0:T(128)S(1)}, ...), condition=%wide.region_13.14_spmd, body=%wide.region_12.13_spmd.sunk | while | flops 469762048 | bytes 5637255 | solution.py:32
  31.4 0.6 dynamic_slice.82
  33.9 3.2 %fusion.39 = f32[3,128,256]{2,1,0:T(8,128)S(1)} fusion(f32[3,128,256]{2,1,0:T(8,128)S(1)} %get-tuple-element.411, s32[]{:T(128)} %get-tuple-element.410, bf16[7168,2,256]{2,0,1:T(8,128)(2,1)} %get-tuple-element.422, s32[]{:T(128)S(6)} %select_n.31, bf16[3,128,7168]{2,1,0:T(8,128)(2,1)} %get-tuple-element.420), kind=kOutput, calls=%fused_computation.19.clone.1 | convolution fusion | flops 469762048 | bytes 5637124 | tf_op jit(solution)/shard_map/while/body/eval_jaxpr/dot_general | solution.py:30
  37.2 0.6 dynamic_slice.82
  39.7 3.2 %fusion.39 = f32[3,128,256]{2,1,0:T(8,128)S(1)} fusion(f32[3,128,256]{2,1,0:T(8,128)S(1)} %get-tuple-element.411, s32[]{:T(128)} %get-tuple-element.410, bf16[7168,2,256]{2,0,1:T(8,128)(2,1)} %get-tuple-element.422, s32[]{:T(128)S(6)} %select_n.31, bf16[3,128,7168]{2,1,0:T(8,128)(2,1)} %get-tuple-element.420), kind=kOutput, calls=%fused_computation.19.clone.1 | convolution fusion | flops 469762048 | bytes 5637124 | tf_op jit(solution)/shard_map/while/body/eval_jaxpr/dot_general | solution.py:30
  43.0 0.6 dynamic_slice.82
  45.5 3.2 %fusion.39 = f32[3,128,256]{2,1,0:T(8,128)S(1)} fusion(f32[3,128,256]{2,1,0:T(8,128)S(1)} %get-tuple-element.411, s32[]{:T(128)} %get-tuple-element.410, bf16[7168,2,256]{2,0,1:T(8,128)(2,1)} %get-tuple-element.422, s32[]{:T(128)S(6)} %select_n.31, bf16[3,128,7168]{2,1,0:T(8,128)(2,1)} %get-tuple-element.420), kind=kOutput, calls=%fused_computation.19.clone.1 | convolution fusion | flops 469762048 | bytes 5637124 | tf_op jit(solution)/shard_map/while/body/eval_jaxpr/dot_general | solution.py:30
  48.8 0.0 copy-done
  48.8 0.0 copy-done.1
  48.8 0.0 copy-done.2
  48.8 1.1 fusion.28
  49.9 3.5 %broadcast.11.clone.1 = f32[7168,256]{1,0:T(8,128)} broadcast(f32[]{:T(128)} %constant.89.clone.1), dimensions={} | broadcast | bytes 7340036 | tf_op jit(solution)/shard_map/broadcast.4
  53.4 3.8 %while.42 = (s32[]{:T(128)}, f32[7168,256]{1,0:T(8,128)}, s32[3]{0:T(128)S(1)}, bf16[3,128,7168]{2,1,0:T(8,128)(2,1)}, bf16[3,128,256]{2,1,0:T(8,128)(2,1)S(1)}, /*index=5*/s32[]{:T(128)}, s32[1]{0:T(128)}) while((s32[]{:T(128)}, f32[7168,256]{1,0:T(8,128)}, s32[3]{0:T(128)S(1)}, bf16[3,128,7168]{2,1,0:T(8,128)(2,1)}, ...), condition=%wide.region_3.4_spmd, body=%wide.region_0.3_spmd.sunk | while | flops 471597056 | bytes 16581809 | solution.py:68
  53.4 0.6 dynamic_slice.78
  54.7 0.6 dynamic_slice.78
  55.9 0.6 dynamic_slice.78
  57.2 0.0 reduce-scatter.3.cloned.1.call-update
  57.2 0.2 reduce-scatter.5.cloned.1.call-start
  57.4 3.4 %broadcast.11.clone = f32[7168,256]{1,0:T(8,128)} broadcast(f32[]{:T(128)} %constant.89.clone.1), dimensions={} | broadcast | bytes 7340036 | tf_op jit(solution)/shard_map/broadcast.4
  60.9 27.1 %while.43 = (s32[]{:T(128)}, f32[7168,256]{1,0:T(8,128)}, s32[3]{0:T(128)S(1)}, bf16[3,128,7168]{2,1,0:T(8,128)(2,1)}, bf16[3,128,256]{2,1,0:T(8,128)(2,1)S(1)}, /*index=5*/s32[]{:T(128)}, s32[1]{0:T(128)}) while((s32[]{:T(128)}, f32[7168,256]{1,0:T(8,128)}, s32[3]{0:T(128)S(1)}, bf16[3,128,7168]{2,1,0:T(8,128)(2,1)}, ...), condition=%wide.region_8.9_spmd, body=%wide.region_5.8_spmd.sunk | while | flops 471597056 | bytes 16581809 | solution.py:68
  60.9 0.6 dynamic_slice.79
  62.1 7.8 %conditional.5 = (f32[7168,256]{1,0:T(8,128)}) conditional(s32[]{:T(128)} %bitcast.53, f32[7168,256]{1,0:T(8,128)} %get-tuple-element.434, (s32[]{:T(128)}, bf16[3,128,7168]{2,1,0:T(8,128)(2,1)}, bf16[3,128,256]{2,1,0:T(8,128)(2,1)S(1)}, f32[7168,256]{1,0:T(8,128)}) %tuple.95), branch_computations={%region_6.6_spmd, %region_7.7_spmd} | conditional | flops 471597056 | bytes 16581674 | solution.py:65
  62.1 7.8 %convolution_add_fusion.1 = f32[7168,256]{1,0:T(8,128)} fusion(f32[7168,256]{1,0:T(8,128)} %get-tuple-element.236, bf16[3,128,7168]{2,1,0:T(8,128)(2,1)} %get-tuple-element.237, s32[]{:T(128)S(6)} %select_n.25, bf16[3,128,256]{2,1,0:T(8,128)(2,1)S(1)} %get-tuple-element.239), kind=kOutput, calls=%fused_computation.7 | convolution fusion | flops 471597056 | bytes 16581632 | tf_op jit(solution)/shard_map/while/body/eval_jaxpr/cond/branch_1_fun/dot_general | solution.py:48
  69.9 0.6 dynamic_slice.79
  71.1 7.8 %conditional.5 = (f32[7168,256]{1,0:T(8,128)}) conditional(s32[]{:T(128)} %bitcast.53, f32[7168,256]{1,0:T(8,128)} %get-tuple-element.434, (s32[]{:T(128)}, bf16[3,128,7168]{2,1,0:T(8,128)(2,1)}, bf16[3,128,256]{2,1,0:T(8,128)(2,1)S(1)}, f32[7168,256]{1,0:T(8,128)}) %tuple.95), branch_computations={%region_6.6_spmd, %region_7.7_spmd} | conditional | flops 471597056 | bytes 16581674 | solution.py:65
  71.2 7.8 %convolution_add_fusion.1 = f32[7168,256]{1,0:T(8,128)} fusion(f32[7168,256]{1,0:T(8,128)} %get-tuple-element.236, bf16[3,128,7168]{2,1,0:T(8,128)(2,1)} %get-tuple-element.237, s32[]{:T(128)S(6)} %select_n.25, bf16[3,128,256]{2,1,0:T(8,128)(2,1)S(1)} %get-tuple-element.239), kind=kOutput, calls=%fused_computation.7 | convolution fusion | flops 471597056 | bytes 16581632 | tf_op jit(solution)/shard_map/while/body/eval_jaxpr/cond/branch_1_fun/dot_general | solution.py:48
  78.9 0.6 dynamic_slice.79
  80.2 7.8 %conditional.5 = (f32[7168,256]{1,0:T(8,128)}) conditional(s32[]{:T(128)} %bitcast.53, f32[7168,256]{1,0:T(8,128)} %get-tuple-element.434, (s32[]{:T(128)}, bf16[3,128,7168]{2,1,0:T(8,128)(2,1)}, bf16[3,128,256]{2,1,0:T(8,128)(2,1)S(1)}, f32[7168,256]{1,0:T(8,128)}) %tuple.95), branch_computations={%region_6.6_spmd, %region_7.7_spmd} | conditional | flops 471597056 | bytes 16581674 | solution.py:65
  80.2 7.8 %convolution_add_fusion.1 = f32[7168,256]{1,0:T(8,128)} fusion(f32[7168,256]{1,0:T(8,128)} %get-tuple-element.236, bf16[3,128,7168]{2,1,0:T(8,128)(2,1)} %get-tuple-element.237, s32[]{:T(128)S(6)} %select_n.25, bf16[3,128,256]{2,1,0:T(8,128)(2,1)S(1)} %get-tuple-element.239), kind=kOutput, calls=%fused_computation.7 | convolution fusion | flops 471597056 | bytes 16581632 | tf_op jit(solution)/shard_map/while/body/eval_jaxpr/cond/branch_1_fun/dot_general | solution.py:48
  87.9 0.0 reduce-scatter.5.cloned.1.call-update
  88.0 11.9 %psum.15 = f32[384]{0:T(512)} all-reduce(f32[384]{0:T(512)S(1)} %get-tuple-element.306), channel_id=1, replica_groups=mesh['blk'=4,'wide'=8] {'blk'}, use_global_device_ids=true, to_apply=%region_15.16 | all-reduce | flops 384 | bytes 3072 | tf_op jit(solution)/shard_map/psum | solution.py:39
  99.9 63.3 %reduce-scatter.3.cloned.1.call-done = f32[896,256]{1,0:T(8,128)} async-done(((f32[7168,256]{1,0:T(8,128)}), f32[896,256]{1,0:T(8,128)}) %reduce-scatter.3.cloned.1.call-update) | async-done | bytes 917520 | tf_op jit(solution)/shard_map/reduce_scatter | solution.py:71
  163.2 80.4 %reduce-scatter.5.cloned.1.call-done = f32[896,256]{1,0:T(8,128)} async-done(((f32[7168,256]{1,0:T(8,128)}), f32[896,256]{1,0:T(8,128)}) %reduce-scatter.5.cloned.1.call-update) | async-done | bytes 917520 | tf_op jit(solution)/shard_map/reduce_scatter | solution.py:71
  243.6 1.8 multiply_reduce_fusion
  245.4 2.6 copy.13
  248.1 37.8 %psum.14 = f32[2]{0:T(128)S(1)} all-reduce(f32[2]{0:T(128)S(1)} %get-tuple-element.303), channel_id=1, replica_groups=mesh['blk'=4,'wide'=8] {'blk','wide'}, use_global_device_ids=true, to_apply=%region_11.12 | all-reduce | flops 2 | bytes 16 | tf_op jit(solution)/shard_map/psum | solution.py:80
  285.8 0.5 multiply_sqrt_fusion
  (5 shorter events, 0.0 us)
Async XLA Ops:
  7.2 156.0 %reduce-scatter.3.cloned.1.call-start = ((), (), s32[]{:S(2)}) async-start(), calls=%async_computation.2 | async-start | bytes 8257536 | tf_op jit(solution)/shard_map/reduce_scatter | solution.py:71
  14.9 16.5 %copy-start.3 = (s32[3]{0:T(128)S(1)}, s32[3]{0:T(128)}, u32[]{:S(2)}) copy-start(s32[3]{0:T(128)} %param.21) | copy-start | bytes 40
  31.4 17.4 %copy-start = (bf16[384,256]{1,0:T(8,128)(2,1)S(1)}, bf16[384,256]{1,0:T(8,128)(2,1)}, u32[]{:S(2)}) copy-start(bf16[384,256]{1,0:T(8,128)(2,1)} %param.19) | copy-start | bytes 589828
  31.4 17.4 %copy-start.1 = (bf16[384,256]{1,0:T(8,128)(2,1)S(1)}, bf16[384,256]{1,0:T(8,128)(2,1)}, u32[]{:S(2)}) copy-start(bf16[384,256]{1,0:T(8,128)(2,1)} %param.18) | copy-start | bytes 589828
  31.4 17.4 %copy-start.2 = (f32[384]{0:T(512)S(1)}, f32[384]{0:T(512)}, u32[]{:S(2)}) copy-start(f32[384]{0:T(512)} %param.23) | copy-start | bytes 4612
  57.2 186.4 %reduce-scatter.5.cloned.1.call-start = ((), (), s32[]{:S(2)}) async-start(), calls=%async_computation.3 | async-start | bytes 8257536 | tf_op jit(solution)/shard_map/reduce_scatter | solution.py:71
Sparse Core Ops, SparseCore 0:
  57.3 105.8 reduce-scatter.2
  165.5 78.0 reduce-scatter.4
where the time goes:
time: 294 us; the launch traced here: 293 us
  waiting for transfers between devices  144 us (49%)
  blocking collectives  49.7 us (17%)
  local copies, waits for them, and re-layouts  38.3 us (13%)
  matrix products  33 us (11%)
  between operations  14.1 us (5%)
  loops' own time  9.97 us (3%)
  other arithmetic  4.12 us (1%)
    reduce_scatter x2, waiting for transfers between devices, body(): lax.psum_scatter(one_expert(jnp.int32(0), lax.axis_size('wide') * row_sha...  144 us
    psum x1, blocking collectives, body(): total_sum = lax.psum(squares, ('blk', 'wide'))  37.8 us
    dot_general x3, matrix products, block_product(): jnp.dot(column_block.T, weighted_block, preferred_element_type=jnp.float32)  23.3 us
    gather x1, local copies, waits for them, and re-layouts, body(): routed = upstream[row_token]  16.5 us
    psum x1, blocking collectives, body(): prob_grad = lax.psum(partial_value, 'blk')  11.9 us
    dot_general x3, matrix products, project(): return jnp.dot(rows_block, weights, preferred_element_type=jnp.float32)  9.73 us
    while x1, local copies, waits for them, and re-layouts, body(): lax.map(project, (routed_blocks, block_expert))  6.99 us
    another operation x2, local copies, waits for them, and re-layouts  6.92 us
  transfers between devices with their start and end apart: 2, of which 2 were waited for; matrix products, arithmetic and copies ran while one was open for 10% of the time, Pallas kernels for 0%

commit v1 on v0

--- a/solution.py
+++ b/solution.py
@@ -1,15 +1,18 @@
 import jax
 import jax.numpy as jnp
 from jax import lax
+from jax.experimental import pallas as pl
+from jax.experimental.pallas import tpu as pltpu
 from jax.sharding import PartitionSpec as P
 
 D = 7168
 FFW = 1024
 EXPERTS = 2
 BLOCK = 128
-
-
-def body(upstream, gate_pre, up_pre, down_weight, block_expert, row_token, gate_prob):
+Z_ORDER = (1, 3, 2)
+
+
+def sums_body(upstream, gate_pre, up_pre, down_weight, block_expert, row_token, gate_prob):
     routed = upstream[row_token]
     row_count = routed.shape[0]
     block_count = row_count // BLOCK
@@ -82,7 +85,210 @@
     return (down_grad, grad_rms, prob_grad, gate_grad, up_grad)
 
 
+def add_products(parts, spots, right, total):
+    depth = right.shape[0]
+    share = parts[0].shape[-1]
+
+    def kernel(*refs):
+        part_refs, (right_ref, total_ref, out_ref, left) = refs[: len(parts)], refs[len(parts) :]
+        for part_ref, spot in zip(part_refs, spots):
+            if len(part_ref.shape) == 2:
+                left[spot : spot + part_ref.shape[0], :] = part_ref[...].astype(jnp.bfloat16)
+            else:
+                for one in range(part_ref.shape[0]):
+                    first = spot + one * (depth // part_ref.shape[0])
+                    left[first : first + part_ref.shape[1], :] = part_ref[one].astype(jnp.bfloat16)
+        weights = right_ref[...].astype(jnp.bfloat16)
+        for first in range(0, share, 128):
+            out_ref[first : first + 128, :] = total_ref[first : first + 128, :] + lax.dot_general(
+                left[:, first : first + 128],
+                weights,
+                (((0,), (0,)), ((), ())),
+                preferred_element_type=jnp.float32,
+            )
+
+    return pl.pallas_call(
+        kernel,
+        out_shape=jax.ShapeDtypeStruct(total.shape, jnp.float32),
+        in_specs=[pl.BlockSpec(memory_space=pltpu.VMEM)] * (len(parts) + 2),
+        out_specs=pl.BlockSpec(memory_space=pltpu.VMEM),
+        scratch_shapes=[pltpu.VMEM((depth, share), jnp.bfloat16)],
+        compiler_params=pltpu.CompilerParams(vmem_limit_bytes=24 * 1024 * 1024),
+        cost_estimate=pl.CostEstimate(
+            flops=2 * depth * share * right.shape[1],
+            bytes_accessed=4 * depth * (share + right.shape[1]) + 8 * share * right.shape[1],
+            transcendentals=0,
+        ),
+    )(*parts, right, total)
+
+
+def factors_body(upstream, gate_pre, up_pre, down_weight, block_expert, row_token, gate_prob):
+    rows, width = upstream.shape
+    hidden_share = gate_pre.shape[1]
+    columns = lax.axis_size("blk")
+    wide = lax.axis_size("wide")
+    chips = wide // 2
+    quarter = rows // columns
+    share = width // wide
+    blk_index = lax.axis_index("blk")
+    wide_index = lax.axis_index("wide")
+    chip = wide_index // 2
+    core = wide_index % 2
+
+    def moved(value, target):
+        pairs = []
+        for b in range(columns):
+            for z in range(chips):
+                for c in range(2):
+                    to = target(b, z, c)
+                    if to is not None:
+                        pairs.append((b * wide + z * 2 + c, to[0] * wide + to[1] * 2 + to[2]))
+        return lax.ppermute(value, ("blk", "wide"), pairs)
+
+    def along_x(value):
+        return moved(value, lambda b, z, c: (b ^ 1, z, c))
+
+    def along_y(value):
+        return moved(value, lambda b, z, c: (b ^ 2, z, c))
+
+    def across(value):
+        return moved(value, lambda b, z, c: (b, z, 1 - c))
+
+    def step_up(value):
+        return moved(value, lambda b, z, c: (b, z + 1, c) if z + 1 < chips else None)
+
+    def step_down(value):
+        return moved(value, lambda b, z, c: (b, z - 1, c) if z > 0 else None)
+
+    pieces = {}
+    previous = []
+    for offset in Z_ORDER:
+        pair = []
+        for flip in range(2):
+            first_column = share * (2 * ((chip + offset) % chips) + (core ^ flip))
+            piece = lax.dynamic_slice(upstream, (quarter * blk_index, first_column), (quarter, share))
+            piece = piece.astype(jnp.float32)
+            if len(previous) >= 2:
+                piece, _ = lax.optimization_barrier((piece, previous[-2]))
+            got = moved(
+                piece,
+                lambda b, z, c, offset=offset, flip=flip: (b, (z + offset) % chips, c ^ flip),
+            )
+            previous.append(got)
+            pair.append(got)
+        pieces[offset] = jnp.stack(pair)
+
+    gathered = {}
+    for offset in Z_ORDER:
+        own = pieces[offset]
+        from_x = along_x(own)
+        from_y = along_y(own)
+        half = quarter // 2
+        first = along_y(from_x[:, :half])
+        second = along_x(from_y[:, half:])
+        gathered[offset] = (own, from_x, from_y, first, second)
+
+    gate_value = gate_pre.astype(jnp.float32)
+    up_value = up_pre.astype(jnp.float32)
+    sigmoid_gate = jax.nn.sigmoid(gate_value)
+    active = gate_value * sigmoid_gate
+    hidden = active * up_value
+    weighted = (hidden * gate_prob[:, None]).astype(jnp.bfloat16)
+    expert_of_row = jnp.repeat(block_expert, BLOCK)
+
+    place = lax.iota(jnp.int32, rows)
+    token = quarter * (blk_index ^ (place // quarter)) + place % quarter
+    choose = token[:, None] == row_token[None, :]
+    weighted_tokens = jnp.dot(
+        choose.astype(jnp.bfloat16), weighted, preferred_element_type=jnp.float32
+    )
+    expert_of_token = jnp.sum(jnp.where(choose, expert_of_row[None, :], 0), axis=1)
+    lines = -(-rows // hidden_share)
+    marks = jnp.zeros((8 * hidden_share,), jnp.float32).at[:rows].set(expert_of_token.astype(jnp.float32))
+    factor = jnp.concatenate([weighted_tokens, marks.reshape(8, hidden_share)], axis=0)
+
+    def split_factor(value):
+        marked = value[rows : rows + lines].reshape(lines * hidden_share)[:rows]
+        weight = value[:rows]
+        sides = [jnp.where((marked == expert)[:, None], weight, 0.0) for expert in range(EXPERTS)]
+        return jnp.concatenate(sides, axis=1)
+
+    factor, _ = lax.optimization_barrier((factor, previous[-2]))
+    ups, downs = [], []
+    up_value_now, down_value_now = factor, factor
+    for _ in range(chips - 1):
+        up_value_now = step_up(up_value_now)
+        down_value_now = step_down(down_value_now)
+        ups.append(up_value_now)
+        downs.append(down_value_now)
+
+    def own_columns(of_core):
+        first_column = share * (2 * chip + of_core)
+        parts = [
+            lax.dynamic_slice(upstream, (quarter * (blk_index ^ q), first_column), (quarter, share))
+            for q in range(columns)
+        ]
+        return jnp.concatenate(parts, axis=0).astype(jnp.float32)
+
+    own_tokens = own_columns(core)
+    other_tokens = across(own_columns(1 - core))
+    other_factor = across(factor)
+
+    total = add_products(
+        (own_tokens, other_tokens),
+        (0, rows),
+        jnp.concatenate([split_factor(factor), split_factor(other_factor)], axis=0),
+        jnp.zeros((share, EXPERTS * hidden_share), jnp.float32),
+    )
+    spots = (0, quarter, 2 * quarter, 3 * quarter, 3 * quarter + quarter // 2)
+    for offset in Z_ORDER:
+        from_below = ups[offset - 1]
+        from_above = downs[chips - offset - 1]
+        here = from_below + from_above
+        there = across(here)
+        right = jnp.concatenate([split_factor(here), split_factor(there)], axis=0)
+        total = add_products(gathered[offset], spots, right, total)
+
+    down_grad = total.reshape(share, EXPERTS, hidden_share)
+    squares = jnp.sum(down_grad * down_grad, axis=(0, 2))
+    devices = columns * wide
+    padded = jnp.zeros((1, 128), jnp.float32).at[0, :EXPERTS].set(squares)
+    spread = lax.all_to_all(
+        jnp.broadcast_to(padded, (devices, 128)), ("blk", "wide"), 0, 0, tiled=True
+    )
+    total_sum = jnp.sum(spread, axis=0)[:EXPERTS]
+    grad_rms = jnp.sqrt(total_sum / float(D * FFW))
+
+    both = [
+        jnp.dot(upstream, down_weight[:, expert, :], preferred_element_type=jnp.float32)
+        for expert in range(EXPERTS)
+    ]
+    natural = row_token[:, None] == lax.iota(jnp.int32, rows)[None, :]
+    pick = natural.astype(jnp.float32)
+    rows_of = [jnp.dot(pick, one, precision=lax.Precision.HIGHEST) for one in both]
+    projected = jnp.where((expert_of_row == 0)[:, None], rows_of[0], rows_of[1])
+    scaled = gate_prob[:, None] * projected
+    up_grad = (scaled * active).astype(jnp.bfloat16)
+    gate_grad = (
+        scaled * up_value * sigmoid_gate * (1.0 + gate_value * (1.0 - sigmoid_gate))
+    ).astype(jnp.bfloat16)
+    partial_value = jnp.sum(hidden * projected, axis=1)
+    partial_value = partial_value + along_x(partial_value)
+    prob_grad = partial_value + along_y(partial_value)
+    return (down_grad, grad_rms, prob_grad, gate_grad, up_grad)
+
+
 def solution(mesh):
+    columns, wide = mesh.shape["blk"], mesh.shape["wide"]
+
+    def body(upstream, gate_pre, up_pre, down_weight, block_expert, row_token, gate_prob):
+        rows, width = upstream.shape
+        hidden_share = gate_pre.shape[1]
+        factors = wide * rows * (hidden_share + width // wide)
+        sums = EXPERTS * width * hidden_share
+        plan = factors_body if columns == 4 and wide == 8 and factors < sums else sums_body
+        return plan(upstream, gate_pre, up_pre, down_weight, block_expert, row_token, gate_prob)
+
     in_specs = (
         P("wide", None),
         P("wide", "blk"),

time: 294 us -> 161 us (0.55)
  waiting for transfers between devices: 144 us -> 62.1 us
  starting transfers between devices: 0.26 us -> 53.5 us
  blocking collectives: 49.7 us -> 0 us
  matrix products: 33 us -> 6.84 us
  local copies, waits for them, and re-layouts: 38.3 us -> 22.7 us
  between operations: 14.1 us -> 1.48 us
  loops' own time: 9.97 us -> 0 us
  other arithmetic: 4.12 us -> 10.4 us
  Pallas kernels: 0 us -> 3.88 us
    reduce_scatter x2 -> x0, waiting for transfers between devices: 144 us -> none  [body(): lax.psum_scatter(one_expert(jnp.int32(0), lax.axis_size('wide') * row_sha...]
    ppermute x0 -> x31, waiting for transfers between devices: none -> 62.1 us  [moved(): return lax.ppermute(value, ('blk', 'wide'), pairs)]
    psum x2 -> x0, blocking collectives: 49.7 us -> none  [the longest x1 37.8 us: body(): total_sum = lax.psum(squares, ('blk', 'wide'))]
    ppermute x0 -> x31, starting transfers between devices: none -> 48.9 us  [moved(): return lax.ppermute(value, ('blk', 'wide'), pairs)]
    dot_general x6 -> x5, matrix products: 33 us -> 6.84 us  [the longest x2 3.92 us: factors_body(): jnp.dot(upstream, down_weight[:, expert, :], preferred_element_type=jnp.f...]
    gather x1 -> x0, local copies, waits for them, and re-layouts: 16.5 us -> none  [body(): routed = upstream[row_token]]
    slice x0 -> x7, local copies, waits for them, and re-layouts: none -> 14.6 us  [the longest x1 14.4 us: factors_body(): down_weight[:, expert, :]]
    another operation x9 -> x0, loops' own time: 9.97 us -> none  [the longest x1 5.9 us: body(): lax.map(project, (routed_blocks, block_expert))]
  transfers between devices with their start and end apart: 2 -> 32, of which waited for: 2 -> 15; matrix products, arithmetic and copies ran while one was open for 10% -> 20% of each run, Pallas kernels for 0% -> 2%
where the time goes in v1:
time: 161 us
  waiting for transfers between devices  62.1 us (39%)
  starting transfers between devices  53.5 us (33%)
  local copies, waits for them, and re-layouts  22.7 us (14%)
  other arithmetic  10.4 us (6%)
  matrix products  6.84 us (4%)
  Pallas kernels  3.88 us (2%)
    ppermute x31, waiting for transfers between devices, moved(): return lax.ppermute(value, ('blk', 'wide'), pairs)  62.1 us
    ppermute x31, starting transfers between devices, moved(): return lax.ppermute(value, ('blk', 'wide'), pairs)  48.9 us
    slice x1, local copies, waits for them, and re-layouts, factors_body(): down_weight[:, expert, :]  14.4 us
    unnamed x54, local copies, waits for them, and re-layouts  4.85 us
    all_to_all x1, starting transfers between devices, factors_body(): lax.all_to_all(jnp.broadcast_to(padded, (devices, 128)), ('blk', 'wide'),...  4.52 us
    dot_general x2, matrix products, factors_body(): jnp.dot(upstream, down_weight[:, expert, :], preferred_element_type=jnp.f...  3.92 us
    pallas_call x4, Pallas kernels, add_products(): pl.pallas_call(kernel, out_shape=jax.ShapeDtypeStruct(total.shape, jnp.fl...  3.88 us
    dynamic_slice x1, other arithmetic, own_columns(): lax.dynamic_slice(upstream, (quarter * (blk_index ^ q), first_column), (q...  3.43 us
  transfers between devices with their start and end apart: 32, of which 15 were waited for; matrix products, arithmetic and copies ran while one was open for 20% of the time, Pallas kernels for 2%

profile of v1, /device:TPU:0, one launch (start us, length us, event | category | flops | bytes accessed | tf_op | source)
XLA Modules:
  0.0 160.9 jit_solution(16940169219358371580)
XLA Ops:
  0.8 3.4 %fusion.30 = (bf16[96,896]{1,0:T(8,128)(2,1)}, bf16[96,896]{1,0:T(8,128)(2,1)}, bf16[96,896]{1,0:T(8,128)(2,1)}, bf16[96,896]{1,0:T(8,128)(2,1)}, bf16[96,896]{1...) fusion(bf16[384,7168]{1,0:T(8,128)(2,1)} %param.11, ...), kind=kLoop, calls=%fused_computation.110 | loop fusion | flops 516096 | bytes 5849136 | tf_op jit(solution)/shard_map/dynamic_slice | solution.py:228
  4.3 3.1 %collective-permute-start = (f32[96,896]{1,0:T(8,128)}, f32[96,896]{1,0:T(8,128)}, u32[]{:S(2)}, u32[]{:S(2)}) collective-permute-start(f32[96,896]{1,0:T(8,128)} %get-tuple-element.72), channel_id=1, source_target_pairs={{0,2},{1,3},{2,4},{3,5},{4,6},{5,7},{6,0},{7,1},{8,10},{9,11},{10,... | collective-permute-start | bytes 1032200 | tf_op jit(solution)/shard_map/ppermute | solution.py:146
  10.8 14.4 %fusion.29 = (bf16[7168,1,256]{2,1,0:T(2,128)(2,1)S(1)}, bf16[7168,1,256]{2,1,0:T(2,128)(2,1)S(1)}) fusion(bf16[7168,2,256]{2,1,0:T(2,128)(2,1)} %param.14), kind=kLoop, calls=%fused_computation.109 | loop fusion | bytes 14680064 | tf_op jit(solution)/shard_map/slice | solution.py:263
  25.2 1.6 fusion.1
  26.9 2.3 %fusion = f32[384,256]{1,0:T(8,128)} fusion(bf16[384,7168]{1,0:T(8,128)(2,1)S(1)} %bitcast.49, bf16[7168,1,256]{2,1,0:T(2,128)(2,1)S(1)} %get-tuple-element.59), kind=kOutput, calls=%fused_computation.1 | convolution fusion | flops 1409286144 | bytes 9568256 | tf_op jit(solution)/shard_map/dot_general | solution.py:263
  31.2 2.2 %collective-permute-start.1 = (f32[96,896]{1,0:T(8,128)S(1)}, f32[96,896]{1,0:T(8,128)S(1)}, u32[]{:S(2)}, u32[]{:S(2)}) collective-permute-start(f32[96,896]{1,0:T(8,128)S(1)} %copy-done.7), channel_id=1, source_target_pairs={{0,6},{1,7},{2,0},{3,1},{4,2},{5,3},{6,4},{7,5},{8,14},{9,15},{10,... | collective-permute-start | bytes 1032200 | tf_op jit(solution)/shard_map/ppermute | solution.py:146
  34.2 1.2 pad_maximum_fusion.2.refs_0_
  35.4 1.6 %collective-permute-start.21 = (f32[2,96,896]{2,1,0:T(8,128)S(1)}, f32[2,96,896]{2,1,0:T(8,128)S(1)}, u32[]{:S(2)}, u32[]{:S(2)}) collective-permute-start(f32[2,96,896]{2,1,0:T(8,128)S(1)} %pad_maximum_fusion.2.refs_0_), channel_id=1, source_target_pairs={{0,8},{1,9},{2,10},{3,11},{4,12},{5,13},{6,14},{7,15},{8,0},{9,1},... | collective-permute-start | bytes 2064392 | tf_op jit(solution)/shard_map/ppermute | solution.py:146
  37.0 1.5 collective-permute-start.22
  38.6 3.5 %collective-permute-done.1 = f32[96,896]{1,0:T(8,128)S(1)} collective-permute-done((f32[96,896]{1,0:T(8,128)S(1)}, f32[96,896]{1,0:T(8,128)S(1)}, u32[]{:S(2)}, u32[]{:S(2)}) %collective-permute-start.1) | collective-permute-done | bytes 344096 | tf_op jit(solution)/shard_map/ppermute | solution.py:146
  42.1 1.8 %collective-permute-start.2 = (f32[96,896]{1,0:T(8,128)S(1)}, f32[96,896]{1,0:T(8,128)S(1)}, u32[]{:S(2)}, u32[]{:S(2)}) collective-permute-start(f32[96,896]{1,0:T(8,128)S(1)} %copy-done.5), channel_id=1, source_target_pairs={{0,4},{1,5},{2,6},{3,7},{4,0},{5,1},{6,2},{7,3},{8,12},{9,13},{10,... | collective-permute-start | bytes 1032200 | tf_op jit(solution)/shard_map/ppermute | solution.py:146
  44.0 5.5 %collective-permute-done.4 = f32[96,896]{1,0:T(8,128)S(1)} collective-permute-done((f32[96,896]{1,0:T(8,128)S(1)}, f32[96,896]{1,0:T(8,128)S(1)}, u32[]{:S(2)}, u32[]{:S(2)}) %collective-permute-start.4) | collective-permute-done | bytes 344096 | tf_op jit(solution)/shard_map/ppermute | solution.py:146
  49.5 1.6 collective-permute-start.15
  51.8 1.6 collective-permute-start.16
  53.4 11.9 %collective-permute-done.2 = f32[96,896]{1,0:T(8,128)S(1)} collective-permute-done((f32[96,896]{1,0:T(8,128)S(1)}, f32[96,896]{1,0:T(8,128)S(1)}, u32[]{:S(2)}, u32[]{:S(2)}) %collective-permute-start.2) | collective-permute-done | bytes 344096 | tf_op jit(solution)/shard_map/ppermute | solution.py:146
  65.9 17.9 %collective-permute-done.5 = f32[96,896]{1,0:T(8,128)S(1)} collective-permute-done((f32[96,896]{1,0:T(8,128)S(1)}, f32[96,896]{1,0:T(8,128)S(1)}, u32[]{:S(2)}, u32[]{:S(2)}) %collective-permute-start.5) | collective-permute-done | bytes 344096 | tf_op jit(solution)/shard_map/ppermute | solution.py:146
  83.8 1.3 collective-permute-start.12
  85.1 4.6 %collective-permute-start.10 = (f32[392,256]{1,0:T(8,128)S(1)}, f32[392,256]{1,0:T(8,128)S(1)}, u32[]{:S(2)}, u32[]{:S(2)}) collective-permute-start(f32[392,256]{1,0:T(8,128)S(1)} %pad_maximum_fusion.3), channel_id=1, source_target_pairs={{0,2},{1,3},{2,4},{3,5},{4,6},{5,7},{8,10},{9,11},{10,12},{11,13},... | collective-permute-start | bytes 1204232 | tf_op jit(solution)/shard_map/ppermute | solution.py:146
  90.0 1.6 collective-permute-start.6
  91.6 1.6 collective-permute-start.7
  93.2 3.8 %collective-permute-done.12 = f32[392,256]{1,0:T(8,128)S(1)} collective-permute-done((f32[392,256]{1,0:T(8,128)S(1)}, f32[392,256]{1,0:T(8,128)S(1)}, u32[]{:S(2)}, u32[]{:S(2)}) %collective-permute-start.12) | collective-permute-done | bytes 401440 | tf_op jit(solution)/shard_map/ppermute | solution.py:146
  97.0 1.3 collective-permute-start.13
  98.3 4.6 %collective-permute-start.11 = (f32[392,256]{1,0:T(8,128)S(1)}, f32[392,256]{1,0:T(8,128)S(1)}, u32[]{:S(2)}, u32[]{:S(2)}) collective-permute-start(f32[392,256]{1,0:T(8,128)S(1)} %collective-permute-done.10), channel_id=1, source_target_pairs={{0,2},{1,3},{2,4},{3,5},{4,6},{5,7},{8,10},{9,11},{10,12},{11,13},... | collective-permute-start | bytes 1204232 | tf_op jit(solution)/shard_map/ppermute | solution.py:146
  103.3 1.6 collective-permute-start.23
  105.1 1.0 shard_map.110.refs_6_
  106.1 0.9 collective-permute-done.6.refs_1_
  106.9 1.5 collective-permute-start.24
  108.5 1.6 collective-permute-done.7.refs_2_
  110.0 1.5 collective-permute-start.17
  111.7 1.3 collective-permute-start.25
  113.0 4.8 %collective-permute-start.19 = (f32[392,256]{1,0:T(8,128)S(1)}, f32[392,256]{1,0:T(8,128)S(1)}, u32[]{:S(2)}, u32[]{:S(2)}) collective-permute-start(f32[392,256]{1,0:T(8,128)S(1)} %collective-permute-done.11), channel_id=1, source_target_pairs={{0,2},{1,3},{2,4},{3,5},{4,6},{5,7},{8,10},{9,11},{10,12},{11,13},... | collective-permute-start | bytes 1204232 | tf_op jit(solution)/shard_map/ppermute | solution.py:146
  117.9 4.6 %collective-permute-done.25 = f32[392,256]{1,0:T(8,128)S(1)} collective-permute-done((f32[392,256]{1,0:T(8,128)S(1)}, f32[392,256]{1,0:T(8,128)S(1)}, u32[]{:S(2)}, u32[]{:S(2)}) %collective-permute-start.25) | collective-permute-done | bytes 401440 | tf_op jit(solution)/shard_map/ppermute | solution.py:146
  122.5 1.5 collective-permute-start.18
  124.3 1.6 %collective-permute-done.14 = f32[392,256]{1,0:T(8,128)S(1)} collective-permute-done((f32[392,256]{1,0:T(8,128)S(1)}, f32[392,256]{1,0:T(8,128)S(1)}, u32[]{:S(2)}, u32[]{:S(2)}) %collective-permute-start.14) | collective-permute-done | bytes 401440 | tf_op jit(solution)/shard_map/ppermute | solution.py:146
  127.8 1.6 collective-permute-done.20
  129.4 1.5 collective-permute-start.8
  131.3 1.1 collective-permute-start.9
  132.6 1.0 shard_map.111.refs_6_
  133.8 1.0 shard_map.112.refs_6_
  134.8 4.7 %collective-permute-done.8.refs_3_ = f32[2,48,896]{2,1,0:T(8,128)S(1)} collective-permute-done((f32[2,48,896]{2,1,0:T(8,128)S(1)}, f32[2,48,896]{2,1,0:T(8,128)S(1)}, u32[]{:S(2)}, u32[]{:S(2)}) %collective-permute-start.8) | collective-permute-done | bytes 344096 | tf_op jit(solution)/shard_map/ppermute | solution.py:146
  139.5 1.7 %collective-permute-done.9.refs_4_ = f32[2,48,896]{2,1,0:T(8,128)S(1)} collective-permute-done((f32[2,48,896]{2,1,0:T(8,128)S(1)}, f32[2,48,896]{2,1,0:T(8,128)S(1)}, u32[]{:S(2)}, u32[]{:S(2)}) %collective-permute-start.9) | collective-permute-done | bytes 344096 | tf_op jit(solution)/shard_map/ppermute | solution.py:146
  141.2 1.0 shard_map.113
  143.7 4.5 %all-to-all-start = ((f32[32,1,128]{2,1,0:T(1,128)}), f32[32,1,128]{2,1,0:T(1,128)S(1)}, u32[]{:S(2)}, u32[]{:S(2)}) async-start(f32[32,1,128]{2,1,0:T(1,128)} %broadcast_in_dim.188), calls=%async_computation | async-start | bytes 32768 | tf_op jit(solution)/shard_map/all_to_all | solution.py:256
  148.3 1.9 %fusion.8 = (bf16[384,256]{0,1:T(8,128)(2,1)S(1)}, f32[384]{0:T(512)S(1)}, bf16[384,256]{0,1:T(8,128)(2,1)S(1)}) fusion(bf16[384,256]{0,1:T(8,128)(2,1)S(1)} %copy-done.11, bf16[384,256]{0,1:T(8,128)(2,1)S(1)} %copy-done.10, f32[384]{0:T(512)S(1)} %copy-done.14, f32[384,256]{0,1:T(8,128)S(1)} %fusion.5, f32[384,256]{1,0:T(8,128)} %fusion, ...), kind=kOutput, calls=%fused_computation.29 | convolution fusion | flops 455097984 | bytes 1577856 | tf_op jit(solution)/shard_map/dot_general | solution.py:268
  150.1 1.8 %collective-permute-start.29 = (f32[384]{0:T(512)S(1)}, f32[384]{0:T(512)S(1)}, u32[]{:S(2)}, u32[]{:S(2)}) collective-permute-start(f32[384]{0:T(512)S(1)} %get-tuple-element.76), channel_id=1, source_target_pairs={{0,8},{1,9},{2,10},{3,11},{4,12},{5,13},{6,14},{7,15},{8,0},{9,1},... | collective-permute-start | bytes 4616 | tf_op jit(solution)/shard_map/ppermute | solution.py:146
  152.0 1.8 %collective-permute-done.29 = f32[384]{0:T(512)S(1)} collective-permute-done((f32[384]{0:T(512)S(1)}, f32[384]{0:T(512)S(1)}, u32[]{:S(2)}, u32[]{:S(2)}) %collective-permute-start.29) | collective-permute-done | bytes 1568 | tf_op jit(solution)/shard_map/ppermute | solution.py:146
  153.8 1.8 %collective-permute-start.30 = (f32[384]{0:T(512)S(1)}, f32[384]{0:T(512)S(1)}, u32[]{:S(2)}, u32[]{:S(2)}) collective-permute-start(f32[384]{0:T(512)S(1)} %add.189), channel_id=1, source_target_pairs={{0,16},{1,17},{2,18},{3,19},{4,20},{5,21},{6,22},{7,23},{8,24},{9,... | collective-permute-start | bytes 4616 | tf_op jit(solution)/shard_map/ppermute | solution.py:146
  157.9 2.4 %reshape.163 = f32[896,2,256]{2,1,0:T(2,128)} reshape(f32[896,512]{1,0:T(8,128)S(1)} %shard_map.113) | data formatting | bytes 3670016 | tf_op jit(solution)/shard_map/reshape | solution.py:252
  (137 shorter events, 16.2 us)
Async XLA Ops:
  0.8 8.0 %copy-start.13 = (s32[3]{0:T(128)S(1)}, s32[3]{0:T(128)}, u32[]{:S(2)}) copy-start(s32[3]{0:T(128)} %param.15) | copy-start | bytes 40
  0.8 8.1 %copy-start.8 = (bf16[384,256]{1,0:T(8,128)(2,1)S(1)}, bf16[384,256]{1,0:T(8,128)(2,1)}, u32[]{:S(2)}) copy-start(bf16[384,256]{1,0:T(8,128)(2,1)} %param.12) | copy-start | bytes 589828
  0.8 8.9 %copy-start.9 = (bf16[384,256]{1,0:T(8,128)(2,1)S(1)}, bf16[384,256]{1,0:T(8,128)(2,1)}, u32[]{:S(2)}) copy-start(bf16[384,256]{1,0:T(8,128)(2,1)} %param.13) | copy-start | bytes 589828
  0.8 9.7 %copy-start.12 = (s32[384]{0:T(512)S(1)}, s32[384]{0:T(512)}, u32[]{:S(2)}) copy-start(s32[384]{0:T(512)} %param.16) | copy-start | bytes 4612
  4.3 26.4 %collective-permute-start = (f32[96,896]{1,0:T(8,128)}, f32[96,896]{1,0:T(8,128)}, u32[]{:S(2)}, u32[]{:S(2)}) collective-permute-start(f32[96,896]{1,0:T(8,128)} %get-tuple-element.72), channel_id=1, source_target_pairs={{0,2},{1,3},{2,4},{3,5},{4,6},{5,7},{6,0},{7,1},{8,10},{9,11},{10,... | collective-permute-start | bytes 1032200 | tf_op jit(solution)/shard_map/ppermute | solution.py:146
  7.3 26.1 %collective-permute-start.3 = (f32[96,896]{1,0:T(8,128)}, f32[96,896]{1,0:T(8,128)}, u32[]{:S(2)}, u32[]{:S(2)}) collective-permute-start(f32[96,896]{1,0:T(8,128)} %get-tuple-element.69), channel_id=1, source_target_pairs={{0,3},{1,2},{2,5},{3,4},{4,7},{5,6},{6,1},{7,0},{8,11},{9,10},{10,... | collective-permute-start | bytes 1032200 | tf_op jit(solution)/shard_map/ppermute | solution.py:146
  9.7 15.5 %slice-start = ((s8[5505024]{0:T(1024)(128)(4,1)}), s8[1310720]{0:T(1024)(128)(4,1)S(1)}, s32[]{:S(2)}) async-start(s8[5505024]{0:T(1024)(128)(4,1)} %bitcast.48), calls=%async_computation.1 | async-start | bytes 2621440
  10.8 14.4 %slice-start.1 = ((s8[5505024]{0:T(1024)(128)(4,1)}), s8[4194304]{0:T(1024)(128)(4,1)S(1)}, s32[]{:S(2)}) async-start(s8[5505024]{0:T(1024)(128)(4,1)} %bitcast.48), calls=%async_computation.2 | async-start | bytes 8388608
  26.8 2.4 %copy-start = (bf16[96,896]{1,0:T(8,128)(2,1)S(1)}, bf16[96,896]{1,0:T(8,128)(2,1)}, u32[]{:S(2)}) copy-start(bf16[96,896]{1,0:T(8,128)(2,1)} %get-tuple-element.61) | copy-start | bytes 516100
  26.8 2.4 %copy-start.1 = (bf16[96,896]{1,0:T(8,128)(2,1)S(1)}, bf16[96,896]{1,0:T(8,128)(2,1)}, u32[]{:S(2)}) copy-start(bf16[96,896]{1,0:T(8,128)(2,1)} %get-tuple-element.62) | copy-start | bytes 516100
  26.8 2.4 %copy-start.2 = (bf16[96,896]{1,0:T(8,128)(2,1)S(1)}, bf16[96,896]{1,0:T(8,128)(2,1)}, u32[]{:S(2)}) copy-start(bf16[96,896]{1,0:T(8,128)(2,1)} %get-tuple-element.63) | copy-start | bytes 516100
  26.9 2.4 %copy-start.3 = (bf16[96,896]{1,0:T(8,128)(2,1)S(1)}, bf16[96,896]{1,0:T(8,128)(2,1)}, u32[]{:S(2)}) copy-start(bf16[96,896]{1,0:T(8,128)(2,1)} %get-tuple-element.64) | copy-start | bytes 516100
  29.2 1.0 copy-start.11
  29.2 1.0 copy-start.14
  30.2 1.0 copy-start.7
  30.2 3.2 %copy-start.6 = (f32[96,896]{1,0:T(8,128)S(1)}, f32[96,896]{1,0:T(8,128)}, u32[]{:S(2)}) copy-start(f32[96,896]{1,0:T(8,128)} %get-tuple-element.36) | copy-start | bytes 1032196
  31.2 10.9 %collective-permute-start.1 = (f32[96,896]{1,0:T(8,128)S(1)}, f32[96,896]{1,0:T(8,128)S(1)}, u32[]{:S(2)}, u32[]{:S(2)}) collective-permute-start(f32[96,896]{1,0:T(8,128)S(1)} %copy-done.7), channel_id=1, source_target_pairs={{0,6},{1,7},{2,0},{3,1},{4,2},{5,3},{6,4},{7,5},{8,14},{9,15},{10,... | collective-permute-start | bytes 1032200 | tf_op jit(solution)/shard_map/ppermute | solution.py:146
  33.5 16.0 %collective-permute-start.4 = (f32[96,896]{1,0:T(8,128)S(1)}, f32[96,896]{1,0:T(8,128)S(1)}, u32[]{:S(2)}, u32[]{:S(2)}) collective-permute-start(f32[96,896]{1,0:T(8,128)S(1)} %copy-done.6), channel_id=1, source_target_pairs={{0,7},{1,6},{2,1},{3,0},{4,3},{5,2},{6,5},{7,4},{8,15},{9,14},{10,... | collective-permute-start | bytes 1032200 | tf_op jit(solution)/shard_map/ppermute | solution.py:146
  34.2 7.9 %copy-start.5 = (f32[96,896]{1,0:T(8,128)S(1)}, f32[96,896]{1,0:T(8,128)}, u32[]{:S(2)}) copy-start(f32[96,896]{1,0:T(8,128)} %get-tuple-element.35) | copy-start | bytes 1032196
  35.4 29.9 %copy-start.4 = (f32[96,896]{1,0:T(8,128)S(1)}, f32[96,896]{1,0:T(8,128)}, u32[]{:S(2)}) copy-start(f32[96,896]{1,0:T(8,128)} %get-tuple-element.37) | copy-start | bytes 1032196
  35.4 29.9 %collective-permute-start.21 = (f32[2,96,896]{2,1,0:T(8,128)S(1)}, f32[2,96,896]{2,1,0:T(8,128)S(1)}, u32[]{:S(2)}, u32[]{:S(2)}) collective-permute-start(f32[2,96,896]{2,1,0:T(8,128)S(1)} %pad_maximum_fusion.2.refs_0_), channel_id=1, source_target_pairs={{0,8},{1,9},{2,10},{3,11},{4,12},{5,13},{6,14},{7,15},{8,0},{9,1},... | collective-permute-start | bytes 2064392 | tf_op jit(solution)/shard_map/ppermute | solution.py:146
  37.0 28.4 %collective-permute-start.22 = (f32[2,96,896]{2,1,0:T(8,128)S(1)}, f32[2,96,896]{2,1,0:T(8,128)S(1)}, u32[]{:S(2)}, u32[]{:S(2)}) collective-permute-start(f32[2,96,896]{2,1,0:T(8,128)S(1)} %pad_maximum_fusion.2.refs_0_), channel_id=1, source_target_pairs={{0,16},{1,17},{2,18},{3,19},{4,20},{5,21},{6,22},{7,23},{8,24},{9,... | collective-permute-start | bytes 2064392 | tf_op jit(solution)/shard_map/ppermute | solution.py:146
  42.1 23.1 %collective-permute-start.2 = (f32[96,896]{1,0:T(8,128)S(1)}, f32[96,896]{1,0:T(8,128)S(1)}, u32[]{:S(2)}, u32[]{:S(2)}) collective-permute-start(f32[96,896]{1,0:T(8,128)S(1)} %copy-done.5), channel_id=1, source_target_pairs={{0,4},{1,5},{2,6},{3,7},{4,0},{5,1},{6,2},{7,3},{8,12},{9,13},{10,... | collective-permute-start | bytes 1032200 | tf_op jit(solution)/shard_map/ppermute | solution.py:146
  49.5 35.5 %collective-permute-start.15 = (f32[2,96,896]{2,1,0:T(8,128)S(1)}, f32[2,96,896]{2,1,0:T(8,128)S(1)}, u32[]{:S(2)}, u32[]{:S(2)}) collective-permute-start(f32[2,96,896]{2,1,0:T(8,128)S(1)} %pad_maximum_fusion.1.refs_0_), channel_id=1, source_target_pairs={{0,8},{1,9},{2,10},{3,11},{4,12},{5,13},{6,14},{7,15},{8,0},{9,1},... | collective-permute-start | bytes 2064392 | tf_op jit(solution)/shard_map/ppermute | solution.py:146
  51.8 38.2 %collective-permute-start.16 = (f32[2,96,896]{2,1,0:T(8,128)S(1)}, f32[2,96,896]{2,1,0:T(8,128)S(1)}, u32[]{:S(2)}, u32[]{:S(2)}) collective-permute-start(f32[2,96,896]{2,1,0:T(8,128)S(1)} %pad_maximum_fusion.1.refs_0_), channel_id=1, source_target_pairs={{0,16},{1,17},{2,18},{3,19},{4,20},{5,21},{6,22},{7,23},{8,24},{9,... | collective-permute-start | bytes 2064392 | tf_op jit(solution)/shard_map/ppermute | solution.py:146
  65.3 18.5 %collective-permute-start.5 = (f32[96,896]{1,0:T(8,128)S(1)}, f32[96,896]{1,0:T(8,128)S(1)}, u32[]{:S(2)}, u32[]{:S(2)}) collective-permute-start(f32[96,896]{1,0:T(8,128)S(1)} %copy-done.4), channel_id=1, source_target_pairs={{0,5},{1,4},{2,7},{3,6},{4,1},{5,0},{6,3},{7,2},{8,13},{9,12},{10,... | collective-permute-start | bytes 1032200 | tf_op jit(solution)/shard_map/ppermute | solution.py:146
  65.3 38.0 %collective-permute-start.27 = (f32[384,896]{1,0:T(8,128)S(1)}, f32[384,896]{1,0:T(8,128)S(1)}, u32[]{:S(2)}, u32[]{:S(2)}) collective-permute-start(f32[384,896]{1,0:T(8,128)S(1)} %maximum_convert_fusion.1), channel_id=1, source_target_pairs={{0,1},{1,0},{2,3},{3,2},{4,5},{5,4},{6,7},{7,6},{8,9},{9,8},{10,11... | collective-permute-start | bytes 4128776 | tf_op jit(solution)/shard_map/ppermute | solution.py:146
  65.5 26.1 %collective-permute-start.28 = (f32[392,256]{1,0:T(8,128)S(1)}, f32[392,256]{1,0:T(8,128)S(1)}, u32[]{:S(2)}, u32[]{:S(2)}) collective-permute-start(f32[392,256]{1,0:T(8,128)S(1)} %pad_maximum_fusion.3), channel_id=1, source_target_pairs={{0,1},{1,0},{2,3},{3,2},{4,5},{5,4},{6,7},{7,6},{8,9},{9,8},{10,11... | collective-permute-start | bytes 1204232 | tf_op jit(solution)/shard_map/ppermute | solution.py:146
  83.8 13.2 %collective-permute-start.12 = (f32[392,256]{1,0:T(8,128)S(1)}, f32[392,256]{1,0:T(8,128)S(1)}, u32[]{:S(2)}, u32[]{:S(2)}) collective-permute-start(f32[392,256]{1,0:T(8,128)S(1)} %pad_maximum_fusion.3), channel_id=1, source_target_pairs={{2,0},{3,1},{4,2},{5,3},{6,4},{7,5},{10,8},{11,9},{12,10},{13,11},... | collective-permute-start | bytes 1204232 | tf_op jit(solution)/shard_map/ppermute | solution.py:146
  85.1 13.2 %collective-permute-start.10 = (f32[392,256]{1,0:T(8,128)S(1)}, f32[392,256]{1,0:T(8,128)S(1)}, u32[]{:S(2)}, u32[]{:S(2)}) collective-permute-start(f32[392,256]{1,0:T(8,128)S(1)} %pad_maximum_fusion.3), channel_id=1, source_target_pairs={{0,2},{1,3},{2,4},{3,5},{4,6},{5,7},{8,10},{9,11},{10,12},{11,13},... | collective-permute-start | bytes 1204232 | tf_op jit(solution)/shard_map/ppermute | solution.py:146
  90.0 17.0 %collective-permute-start.6 = (f32[2,96,896]{2,1,0:T(8,128)S(1)}, f32[2,96,896]{2,1,0:T(8,128)S(1)}, u32[]{:S(2)}, u32[]{:S(2)}) collective-permute-start(f32[2,96,896]{2,1,0:T(8,128)S(1)} %pad_maximum_fusion.refs_0_), channel_id=1, source_target_pairs={{0,8},{1,9},{2,10},{3,11},{4,12},{5,13},{6,14},{7,15},{8,0},{9,1},... | collective-permute-start | bytes 2064392 | tf_op jit(solution)/shard_map/ppermute | solution.py:146
  91.6 18.4 %collective-permute-start.7 = (f32[2,96,896]{2,1,0:T(8,128)S(1)}, f32[2,96,896]{2,1,0:T(8,128)S(1)}, u32[]{:S(2)}, u32[]{:S(2)}) collective-permute-start(f32[2,96,896]{2,1,0:T(8,128)S(1)} %pad_maximum_fusion.refs_0_), channel_id=1, source_target_pairs={{0,16},{1,17},{2,18},{3,19},{4,20},{5,21},{6,22},{7,23},{8,24},{9,... | collective-permute-start | bytes 2064392 | tf_op jit(solution)/shard_map/ppermute | solution.py:146
  97.0 14.6 %collective-permute-start.13 = (f32[392,256]{1,0:T(8,128)S(1)}, f32[392,256]{1,0:T(8,128)S(1)}, u32[]{:S(2)}, u32[]{:S(2)}) collective-permute-start(f32[392,256]{1,0:T(8,128)S(1)} %collective-permute-done.12), channel_id=1, source_target_pairs={{2,0},{3,1},{4,2},{5,3},{6,4},{7,5},{10,8},{11,9},{12,10},{13,11},... | collective-permute-start | bytes 1204232 | tf_op jit(solution)/shard_map/ppermute | solution.py:146
  98.3 13.3 %collective-permute-start.11 = (f32[392,256]{1,0:T(8,128)S(1)}, f32[392,256]{1,0:T(8,128)S(1)}, u32[]{:S(2)}, u32[]{:S(2)}) collective-permute-start(f32[392,256]{1,0:T(8,128)S(1)} %collective-permute-done.10), channel_id=1, source_target_pairs={{0,2},{1,3},{2,4},{3,5},{4,6},{5,7},{8,10},{9,11},{10,12},{11,13},... | collective-permute-start | bytes 1204232 | tf_op jit(solution)/shard_map/ppermute | solution.py:146
  103.3 28.0 %collective-permute-start.23 = (f32[2,48,896]{2,1,0:T(8,128)S(1)}, f32[2,48,896]{2,1,0:T(8,128)S(1)}, u32[]{:S(2)}, u32[]{:S(2)}) collective-permute-start(f32[2,48,896]{2,1,0:T(8,128)S(1)} %slice.171), channel_id=1, source_target_pairs={{0,16},{1,17},{2,18},{3,19},{4,20},{5,21},{6,22},{7,23},{8,24},{9,... | collective-permute-start | bytes 1032200 | tf_op jit(solution)/shard_map/ppermute | solution.py:146
  106.9 25.7 %collective-permute-start.24 = (f32[2,48,896]{2,1,0:T(8,128)S(1)}, f32[2,48,896]{2,1,0:T(8,128)S(1)}, u32[]{:S(2)}, u32[]{:S(2)}) collective-permute-start(f32[2,48,896]{2,1,0:T(8,128)S(1)} %slice.172), channel_id=1, source_target_pairs={{0,8},{1,9},{2,10},{3,11},{4,12},{5,13},{6,14},{7,15},{8,0},{9,1},... | collective-permute-start | bytes 1032200 | tf_op jit(solution)/shard_map/ppermute | solution.py:146
  110.0 23.8 %collective-permute-start.17 = (f32[2,48,896]{2,1,0:T(8,128)S(1)}, f32[2,48,896]{2,1,0:T(8,128)S(1)}, u32[]{:S(2)}, u32[]{:S(2)}) collective-permute-start(f32[2,48,896]{2,1,0:T(8,128)S(1)} %slice.165), channel_id=1, source_target_pairs={{0,16},{1,17},{2,18},{3,19},{4,20},{5,21},{6,22},{7,23},{8,24},{9,... | collective-permute-start | bytes 1032200 | tf_op jit(solution)/shard_map/ppermute | solution.py:146
  111.7 10.8 %collective-permute-start.25 = (f32[392,256]{1,0:T(8,128)S(1)}, f32[392,256]{1,0:T(8,128)S(1)}, u32[]{:S(2)}, u32[]{:S(2)}) collective-permute-start(f32[392,256]{1,0:T(8,128)S(1)} %collective-permute-done.13), channel_id=1, source_target_pairs={{2,0},{3,1},{4,2},{5,3},{6,4},{7,5},{10,8},{11,9},{12,10},{13,11},... | collective-permute-start | bytes 1204232 | tf_op jit(solution)/shard_map/ppermute | solution.py:146
  113.0 11.1 %collective-permute-start.19 = (f32[392,256]{1,0:T(8,128)S(1)}, f32[392,256]{1,0:T(8,128)S(1)}, u32[]{:S(2)}, u32[]{:S(2)}) collective-permute-start(f32[392,256]{1,0:T(8,128)S(1)} %collective-permute-done.11), channel_id=1, source_target_pairs={{0,2},{1,3},{2,4},{3,5},{4,6},{5,7},{8,10},{9,11},{10,12},{11,13},... | collective-permute-start | bytes 1204232 | tf_op jit(solution)/shard_map/ppermute | solution.py:146
  122.5 11.3 %collective-permute-start.18 = (f32[2,48,896]{2,1,0:T(8,128)S(1)}, f32[2,48,896]{2,1,0:T(8,128)S(1)}, u32[]{:S(2)}, u32[]{:S(2)}) collective-permute-start(f32[2,48,896]{2,1,0:T(8,128)S(1)} %slice.166), channel_id=1, source_target_pairs={{0,8},{1,9},{2,10},{3,11},{4,12},{5,13},{6,14},{7,15},{8,0},{9,1},... | collective-permute-start | bytes 1032200 | tf_op jit(solution)/shard_map/ppermute | solution.py:146
  124.1 1.8 %collective-permute-start.14 = (f32[392,256]{1,0:T(8,128)S(1)}, f32[392,256]{1,0:T(8,128)S(1)}, u32[]{:S(2)}, u32[]{:S(2)}) collective-permute-start(f32[392,256]{1,0:T(8,128)S(1)} %add.179), channel_id=1, source_target_pairs={{0,1},{1,0},{2,3},{3,2},{4,5},{5,4},{6,7},{7,6},{8,9},{9,8},{10,11... | collective-permute-start | bytes 1204232 | tf_op jit(solution)/shard_map/ppermute | solution.py:146
  125.9 1.7 %collective-permute-start.26 = (f32[392,256]{1,0:T(8,128)S(1)}, f32[392,256]{1,0:T(8,128)S(1)}, u32[]{:S(2)}, u32[]{:S(2)}) collective-permute-start(f32[392,256]{1,0:T(8,128)S(1)} %add.181), channel_id=1, source_target_pairs={{0,1},{1,0},{2,3},{3,2},{4,5},{5,4},{6,7},{7,6},{8,9},{9,8},{10,11... | collective-permute-start | bytes 1204232 | tf_op jit(solution)/shard_map/ppermute | solution.py:146
  127.6 1.7 %collective-permute-start.20 = (f32[392,256]{1,0:T(8,128)S(1)}, f32[392,256]{1,0:T(8,128)S(1)}, u32[]{:S(2)}, u32[]{:S(2)}) collective-permute-start(f32[392,256]{1,0:T(8,128)S(1)} %add.180), channel_id=1, source_target_pairs={{0,1},{1,0},{2,3},{3,2},{4,5},{5,4},{6,7},{7,6},{8,9},{9,8},{10,11... | collective-permute-start | bytes 1204232 | tf_op jit(solution)/shard_map/ppermute | solution.py:146
  129.4 10.1 %collective-permute-start.8 = (f32[2,48,896]{2,1,0:T(8,128)S(1)}, f32[2,48,896]{2,1,0:T(8,128)S(1)}, u32[]{:S(2)}, u32[]{:S(2)}) collective-permute-start(f32[2,48,896]{2,1,0:T(8,128)S(1)} %slice.159), channel_id=1, source_target_pairs={{0,16},{1,17},{2,18},{3,19},{4,20},{5,21},{6,22},{7,23},{8,24},{9,... | collective-permute-start | bytes 1032200 | tf_op jit(solution)/shard_map/ppermute | solution.py:146
  131.3 9.9 %collective-permute-start.9 = (f32[2,48,896]{2,1,0:T(8,128)S(1)}, f32[2,48,896]{2,1,0:T(8,128)S(1)}, u32[]{:S(2)}, u32[]{:S(2)}) collective-permute-start(f32[2,48,896]{2,1,0:T(8,128)S(1)} %slice.160), channel_id=1, source_target_pairs={{0,8},{1,9},{2,10},{3,11},{4,12},{5,13},{6,14},{7,15},{8,0},{9,1},... | collective-permute-start | bytes 1032200 | tf_op jit(solution)/shard_map/ppermute | solution.py:146
  143.7 16.6 %all-to-all-start = ((f32[32,1,128]{2,1,0:T(1,128)}), f32[32,1,128]{2,1,0:T(1,128)S(1)}, u32[]{:S(2)}, u32[]{:S(2)}) async-start(f32[32,1,128]{2,1,0:T(1,128)} %broadcast_in_dim.188), calls=%async_computation | async-start | bytes 32768 | tf_op jit(solution)/shard_map/all_to_all | solution.py:256
  150.1 3.6 %collective-permute-start.29 = (f32[384]{0:T(512)S(1)}, f32[384]{0:T(512)S(1)}, u32[]{:S(2)}, u32[]{:S(2)}) collective-permute-start(f32[384]{0:T(512)S(1)} %get-tuple-element.76), channel_id=1, source_target_pairs={{0,8},{1,9},{2,10},{3,11},{4,12},{5,13},{6,14},{7,15},{8,0},{9,1},... | collective-permute-start | bytes 4616 | tf_op jit(solution)/shard_map/ppermute | solution.py:146
  153.8 3.6 %collective-permute-start.30 = (f32[384]{0:T(512)S(1)}, f32[384]{0:T(512)S(1)}, u32[]{:S(2)}, u32[]{:S(2)}) collective-permute-start(f32[384]{0:T(512)S(1)} %add.189), channel_id=1, source_target_pairs={{0,16},{1,17},{2,18},{3,19},{4,20},{5,21},{6,22},{7,23},{8,24},{9,... | collective-permute-start | bytes 4616 | tf_op jit(solution)/shard_map/ppermute | solution.py:146
  (1 other events, 0.9 us)

commit v2 on v0

--- a/solution.py
+++ b/solution.py
@@ -1,15 +1,437 @@
 import jax
 import jax.numpy as jnp
 from jax import lax
+from jax.experimental import pallas as pl
+from jax.experimental.pallas import tpu as pltpu
 from jax.sharding import PartitionSpec as P
 
 D = 7168
 FFW = 1024
 EXPERTS = 2
 BLOCK = 128
-
-
-def body(upstream, gate_pre, up_pre, down_weight, block_expert, row_token, gate_prob):
+VMEM = 56 * 1024 * 1024
+EARLY = 20_000_000_000
+
+
+def add_products(parts, pieces, here, there, total, rows, devices=0):
+    depth = 2 * rows
+    share = parts[0].shape[-1]
+    hidden_share = here.shape[1]
+
+    def kernel(*refs):
+        part_refs, (here_ref, there_ref, total_ref, out_ref) = refs[: len(parts)], refs[len(parts) : len(parts) + 4]
+        left, right = refs[-2:]
+        for part, first, amount, spot in pieces:
+            left[spot : spot + amount, :] = part_refs[part][first : first + amount, :].astype(jnp.bfloat16)
+        for side, factor_ref in enumerate((here_ref, there_ref)):
+            marks = factor_ref[rows:, :].T
+            for first in range(0, rows, hidden_share):
+                amount = min(hidden_share, rows - first)
+                line = first // hidden_share
+                mark = marks[:amount, line : line + 1]
+                weight = factor_ref[first : first + amount, :]
+                spot = side * rows + first
+                for expert in range(EXPERTS):
+                    right[spot : spot + amount, expert * hidden_share : (expert + 1) * hidden_share] = jnp.where(
+                        mark == float(expert), weight, 0.0
+                    ).astype(jnp.bfloat16)
+        weights = right[...]
+        squares = jnp.zeros((1, EXPERTS * hidden_share), jnp.float32)
+        for first in range(0, share, 128):
+            block = total_ref[first : first + 128, :] + lax.dot_general(
+                left[:, first : first + 128],
+                weights,
+                (((0,), (0,)), ((), ())),
+                preferred_element_type=jnp.float32,
+            )
+            out_ref[first : first + 128, :] = block
+            if devices:
+                squares = squares + jnp.sum(block * block, axis=0, keepdims=True)
+        if devices:
+            lane = lax.broadcasted_iota(jnp.int32, (devices, 128), 1)
+            sums = jnp.zeros((devices, 128), jnp.float32)
+            for expert in range(EXPERTS):
+                own = squares[:, expert * hidden_share : (expert + 1) * hidden_share]
+                sums = jnp.where(lane == expert, jnp.sum(own, axis=1, keepdims=True), sums)
+            refs[-3][...] = sums
+
+    out_shape = [jax.ShapeDtypeStruct(total.shape, jnp.float32)]
+    if devices:
+        out_shape.append(jax.ShapeDtypeStruct((devices, 128), jnp.float32))
+    results = pl.pallas_call(
+        kernel,
+        out_shape=out_shape,
+        in_specs=[pl.BlockSpec(memory_space=pltpu.VMEM)] * (len(parts) + 3),
+        out_specs=[pl.BlockSpec(memory_space=pltpu.VMEM)] * len(out_shape),
+        scratch_shapes=[
+            pltpu.VMEM((depth, share), jnp.bfloat16),
+            pltpu.VMEM((depth, EXPERTS * hidden_share), jnp.bfloat16),
+        ],
+        compiler_params=pltpu.CompilerParams(vmem_limit_bytes=16 * 1024 * 1024),
+        cost_estimate=pl.CostEstimate(
+            flops=2 * depth * share * EXPERTS * hidden_share,
+            bytes_accessed=4 * depth * (share + hidden_share) + 8 * share * EXPERTS * hidden_share,
+            transcendentals=0,
+        ),
+    )(*parts, here, there, total)
+    return results if devices else results[0]
+
+
+def stack_rows(lists, flops=0):
+    arrays = []
+    for pieces in lists:
+        for array, _, _ in pieces:
+            if not any(array is one for one in arrays):
+                arrays.append(array)
+    places = [
+        [([array is one for one in arrays].index(True), first, amount) for array, first, amount in pieces]
+        for pieces in lists
+    ]
+    share = arrays[0].shape[1]
+    heights = [sum(amount for _, _, amount in pieces) for pieces in lists]
+
+    def kernel(*refs):
+        for out_ref, pieces in zip(refs[len(arrays) :], places):
+            spot = 0
+            for index, first, amount in pieces:
+                out_ref[spot : spot + amount, :] = refs[index][first : first + amount, :]
+                spot += amount
+
+    return pl.pallas_call(
+        kernel,
+        out_shape=[jax.ShapeDtypeStruct((height, share), jnp.float32) for height in heights],
+        in_specs=[pl.BlockSpec(memory_space=pltpu.VMEM)] * len(arrays),
+        out_specs=[pl.BlockSpec(memory_space=pltpu.VMEM)] * len(lists),
+        compiler_params=pltpu.CompilerParams(vmem_limit_bytes=12 * 1024 * 1024),
+        cost_estimate=pl.CostEstimate(flops=flops, bytes_accessed=8 * sum(heights) * share, transcendentals=0),
+    )(*arrays)
+
+
+def project(upstream, weights):
+    rows, width = upstream.shape
+    hidden_share = weights.shape[2]
+    steps = 7 if width % (7 * 128) == 0 else 1
+    block = width // steps
+
+    def kernel(upstream_ref, weights_ref, out_ref):
+        @pl.when(pl.program_id(0) == 0)
+        def _():
+            out_ref[...] = jnp.zeros_like(out_ref)
+
+        for expert in range(EXPERTS):
+            out_ref[expert] += jnp.dot(
+                upstream_ref[...], weights_ref[expert], preferred_element_type=jnp.float32
+            )
+
+    return pl.pallas_call(
+        kernel,
+        out_shape=jax.ShapeDtypeStruct((EXPERTS, rows, hidden_share), jnp.float32),
+        grid=(steps,),
+        in_specs=[
+            pl.BlockSpec((rows, block), lambda i: (0, i)),
+            pl.BlockSpec((EXPERTS, block, hidden_share), lambda i: (0, i, 0)),
+        ],
+        out_specs=pl.BlockSpec((EXPERTS, rows, hidden_share), lambda i: (0, 0, 0)),
+        compiler_params=pltpu.CompilerParams(vmem_limit_bytes=VMEM),
+        cost_estimate=pl.CostEstimate(
+            flops=2 * rows * width * EXPERTS * hidden_share,
+            bytes_accessed=2 * width * (rows + EXPERTS * hidden_share),
+            transcendentals=0,
+        ),
+    )(upstream, weights)
+
+
+def expert_line(expert_ref, rows):
+    block = lax.broadcasted_iota(jnp.int32, (1, rows), 1) // BLOCK
+    line = jnp.zeros((1, rows), jnp.float32)
+    for index in range(rows // BLOCK):
+        line = jnp.where(block == index, expert_ref[index].astype(jnp.float32), line)
+    return line
+
+
+def column_of(line):
+    return jnp.broadcast_to(line, (8, line.shape[1])).T[:, :1]
+
+
+def factor_of_tokens(gate_pre, up_pre, gate_prob, row_token, block_expert, blk_index, columns):
+    rows, hidden_share = gate_pre.shape
+    quarter = rows // columns
+
+    def kernel(expert_ref, index_ref, gate_ref, up_ref, prob_ref, token_ref, out_ref):
+        gate_value = gate_ref[...].astype(jnp.float32)
+        hidden = gate_value * jax.nn.sigmoid(gate_value) * up_ref[...].astype(jnp.float32)
+        weighted = (hidden * column_of(prob_ref[...].reshape(1, rows))).astype(jnp.bfloat16)
+        place = lax.broadcasted_iota(jnp.int32, (rows, rows), 0)
+        part = place // quarter
+        token = (index_ref[0] ^ part) * quarter + (place - part * quarter)
+        choose = jnp.where(token == token_ref[...].reshape(1, rows), 1.0, 0.0).astype(jnp.bfloat16)
+        out_ref[:rows, :] = jnp.dot(choose, weighted, preferred_element_type=jnp.float32)
+        experts = jnp.broadcast_to(expert_line(expert_ref, rows), (8, rows)).astype(jnp.bfloat16)
+        marks = lax.dot_general(
+            experts, choose, (((1,), (1,)), ((), ())), preferred_element_type=jnp.float32
+        )
+        out_ref[rows:, :] = jnp.zeros((8, hidden_share), jnp.float32)
+        for first in range(0, rows, hidden_share):
+            amount = min(hidden_share, rows - first)
+            line = rows + first // hidden_share
+            out_ref[line : line + 1, :amount] = marks[:1, first : first + amount]
+
+    smem, vmem = pl.BlockSpec(memory_space=pltpu.SMEM), pl.BlockSpec(memory_space=pltpu.VMEM)
+    return pl.pallas_call(
+        kernel,
+        out_shape=jax.ShapeDtypeStruct((rows + 8, hidden_share), jnp.float32),
+        in_specs=[smem] * 2 + [vmem] * 4,
+        out_specs=vmem,
+        compiler_params=pltpu.CompilerParams(vmem_limit_bytes=VMEM),
+        cost_estimate=pl.CostEstimate(flops=2 * rows * rows * hidden_share, bytes_accessed=12 * rows * hidden_share, transcendentals=0),
+    )(block_expert, blk_index.reshape(1), gate_pre, up_pre, gate_prob, row_token)
+
+
+def row_gradients(both, gate_pre, up_pre, gate_prob, row_token, block_expert):
+    rows, hidden_share = gate_pre.shape
+
+    def kernel(expert_ref, both_ref, gate_ref, up_ref, prob_ref, token_ref, up_grad_ref, gate_grad_ref, part_ref):
+        place = lax.broadcasted_iota(jnp.int32, (rows, rows), 0)
+        mine = place == token_ref[...].reshape(1, rows)
+        expert_of_token = jnp.sum(jnp.where(mine, expert_line(expert_ref, rows), 0.0), axis=1, keepdims=True)
+        of_token = both_ref[0]
+        for expert in range(1, EXPERTS):
+            of_token = jnp.where(expert_of_token == float(expert), both_ref[expert], of_token)
+        choose = jnp.where(mine, 1.0, 0.0).astype(jnp.bfloat16)
+        projected = jnp.zeros((rows, hidden_share), jnp.float32)
+        rest = of_token
+        for _ in range(3):
+            top = rest.astype(jnp.bfloat16)
+            projected = projected + lax.dot_general(
+                choose, top, (((0,), (0,)), ((), ())), preferred_element_type=jnp.float32
+            )
+            rest = rest - top.astype(jnp.float32)
+        gate_value = gate_ref[...].astype(jnp.float32)
+        up_value = up_ref[...].astype(jnp.float32)
+        sigmoid_gate = jax.nn.sigmoid(gate_value)
+        active = gate_value * sigmoid_gate
+        scaled = column_of(prob_ref[...].reshape(1, rows)) * projected
+        up_grad_ref[...] = (scaled * active).astype(jnp.bfloat16)
+        gate_grad_ref[...] = (
+            scaled * up_value * sigmoid_gate * (1.0 + gate_value * (1.0 - sigmoid_gate))
+        ).astype(jnp.bfloat16)
+        part = jnp.sum(active * up_value * projected, axis=1, keepdims=True)
+        part_ref[...] = jnp.broadcast_to(part, (rows, 128)).T[:8, :]
+
+    smem, vmem = pl.BlockSpec(memory_space=pltpu.SMEM), pl.BlockSpec(memory_space=pltpu.VMEM)
+    return pl.pallas_call(
+        kernel,
+        out_shape=[
+            jax.ShapeDtypeStruct((rows, hidden_share), jnp.bfloat16),
+            jax.ShapeDtypeStruct((rows, hidden_share), jnp.bfloat16),
+            jax.ShapeDtypeStruct((8, rows), jnp.float32),
+        ],
+        in_specs=[smem] + [vmem] * 5,
+        out_specs=[vmem] * 3,
+        compiler_params=pltpu.CompilerParams(vmem_limit_bytes=VMEM),
+        cost_estimate=pl.CostEstimate(flops=6 * rows * rows * hidden_share, bytes_accessed=20 * rows * hidden_share, transcendentals=0),
+    )(block_expert, both, gate_pre, up_pre, gate_prob, row_token)
+
+
+def together(*values):
+    return lax.optimization_barrier(values)
+
+
+def factors_body(upstream, gate_pre, up_pre, down_weight, block_expert, row_token, gate_prob):
+    rows, width = upstream.shape
+    hidden_share = gate_pre.shape[1]
+    columns = lax.axis_size("blk")
+    wide = lax.axis_size("wide")
+    chips = wide // 2
+    quarter = rows // columns
+    half = quarter // 2
+    share = width // wide
+    blk_index = lax.axis_index("blk")
+    wide_index = lax.axis_index("wide")
+    chip = wide_index // 2
+    core = wide_index % 2
+
+    def moved(value, target):
+        pairs = []
+        for b in range(columns):
+            for z in range(chips):
+                for c in range(2):
+                    to = target(b, z, c)
+                    pairs.append((b * wide + z * 2 + c, to[0] * wide + to[1] * 2 + to[2]))
+        return lax.ppermute(value, ("blk", "wide"), pairs)
+
+    def along_x(value):
+        return moved(value, lambda b, z, c: (b ^ 1, z, c))
+
+    def along_y(value):
+        return moved(value, lambda b, z, c: (b ^ 2, z, c))
+
+    def across(value):
+        return moved(value, lambda b, z, c: (b, z, 1 - c))
+
+    def outer_swap(value):
+        return moved(value, lambda b, z, c: (b, z ^ 1, c))
+
+    def middle_swap(value):
+        return moved(value, lambda b, z, c: (b, 3 - z, c) if 0 < z < 3 else (b, z, 1 - c))
+
+    def piece_for(key, index):
+        offset, flip = key
+        first_column = share * (2 * (chip ^ offset) + (core ^ flip))
+        piece = lax.dynamic_slice(upstream, (quarter * index, first_column), (quarter, share))
+        return piece.astype(jnp.float32)
+
+    def sent(key, piece):
+        offset, flip = key
+        return moved(piece, lambda b, z, c: (b, z ^ offset, c ^ flip))
+
+    near_0 = sent((1, 0), piece_for((1, 0), blk_index))
+    skip_0 = sent((2, 0), piece_for((2, 0), blk_index))
+    (spread,) = stack_rows([[(near_0, 0, quarter), (skip_0, 0, quarter)]], EARLY)
+
+    factor = factor_of_tokens(gate_pre, up_pre, gate_prob, row_token, block_expert, blk_index, columns)
+
+    def own_columns(of_core, index):
+        first_column = share * (2 * chip + of_core)
+        parts = [
+            lax.dynamic_slice(upstream, (quarter * (index ^ q), first_column), (quarter, share))
+            for q in range(columns)
+        ]
+        return jnp.concatenate(parts, axis=0).astype(jnp.float32)
+
+    factor_near = outer_swap(factor)
+    mid_own = middle_swap(factor)
+    down_weight, _ = together(down_weight, factor)
+    spread, index = together(spread, blk_index)
+    weights = jnp.transpose(down_weight, (1, 0, 2))
+    pieces = [piece_for(key, index) for key in ((1, 1), (2, 1), (3, 0), (3, 1))]
+    own_tokens, other_tokens = own_columns(core, index), own_columns(1 - core, index)
+    other_factor = across(factor)
+
+    spread, factor_near, mid_own, other_factor, weights, pieces, other_tokens = together(
+        spread, factor_near, mid_own, other_factor, weights, pieces, other_tokens
+    )
+    piece_11, piece_21, piece_30, piece_31 = pieces
+    near_1 = sent((1, 1), piece_11)
+    skip_1 = sent((2, 1), piece_21)
+    x_0, y_0 = along_x(spread), along_y(spread)
+    (pair,) = stack_rows([[(near_1, 0, quarter), (skip_1, 0, quarter)]], EARLY)
+    both = project(upstream, weights)
+    other_tokens = across(other_tokens)
+
+    (
+        pair, x_0, y_0, both, factor_near, mid_own, other_tokens, piece_30, piece_31, gate_pre
+    ) = together(
+        pair, x_0, y_0, both, factor_near, mid_own, other_tokens, piece_30, piece_31, gate_pre
+    )
+    far_0 = sent((3, 0), piece_30)
+    (far_0,) = stack_rows([[(far_0, 0, quarter)]], EARLY)
+    mid_near = middle_swap(factor_near)
+    to_x, to_y = stack_rows(
+        [
+            [(pair, 0, 2 * quarter), (y_0, quarter, quarter)],
+            [(pair, 0, 2 * quarter), (x_0, 0, quarter)],
+        ]
+    )
+    x_1, y_1 = along_x(to_x), along_y(to_y)
+    out_own = outer_swap(mid_own)
+
+    up_grad, gate_grad, partial_value = row_gradients(both, gate_pre, up_pre, gate_prob, row_token, block_expert)
+
+    far_0, mid_near, x_1, y_1, out_own, partial_value, up_grad, gate_grad, piece_31, factor_near = together(
+        far_0, mid_near, x_1, y_1, out_own, partial_value, up_grad, gate_grad, piece_31, factor_near
+    )
+    far_1 = sent((3, 1), piece_31)
+    (far_1,) = stack_rows([[(far_1, 0, quarter)]], EARLY)
+    to_x, to_y = stack_rows(
+        [
+            [(far_0, 0, quarter), (y_1, quarter, quarter)],
+            [(far_0, 0, quarter), (x_1, 0, quarter)],
+        ]
+    )
+    x_2, y_2 = along_x(to_x), along_y(to_y)
+    out_near = outer_swap(mid_near)
+    outer = (chip == 0) | (chip == chips - 1)
+    factor_skip = jnp.where(outer, out_own, mid_near)
+    near_factor = across(factor_near)
+
+    far_1, x_2, y_2, out_near, near_factor, partial_value, factor_skip = together(
+        far_1, x_2, y_2, out_near, near_factor, partial_value, factor_skip
+    )
+    to_x, to_y = stack_rows(
+        [
+            [(far_1, 0, quarter), (y_2, quarter // 2, quarter // 2)],
+            [(far_1, 0, quarter), (x_2, 0, quarter // 2)],
+        ]
+    )
+    x_3, y_3 = along_x(to_x), along_y(to_y)
+    factor_far = jnp.where(outer, out_near, mid_own)
+    skip_factor = across(factor_skip)
+    far_factor = across(factor_far)
+    partial_value = partial_value + along_x(partial_value)
+
+    total = add_products(
+        (own_tokens, other_tokens),
+        ((0, 0, rows, 0), (1, 0, rows, rows)),
+        factor,
+        other_factor,
+        jnp.zeros((share, EXPERTS * hidden_share), jnp.float32),
+        rows,
+    )
+
+    def gathered(pairs, near, far, running, devices=0):
+        parts, pieces = [], []
+        for side, (own, x_hop, y_hop, row, diagonal) in enumerate(pairs):
+            spot = side * rows
+            base = len(parts)
+            parts += [own, x_hop, y_hop] + [hop for hop, _, _ in diagonal]
+            pieces += [
+                (base, 0, quarter, spot),
+                (base + 1, row, quarter, spot + quarter),
+                (base + 2, row, quarter, spot + 2 * quarter),
+            ]
+            spot += 3 * quarter
+            for index, (_, first, amount) in enumerate(diagonal):
+                pieces.append((base + 3 + index, first, amount, spot))
+                spot += amount
+        return add_products(tuple(parts), tuple(pieces), near, far, running, rows, devices)
+
+    half = quarter // 2
+    total = gathered(
+        (
+            (near_0, x_0, y_0, 0, ((y_1, 2 * quarter, quarter),)),
+            (near_1, x_1, y_1, 0, ((y_2, quarter, quarter),)),
+        ),
+        factor_near, near_factor, total,
+    )
+    total = gathered(
+        (
+            (skip_0, x_0, y_0, quarter, ((x_1, 2 * quarter, quarter),)),
+            (skip_1, x_1, y_1, quarter, ((x_2, quarter, quarter),)),
+        ),
+        factor_skip, skip_factor, total,
+    )
+
+    x_3, y_3, total, partial_value, far_factor = together(x_3, y_3, total, partial_value, far_factor)
+    prob_grad = (partial_value + along_y(partial_value))[0]
+    x_4, y_4 = along_x(y_3[half:quarter]), along_y(x_3[:half])
+    devices = columns * wide
+    total, sums = gathered(
+        (
+            (far_0, x_2, y_2, 0, ((y_3, quarter, half), (x_3, quarter, half))),
+            (far_1, x_3, y_3, 0, ((y_4, 0, half), (x_4, 0, half))),
+        ),
+        factor_far, far_factor, total, devices,
+    )
+
+    down_grad = total.reshape(share, EXPERTS, hidden_share)
+    spread = lax.all_to_all(sums, ("blk", "wide"), 0, 0, tiled=True)
+    total_sum = jnp.sum(spread, axis=0)[:EXPERTS]
+    grad_rms = jnp.sqrt(total_sum / float(D * FFW))
+    return (down_grad, grad_rms, prob_grad, gate_grad, up_grad)
+
+
+def sums_body(upstream, gate_pre, up_pre, down_weight, block_expert, row_token, gate_prob):
     routed = upstream[row_token]
     row_count = routed.shape[0]
     block_count = row_count // BLOCK
@@ -83,6 +505,16 @@
 
 
 def solution(mesh):
+    columns, wide = mesh.shape["blk"], mesh.shape["wide"]
+
+    def body(upstream, gate_pre, up_pre, down_weight, block_expert, row_token, gate_prob):
+        rows, width = upstream.shape
+        hidden_share = gate_pre.shape[1]
+        factors = wide * rows * (hidden_share + width // wide)
+        sums = EXPERTS * width * hidden_share
+        plan = factors_body if columns == 4 and wide == 8 and factors < sums else sums_body
+        return plan(upstream, gate_pre, up_pre, down_weight, block_expert, row_token, gate_prob)
+
     in_specs = (
         P("wide", None),
         P("wide", "blk"),

time: 294 us -> 137 us (0.47)
  waiting for transfers between devices: 144 us -> 59.9 us
  blocking collectives: 49.7 us -> 0 us
  matrix products: 33 us -> 0 us
  starting transfers between devices: 0.26 us -> 31.2 us
  local copies, waits for them, and re-layouts: 38.3 us -> 15.6 us
  Pallas kernels: 0 us -> 22.5 us
  between operations: 14.1 us -> 1.02 us
  loops' own time: 9.97 us -> 0 us
    reduce_scatter x2 -> x0, waiting for transfers between devices: 144 us -> none  [body(): lax.psum_scatter(one_expert(jnp.int32(0), lax.axis_size('wide') * row_sha...]
    ppermute x0 -> x28, waiting for transfers between devices: none -> 55.7 us  [moved(): return lax.ppermute(value, ('blk', 'wide'), pairs)]
    psum x2 -> x0, blocking collectives: 49.7 us -> none  [the longest x1 37.8 us: body(): total_sum = lax.psum(squares, ('blk', 'wide'))]
    dot_general x6 -> x0, matrix products: 33 us -> none  [the longest x3 23.3 us: block_product(): jnp.dot(column_block.T, weighted_block, preferred_element_type=jnp.float32)]
    ppermute x0 -> x28, starting transfers between devices: none -> 28 us  [moved(): return lax.ppermute(value, ('blk', 'wide'), pairs)]
    pallas_call x0 -> x14, Pallas kernels: none -> 22.5 us  [the longest x1 9.29 us: project(): pl.pallas_call(kernel, out_shape=jax.ShapeDtypeStruct((EXPERTS, rows, hid...]
    gather x1 -> x0, local copies, waits for them, and re-layouts: 16.5 us -> none  [body(): routed = upstream[row_token]]
    another operation x9 -> x0, loops' own time: 9.97 us -> none  [the longest x1 5.9 us: body(): lax.map(project, (routed_blocks, block_expert))]
  transfers between devices with their start and end apart: 2 -> 29, of which waited for: 2 -> 15; matrix products, arithmetic and copies ran while one was open for 10% -> 10% of each run, Pallas kernels for 0% -> 17%
where the time goes in v2:
time: 137 us; the launch traced here: 136 us
  waiting for transfers between devices  59.9 us (44%)
  starting transfers between devices  31.2 us (23%)
  Pallas kernels  22.5 us (16%)
  local copies, waits for them, and re-layouts  15.6 us (11%)
  other arithmetic  6.3 us (5%)
    ppermute x28, waiting for transfers between devices, moved(): return lax.ppermute(value, ('blk', 'wide'), pairs)  55.7 us
    ppermute x28, starting transfers between devices, moved(): return lax.ppermute(value, ('blk', 'wide'), pairs)  28 us
    pallas_call x1, Pallas kernels, project(): pl.pallas_call(kernel, out_shape=jax.ShapeDtypeStruct((EXPERTS, rows, hid...  9.29 us
    optimization_barrier x1, local copies, waits for them, and re-layouts, together(): return lax.optimization_barrier(values)  6.92 us
    unnamed x48, local copies, waits for them, and re-layouts  6.05 us
    pallas_call x4, Pallas kernels, add_products(): pl.pallas_call(kernel, out_shape=out_shape, in_specs=[pl.BlockSpec(memory...  5.68 us
    all_to_all x1, waiting for transfers between devices, factors_body(): spread = lax.all_to_all(sums, ('blk', 'wide'), 0, 0, tiled=True)  4.16 us
    all_to_all x1, starting transfers between devices, factors_body(): spread = lax.all_to_all(sums, ('blk', 'wide'), 0, 0, tiled=True)  3.15 us
  transfers between devices with their start and end apart: 29, of which 15 were waited for; matrix products, arithmetic and copies ran while one was open for 10% of the time, Pallas kernels for 17%

profile of v2, /device:TPU:0, one launch (start us, length us, event | category | flops | bytes accessed | tf_op | source)
XLA Modules:
  0.0 136.5 jit_solution(11156256616476814998)
XLA Ops:
  0.7 1.1 dynamic-slice_convert_fusion.4
  1.7 3.1 %collective-permute-start = (f32[96,896]{1,0:T(8,128)S(1)}, f32[96,896]{1,0:T(8,128)S(1)}, u32[]{:S(2)}, u32[]{:S(2)}) collective-permute-start(f32[96,896]{1,0:T(8,128)S(1)} %get-tuple-element.130), channel_id=1, source_target_pairs={{0,2},{1,3},{2,0},{3,1},{4,6},{5,7},{6,4},{7,5},{8,10},{9,11},{10,... | collective-permute-start | bytes 1032200 | tf_op jit(solution)/shard_map/ppermute | solution.py:261
  4.8 2.6 %collective-permute-start.1 = (f32[96,896]{1,0:T(8,128)S(1)}, f32[96,896]{1,0:T(8,128)S(1)}, u32[]{:S(2)}, u32[]{:S(2)}) collective-permute-start(f32[96,896]{1,0:T(8,128)S(1)} %get-tuple-element.129), channel_id=1, source_target_pairs={{0,4},{1,5},{2,6},{3,7},{4,0},{5,1},{6,2},{7,3},{8,12},{9,13},{10,... | collective-permute-start | bytes 1032200 | tf_op jit(solution)/shard_map/ppermute | solution.py:261
  7.4 2.4 %shard_map.111.refs_2_ = f32[392,256]{1,0:T(8,128)} custom-call(s32[3]{0:T(128)} %expert_ref.3, s32[1]{0:T(128)} %bitcast.index_ref, bf16[384,256]{1,0:T(8,128)(2,1)} %gate_ref.2, bf16[384,256]{1,0:T(8,128)(2,1)} %up_ref.3, f32[384]{0:T(512)} %prob_ref.3, s32[384]{0:T(512)} %token_ref.3), custom_call_target="tpu_custom_call" | custom-call | flops 75497472 | bytes 1179648 | tf_op jit(solution)/shard_map/pallas_call | solution.py:180
  10.7 6.9 %copy.16 = bf16[7168,2,256]{2,0,1:T(8,128)(2,1)} copy(bf16[7168,2,256]{2,1,0:T(2,128)(2,1)} %param.10) | data formatting | bytes 14680064 | tf_op jit(solution)/shard_map/optimization_barrier | solution.py:237
  17.6 2.7 %collective-permute-done.refs_0_ = f32[96,896]{1,0:T(8,128)S(1)} collective-permute-done((f32[96,896]{1,0:T(8,128)S(1)}, f32[96,896]{1,0:T(8,128)S(1)}, u32[]{:S(2)}, u32[]{:S(2)}) %collective-permute-start) | collective-permute-done | bytes 344096 | tf_op jit(solution)/shard_map/ppermute | solution.py:261
  20.3 3.8 %collective-permute-done.1.refs_1_.refs_0_ = f32[96,896]{1,0:T(8,128)S(1)} collective-permute-done((f32[96,896]{1,0:T(8,128)S(1)}, f32[96,896]{1,0:T(8,128)S(1)}, u32[]{:S(2)}, u32[]{:S(2)}) %collective-permute-start.1) | collective-permute-done | bytes 344096 | tf_op jit(solution)/shard_map/ppermute | solution.py:261
  24.9 2.8 %fusion.1 = (bf16[96,896]{1,0:T(8,128)(2,1)}, bf16[96,896]{1,0:T(8,128)(2,1)}, bf16[96,896]{1,0:T(8,128)(2,1)S(1)}, bf16[96,896]{1,0:T(8,128)(2,1)S(1)}, bf16[96...) fusion(bf16[384,7168]{1,0:T(8,128)(2,1)} %upstream_ref.1, ...), kind=kLoop, calls=%fused_computation.14 | loop fusion | flops 344064 | bytes 4816936 | tf_op jit(solution)/shard_map/dynamic_slice | solution.py:297
  27.7 1.1 collective-permute-done.2.refs_8_
  28.9 0.8 copy-done.9
  29.7 1.3 collective-permute-start.5
  31.0 2.8 %collective-permute-start.6 = (f32[96,896]{1,0:T(8,128)S(1)}, f32[96,896]{1,0:T(8,128)S(1)}, u32[]{:S(2)}, u32[]{:S(2)}) collective-permute-start(f32[96,896]{1,0:T(8,128)S(1)} %get-tuple-element.65), channel_id=1, source_target_pairs={{0,5},{1,4},{2,7},{3,6},{4,1},{5,0},{6,3},{7,2},{8,13},{9,12},{10,... | collective-permute-start | bytes 1032200 | tf_op jit(solution)/shard_map/ppermute | solution.py:261
  33.8 1.5 %collective-permute-start.7 = (f32[192,896]{1,0:T(8,128)S(1)}, f32[192,896]{1,0:T(8,128)S(1)}, u32[]{:S(2)}, u32[]{:S(2)}) collective-permute-start(f32[192,896]{1,0:T(8,128)S(1)} %shard_map.110), channel_id=1, source_target_pairs={{0,8},{1,9},{2,10},{3,11},{4,12},{5,13},{6,14},{7,15},{8,0},{9,1},... | collective-permute-start | bytes 2064392 | tf_op jit(solution)/shard_map/ppermute | solution.py:261
  35.2 1.5 %collective-permute-start.8 = (f32[192,896]{1,0:T(8,128)S(1)}, f32[192,896]{1,0:T(8,128)S(1)}, u32[]{:S(2)}, u32[]{:S(2)}) collective-permute-start(f32[192,896]{1,0:T(8,128)S(1)} %shard_map.110), channel_id=1, source_target_pairs={{0,16},{1,17},{2,18},{3,19},{4,20},{5,21},{6,22},{7,23},{8,24},{9,... | collective-permute-start | bytes 2064392 | tf_op jit(solution)/shard_map/ppermute | solution.py:261
  36.8 9.3 %shard_map.113.both_ref = f32[2,384,256]{2,1,0:T(8,128)} custom-call(bf16[384,7168]{1,0:T(8,128)(2,1)} %upstream_ref.1, bf16[2,7168,256]{2,1,0:T(8,128)(2,1)} %bitcast.7), custom_call_target="tpu_custom_call" | custom-call | flops 2818572288 | bytes 12845056 | tf_op jit(solution)/shard_map/pallas_call | solution.py:126
  46.1 0.7 copy-done.15
  46.9 0.8 copy-done.17
  47.6 3.5 %collective-permute-done.7.refs_2_.refs_1_ = f32[192,896]{1,0:T(8,128)S(1)} collective-permute-done((f32[192,896]{1,0:T(8,128)S(1)}, f32[192,896]{1,0:T(8,128)S(1)}, u32[]{:S(2)}, u32[]{:S(2)}) %collective-permute-start.7) | collective-permute-done | bytes 688160 | tf_op jit(solution)/shard_map/ppermute | solution.py:261
  51.2 1.2 collective-permute-done.8.refs_1_.refs_2_
  52.4 1.3 collective-permute-start.10
  54.1 1.8 %collective-permute-start.13 = (f32[288,896]{1,0:T(8,128)S(1)}, f32[288,896]{1,0:T(8,128)S(1)}, u32[]{:S(2)}, u32[]{:S(2)}) collective-permute-start(f32[288,896]{1,0:T(8,128)S(1)} %get-tuple-element.79), channel_id=1, source_target_pairs={{0,16},{1,17},{2,18},{3,19},{4,20},{5,21},{6,22},{7,23},{8,24},{9,... | collective-permute-start | bytes 3096584 | tf_op jit(solution)/shard_map/ppermute | solution.py:261
  56.1 1.2 collective-permute-start.14
  57.2 2.8 %shard_map.116 = (bf16[384,256]{1,0:T(8,128)(2,1)}, bf16[384,256]{1,0:T(8,128)(2,1)}, f32[8,384]{1,0:T(8,128)}) custom-call(s32[3]{0:T(128)} %expert_ref.3, f32[2,384,256]{2,1,0:T(8,128)} %shard_map.113.both_ref, bf16[384,256]{1,0:T(8,128)(2,1)} %gate_ref.2, bf16[384,256]{1,0:T(8,128)(2,1)} %up_ref.3, f32[384]{0:T(512)} %prob_ref.3, s32[384]{0:T(512)} %token_ref.3), custom_call_target="tpu_custom_call" | custom-call | flops 226492416 | bytes 1966080 | tf_op jit(solution)/shard_map/pallas_call | solution.py:222
  60.1 5.4 %collective-permute-done.10.refs_0_ = f32[96,896]{1,0:T(8,128)} collective-permute-done((f32[96,896]{1,0:T(8,128)}, f32[96,896]{1,0:T(8,128)}, u32[]{:S(2)}, u32[]{:S(2)}) %collective-permute-start.10) | collective-permute-done | bytes 344096 | tf_op jit(solution)/shard_map/ppermute | solution.py:261
  65.5 1.0 shard_map.114.refs_0_
  67.2 4.9 %collective-permute-done.14 = f32[392,256]{1,0:T(8,128)} collective-permute-done((f32[392,256]{1,0:T(8,128)}, f32[392,256]{1,0:T(8,128)}, u32[]{:S(2)}, u32[]{:S(2)}) %collective-permute-start.14) | collective-permute-done | bytes 401440 | tf_op jit(solution)/shard_map/ppermute | solution.py:261
  72.1 6.3 %collective-permute-done.12.refs_2_.refs_5_.refs_3_ = f32[288,896]{1,0:T(8,128)S(1)} collective-permute-done((f32[288,896]{1,0:T(8,128)S(1)}, f32[288,896]{1,0:T(8,128)S(1)}, u32[]{:S(2)}, u32[]{:S(2)}) %collective-permute-start.12) | collective-permute-done | bytes 1032224 | tf_op jit(solution)/shard_map/ppermute | solution.py:261
  78.4 1.1 collective-permute-done.13.refs_1_.refs_3_.refs_6_
  79.5 1.0 copy-done.4
  81.3 1.5 %collective-permute-start.17 = (f32[192,896]{1,0:T(8,128)S(1)}, f32[192,896]{1,0:T(8,128)S(1)}, u32[]{:S(2)}, u32[]{:S(2)}) collective-permute-start(f32[192,896]{1,0:T(8,128)S(1)} %get-tuple-element.92), channel_id=1, source_target_pairs={{0,16},{1,17},{2,18},{3,19},{4,20},{5,21},{6,22},{7,23},{8,24},{9,... | collective-permute-start | bytes 2064392 | tf_op jit(solution)/shard_map/ppermute | solution.py:261
  82.8 0.9 collective-permute-start.19
  83.7 1.1 broadcast_select_fusion.1.refs_8_
  84.8 7.3 %collective-permute-done.15.refs_0_ = f32[96,896]{1,0:T(8,128)} collective-permute-done((f32[96,896]{1,0:T(8,128)}, f32[96,896]{1,0:T(8,128)}, u32[]{:S(2)}, u32[]{:S(2)}) %collective-permute-start.15) | collective-permute-done | bytes 344096 | tf_op jit(solution)/shard_map/ppermute | solution.py:261
  92.1 1.0 shard_map.117.refs_0_.refs_5_
  93.2 7.4 %collective-permute-done.18 = f32[392,256]{1,0:T(8,128)S(1)} collective-permute-done((f32[392,256]{1,0:T(8,128)}, f32[392,256]{1,0:T(8,128)S(1)}, u32[]{:S(2)}, u32[]{:S(2)}) %collective-permute-start.18) | collective-permute-done | bytes 401440 | tf_op jit(solution)/shard_map/ppermute | solution.py:261
  101.4 1.3 collective-permute-start.21
  104.5 1.2 shard_map.120.refs_10_
  105.8 1.7 %collective-permute-start.23 = (f32[8,384]{1,0:T(8,128)S(1)}, f32[8,384]{1,0:T(8,128)S(1)}, u32[]{:S(2)}, u32[]{:S(2)}) collective-permute-start(f32[8,384]{1,0:T(8,128)S(1)} %copy-done.23), channel_id=1, source_target_pairs={{0,8},{1,9},{2,10},{3,11},{4,12},{5,13},{6,14},{7,15},{8,0},{9,1},... | collective-permute-start | bytes 36872 | tf_op jit(solution)/shard_map/ppermute | solution.py:261
  107.5 1.2 shard_map.121.refs_10_
  108.7 6.5 %collective-permute-done.23 = f32[8,384]{1,0:T(8,128)S(1)} collective-permute-done((f32[8,384]{1,0:T(8,128)S(1)}, f32[8,384]{1,0:T(8,128)S(1)}, u32[]{:S(2)}, u32[]{:S(2)}) %collective-permute-start.23) | collective-permute-done | bytes 12320 | tf_op jit(solution)/shard_map/ppermute | solution.py:261
  115.3 1.2 shard_map.122.refs_12_
  116.6 1.4 %collective-permute-start.25 = (f32[48,896]{1,0:T(8,128)S(1)}, f32[48,896]{1,0:T(8,128)S(1)}, u32[]{:S(2)}, u32[]{:S(2)}) collective-permute-start(f32[48,896]{1,0:T(8,128)S(1)} %slice.12), channel_id=1, source_target_pairs={{0,16},{1,17},{2,18},{3,19},{4,20},{5,21},{6,22},{7,23},{8,24},{9,... | collective-permute-start | bytes 516104 | tf_op jit(solution)/shard_map/ppermute | solution.py:261
  119.3 3.4 %collective-permute-done.25.refs_8_ = f32[48,896]{1,0:T(8,128)S(1)} collective-permute-done((f32[48,896]{1,0:T(8,128)S(1)}, f32[48,896]{1,0:T(8,128)S(1)}, u32[]{:S(2)}, u32[]{:S(2)}) %collective-permute-start.25) | collective-permute-done | bytes 172064 | tf_op jit(solution)/shard_map/ppermute | solution.py:261
  122.6 1.0 collective-permute-done.26.refs_9_
  123.6 2.0 %shard_map.123 = (f32[896,512]{1,0:T(8,128)S(1)}, f32[32,128]{1,0:T(8,128)}) custom-call(f32[96,896]{1,0:T(8,128)S(1)} %copy-done.5, f32[192,896]{1,0:T(8,128)S(1)} %collective-permute-done.16.refs_2_.refs_7_.refs_1_, f32[192,896]{1,0:T(8,128)S(1)} %collective-permute-done.17.refs_1_.refs_7_.refs_2_, f32[144,896]{1,0:T(8,128)S(1)} %collective-permute-done.21.refs_3_.refs_7_, ...), custom_call_target="tpu_custom_call" | custom-call | flops 704643072 | bytes 7208960 | tf_op jit(solution)/shard_map/pallas_call | solution.py:61
  125.6 3.2 %all-to-all-start = ((f32[32,1,128]{2,1,0:T(1,128)}), f32[32,1,128]{2,1,0:T(1,128)S(1)}, u32[]{:S(2)}, u32[]{:S(2)}) async-start(f32[32,1,128]{2,1,0:T(1,128)} %bitcast.3), calls=%async_computation | async-start | bytes 32768 | tf_op jit(solution)/shard_map/all_to_all | solution.py:428
  129.4 2.4 %reshape.19 = f32[896,2,256]{2,1,0:T(2,128)} reshape(f32[896,512]{1,0:T(8,128)S(1)} %get-tuple-element.112) | data formatting | bytes 3670016 | tf_op jit(solution)/shard_map/reshape | solution.py:427
  131.8 4.2 %all-to-all-done = f32[32,1,128]{2,1,0:T(1,128)S(1)} async-done(((f32[32,1,128]{2,1,0:T(1,128)}), f32[32,1,128]{2,1,0:T(1,128)S(1)}, u32[]{:S(2)}, u32[]{:S(2)}) %all-to-all-start) | async-done | bytes 16416 | tf_op jit(solution)/shard_map/all_to_all | solution.py:428
  (87 shorter events, 8.9 us)
Async XLA Ops:
  1.7 18.6 %collective-permute-start = (f32[96,896]{1,0:T(8,128)S(1)}, f32[96,896]{1,0:T(8,128)S(1)}, u32[]{:S(2)}, u32[]{:S(2)}) collective-permute-start(f32[96,896]{1,0:T(8,128)S(1)} %get-tuple-element.130), channel_id=1, source_target_pairs={{0,2},{1,3},{2,0},{3,1},{4,6},{5,7},{6,4},{7,5},{8,10},{9,11},{10,... | collective-permute-start | bytes 1032200 | tf_op jit(solution)/shard_map/ppermute | solution.py:261
  4.8 19.3 %collective-permute-start.1 = (f32[96,896]{1,0:T(8,128)S(1)}, f32[96,896]{1,0:T(8,128)S(1)}, u32[]{:S(2)}, u32[]{:S(2)}) collective-permute-start(f32[96,896]{1,0:T(8,128)S(1)} %get-tuple-element.129), channel_id=1, source_target_pairs={{0,4},{1,5},{2,6},{3,7},{4,0},{5,1},{6,2},{7,3},{8,12},{9,13},{10,... | collective-permute-start | bytes 1032200 | tf_op jit(solution)/shard_map/ppermute | solution.py:261
  9.8 19.1 %collective-permute-start.2 = (f32[392,256]{1,0:T(8,128)}, f32[392,256]{1,0:T(8,128)S(1)}, u32[]{:S(2)}, u32[]{:S(2)}) collective-permute-start(f32[392,256]{1,0:T(8,128)} %shard_map.111.refs_2_), channel_id=1, source_target_pairs={{0,2},{1,3},{2,0},{3,1},{4,6},{5,7},{6,4},{7,5},{8,10},{9,11},{10,... | collective-permute-start | bytes 1204232 | tf_op jit(solution)/shard_map/ppermute | solution.py:261
  10.2 18.6 %collective-permute-start.3 = (f32[392,256]{1,0:T(8,128)}, f32[392,256]{1,0:T(8,128)}, u32[]{:S(2)}, u32[]{:S(2)}) collective-permute-start(f32[392,256]{1,0:T(8,128)} %shard_map.111.refs_2_), channel_id=1, source_target_pairs={{0,1},{1,0},{2,4},{3,5},{4,2},{5,3},{6,7},{7,6},{8,9},{9,8},{10,12... | collective-permute-start | bytes 1204232 | tf_op jit(solution)/shard_map/ppermute | solution.py:261
  10.2 18.6 %collective-permute-start.4 = (f32[392,256]{1,0:T(8,128)}, f32[392,256]{1,0:T(8,128)S(1)}, u32[]{:S(2)}, u32[]{:S(2)}) collective-permute-start(f32[392,256]{1,0:T(8,128)} %shard_map.111.refs_2_), channel_id=1, source_target_pairs={{0,1},{1,0},{2,3},{3,2},{4,5},{5,4},{6,7},{7,6},{8,9},{9,8},{10,11... | collective-permute-start | bytes 1204232 | tf_op jit(solution)/shard_map/ppermute | solution.py:261
  20.3 3.8 %copy-start.13 = (f32[96,896]{1,0:T(8,128)}, f32[96,896]{1,0:T(8,128)S(1)}, u32[]{:S(2)}) copy-start(f32[96,896]{1,0:T(8,128)S(1)} %collective-permute-done.refs_0_) | copy-start | bytes 1032196
  28.9 2.1 %copy-start.6 = (f32[392,256]{1,0:T(8,128)}, f32[392,256]{1,0:T(8,128)S(1)}, u32[]{:S(2)}) copy-start(f32[392,256]{1,0:T(8,128)S(1)} %collective-permute-done.2.refs_8_) | copy-start | bytes 1204228
  29.7 16.4 %collective-permute-start.5 = (f32[96,896]{1,0:T(8,128)S(1)}, f32[96,896]{1,0:T(8,128)S(1)}, u32[]{:S(2)}, u32[]{:S(2)}) collective-permute-start(f32[96,896]{1,0:T(8,128)S(1)} %get-tuple-element.64), channel_id=1, source_target_pairs={{0,3},{1,2},{2,1},{3,0},{4,7},{5,6},{6,5},{7,4},{8,11},{9,10},{10,... | collective-permute-start | bytes 1032200 | tf_op jit(solution)/shard_map/ppermute | solution.py:261
  31.0 15.1 %collective-permute-start.6 = (f32[96,896]{1,0:T(8,128)S(1)}, f32[96,896]{1,0:T(8,128)S(1)}, u32[]{:S(2)}, u32[]{:S(2)}) collective-permute-start(f32[96,896]{1,0:T(8,128)S(1)} %get-tuple-element.65), channel_id=1, source_target_pairs={{0,5},{1,4},{2,7},{3,6},{4,1},{5,0},{6,3},{7,2},{8,13},{9,12},{10,... | collective-permute-start | bytes 1032200 | tf_op jit(solution)/shard_map/ppermute | solution.py:261
  33.8 17.4 %collective-permute-start.7 = (f32[192,896]{1,0:T(8,128)S(1)}, f32[192,896]{1,0:T(8,128)S(1)}, u32[]{:S(2)}, u32[]{:S(2)}) collective-permute-start(f32[192,896]{1,0:T(8,128)S(1)} %shard_map.110), channel_id=1, source_target_pairs={{0,8},{1,9},{2,10},{3,11},{4,12},{5,13},{6,14},{7,15},{8,0},{9,1},... | collective-permute-start | bytes 2064392 | tf_op jit(solution)/shard_map/ppermute | solution.py:261
  35.2 17.1 %collective-permute-start.8 = (f32[192,896]{1,0:T(8,128)S(1)}, f32[192,896]{1,0:T(8,128)S(1)}, u32[]{:S(2)}, u32[]{:S(2)}) collective-permute-start(f32[192,896]{1,0:T(8,128)S(1)} %shard_map.110), channel_id=1, source_target_pairs={{0,16},{1,17},{2,18},{3,19},{4,20},{5,21},{6,22},{7,23},{8,24},{9,... | collective-permute-start | bytes 2064392 | tf_op jit(solution)/shard_map/ppermute | solution.py:261
  36.8 15.6 %collective-permute-start.9 = (f32[384,896]{1,0:T(8,128)S(1)}, f32[384,896]{1,0:T(8,128)S(1)}, u32[]{:S(2)}, u32[]{:S(2)}) collective-permute-start(f32[384,896]{1,0:T(8,128)S(1)} %maximum_convert_fusion), channel_id=1, source_target_pairs={{0,1},{1,0},{2,3},{3,2},{4,5},{5,4},{6,7},{7,6},{8,9},{9,8},{10,11... | collective-permute-start | bytes 4128776 | tf_op jit(solution)/shard_map/ppermute | solution.py:261
  47.6 8.3 %copy-start.7 = (f32[392,256]{1,0:T(8,128)S(1)}, f32[392,256]{1,0:T(8,128)}, u32[]{:S(2)}) copy-start(f32[392,256]{1,0:T(8,128)} %copy-done.6) | copy-start | bytes 1204228
  52.4 7.7 %copy-start.1 = (f32[384,896]{1,0:T(8,128)}, f32[384,896]{1,0:T(8,128)S(1)}, u32[]{:S(2)}) copy-start(f32[384,896]{1,0:T(8,128)S(1)} %collective-permute-done.9.refs_1_) | copy-start | bytes 4128772
  52.4 13.1 %collective-permute-start.10 = (f32[96,896]{1,0:T(8,128)}, f32[96,896]{1,0:T(8,128)}, u32[]{:S(2)}, u32[]{:S(2)}) collective-permute-start(f32[96,896]{1,0:T(8,128)} %get-tuple-element.73), channel_id=1, source_target_pairs={{0,6},{1,7},{2,4},{3,5},{4,2},{5,3},{6,0},{7,1},{8,14},{9,15},{10,... | collective-permute-start | bytes 1032200 | tf_op jit(solution)/shard_map/ppermute | solution.py:261
  53.8 24.6 %collective-permute-start.12 = (f32[288,896]{1,0:T(8,128)S(1)}, f32[288,896]{1,0:T(8,128)S(1)}, u32[]{:S(2)}, u32[]{:S(2)}) collective-permute-start(f32[288,896]{1,0:T(8,128)S(1)} %get-tuple-element.78), channel_id=1, source_target_pairs={{0,8},{1,9},{2,10},{3,11},{4,12},{5,13},{6,14},{7,15},{8,0},{9,1},... | collective-permute-start | bytes 3096584 | tf_op jit(solution)/shard_map/ppermute | solution.py:261
  54.1 25.5 %collective-permute-start.13 = (f32[288,896]{1,0:T(8,128)S(1)}, f32[288,896]{1,0:T(8,128)S(1)}, u32[]{:S(2)}, u32[]{:S(2)}) collective-permute-start(f32[288,896]{1,0:T(8,128)S(1)} %get-tuple-element.79), channel_id=1, source_target_pairs={{0,16},{1,17},{2,18},{3,19},{4,20},{5,21},{6,22},{7,23},{8,24},{9,... | collective-permute-start | bytes 3096584 | tf_op jit(solution)/shard_map/ppermute | solution.py:261
  55.9 11.3 %collective-permute-start.11 = (f32[392,256]{1,0:T(8,128)S(1)}, f32[392,256]{1,0:T(8,128)}, u32[]{:S(2)}, u32[]{:S(2)}) collective-permute-start(f32[392,256]{1,0:T(8,128)S(1)} %copy-done.7), channel_id=1, source_target_pairs={{0,1},{1,0},{2,4},{3,5},{4,2},{5,3},{6,7},{7,6},{8,9},{9,8},{10,12... | collective-permute-start | bytes 1204232 | tf_op jit(solution)/shard_map/ppermute | solution.py:261
  56.1 16.0 %collective-permute-start.14 = (f32[392,256]{1,0:T(8,128)}, f32[392,256]{1,0:T(8,128)}, u32[]{:S(2)}, u32[]{:S(2)}) collective-permute-start(f32[392,256]{1,0:T(8,128)} %collective-permute-done.3), channel_id=1, source_target_pairs={{0,2},{1,3},{2,0},{3,1},{4,6},{5,7},{6,4},{7,5},{8,10},{9,11},{10,... | collective-permute-start | bytes 1204232 | tf_op jit(solution)/shard_map/ppermute | solution.py:261
  79.5 12.6 %collective-permute-start.15 = (f32[96,896]{1,0:T(8,128)}, f32[96,896]{1,0:T(8,128)}, u32[]{:S(2)}, u32[]{:S(2)}) collective-permute-start(f32[96,896]{1,0:T(8,128)} %get-tuple-element.88), channel_id=1, source_target_pairs={{0,7},{1,6},{2,5},{3,4},{4,3},{5,2},{6,1},{7,0},{8,15},{9,14},{10,... | collective-permute-start | bytes 1032200 | tf_op jit(solution)/shard_map/ppermute | solution.py:261
  79.5 1.0 copy-start.4
  80.5 2.3 %copy-start.8 = (f32[392,256]{1,0:T(8,128)S(1)}, f32[392,256]{1,0:T(8,128)}, u32[]{:S(2)}) copy-start(f32[392,256]{1,0:T(8,128)} %copy-done.6) | copy-start | bytes 1204228
  80.6 20.0 %collective-permute-start.16 = (f32[192,896]{1,0:T(8,128)S(1)}, f32[192,896]{1,0:T(8,128)S(1)}, u32[]{:S(2)}, u32[]{:S(2)}) collective-permute-start(f32[192,896]{1,0:T(8,128)S(1)} %get-tuple-element.91), channel_id=1, source_target_pairs={{0,8},{1,9},{2,10},{3,11},{4,12},{5,13},{6,14},{7,15},{8,0},{9,1},... | collective-permute-start | bytes 2064392 | tf_op jit(solution)/shard_map/ppermute | solution.py:261
  81.3 19.3 %collective-permute-start.17 = (f32[192,896]{1,0:T(8,128)S(1)}, f32[192,896]{1,0:T(8,128)S(1)}, u32[]{:S(2)}, u32[]{:S(2)}) collective-permute-start(f32[192,896]{1,0:T(8,128)S(1)} %get-tuple-element.92), channel_id=1, source_target_pairs={{0,16},{1,17},{2,18},{3,19},{4,20},{5,21},{6,22},{7,23},{8,24},{9,... | collective-permute-start | bytes 2064392 | tf_op jit(solution)/shard_map/ppermute | solution.py:261
  82.8 17.8 %collective-permute-start.18 = (f32[392,256]{1,0:T(8,128)}, f32[392,256]{1,0:T(8,128)S(1)}, u32[]{:S(2)}, u32[]{:S(2)}) collective-permute-start(f32[392,256]{1,0:T(8,128)} %collective-permute-done.11), channel_id=1, source_target_pairs={{0,2},{1,3},{2,0},{3,1},{4,6},{5,7},{6,4},{7,5},{8,10},{9,11},{10,... | collective-permute-start | bytes 1204232 | tf_op jit(solution)/shard_map/ppermute | solution.py:261
  82.8 17.8 %collective-permute-start.19 = (f32[392,256]{1,0:T(8,128)S(1)}, f32[392,256]{1,0:T(8,128)S(1)}, u32[]{:S(2)}, u32[]{:S(2)}) collective-permute-start(f32[392,256]{1,0:T(8,128)S(1)} %copy-done.8), channel_id=1, source_target_pairs={{0,1},{1,0},{2,3},{3,2},{4,5},{5,4},{6,7},{7,6},{8,9},{9,8},{10,11... | collective-permute-start | bytes 1204232 | tf_op jit(solution)/shard_map/ppermute | solution.py:261
  93.1 9.7 %copy-start.19 = (bf16[96,896]{1,0:T(8,128)(2,1)S(1)}, bf16[96,896]{1,0:T(8,128)(2,1)}, u32[]{:S(2)}) copy-start(bf16[96,896]{1,0:T(8,128)(2,1)} %get-tuple-element.117) | copy-start | bytes 516100
  93.1 9.7 %copy-start.20 = (bf16[96,896]{1,0:T(8,128)(2,1)S(1)}, bf16[96,896]{1,0:T(8,128)(2,1)}, u32[]{:S(2)}) copy-start(bf16[96,896]{1,0:T(8,128)(2,1)} %get-tuple-element.118) | copy-start | bytes 516100
  93.2 9.7 %copy-start.21 = (bf16[96,896]{1,0:T(8,128)(2,1)S(1)}, bf16[96,896]{1,0:T(8,128)(2,1)}, u32[]{:S(2)}) copy-start(bf16[96,896]{1,0:T(8,128)(2,1)} %get-tuple-element.127) | copy-start | bytes 516100
  93.2 9.7 %copy-start.22 = (bf16[96,896]{1,0:T(8,128)(2,1)S(1)}, bf16[96,896]{1,0:T(8,128)(2,1)}, u32[]{:S(2)}) copy-start(bf16[96,896]{1,0:T(8,128)(2,1)} %get-tuple-element.128) | copy-start | bytes 516100
  100.6 14.6 %collective-permute-start.22 = (f32[392,256]{1,0:T(8,128)S(1)}, f32[392,256]{1,0:T(8,128)S(1)}, u32[]{:S(2)}, u32[]{:S(2)}) collective-permute-start(f32[392,256]{1,0:T(8,128)S(1)} %broadcast_select_fusion.1.refs_8_), channel_id=1, source_target_pairs={{0,1},{1,0},{2,3},{3,2},{4,5},{5,4},{6,7},{7,6},{8,9},{9,8},{10,11... | collective-permute-start | bytes 1204232 | tf_op jit(solution)/shard_map/ppermute | solution.py:261
  100.9 15.7 %collective-permute-start.20 = (f32[144,896]{1,0:T(8,128)S(1)}, f32[144,896]{1,0:T(8,128)S(1)}, u32[]{:S(2)}, u32[]{:S(2)}) collective-permute-start(f32[144,896]{1,0:T(8,128)S(1)} %get-tuple-element.100), channel_id=1, source_target_pairs={{0,8},{1,9},{2,10},{3,11},{4,12},{5,13},{6,14},{7,15},{8,0},{9,1},... | collective-permute-start | bytes 1548296 | tf_op jit(solution)/shard_map/ppermute | solution.py:261
  101.4 15.2 %collective-permute-start.21 = (f32[144,896]{1,0:T(8,128)S(1)}, f32[144,896]{1,0:T(8,128)S(1)}, u32[]{:S(2)}, u32[]{:S(2)}) collective-permute-start(f32[144,896]{1,0:T(8,128)S(1)} %get-tuple-element.101), channel_id=1, source_target_pairs={{0,16},{1,17},{2,18},{3,19},{4,20},{5,21},{6,22},{7,23},{8,24},{9,... | collective-permute-start | bytes 1548296 | tf_op jit(solution)/shard_map/ppermute | solution.py:261
  102.8 13.8 %collective-permute-start.24 = (f32[392,256]{1,0:T(8,128)S(1)}, f32[392,256]{1,0:T(8,128)S(1)}, u32[]{:S(2)}, u32[]{:S(2)}) collective-permute-start(f32[392,256]{1,0:T(8,128)S(1)} %broadcast_select_fusion.refs_10_), channel_id=1, source_target_pairs={{0,1},{1,0},{2,3},{3,2},{4,5},{5,4},{6,7},{7,6},{8,9},{9,8},{10,11... | collective-permute-start | bytes 1204232 | tf_op jit(solution)/shard_map/ppermute | solution.py:261
  102.9 1.0 copy-start.10
  103.0 1.0 copy-start
  103.0 1.5 %copy-start.2 = (f32[384,896]{1,0:T(8,128)S(1)}, f32[384,896]{1,0:T(8,128)}, u32[]{:S(2)}) copy-start(f32[384,896]{1,0:T(8,128)} %copy-done.1) | copy-start | bytes 4128772
  104.5 1.2 copy-start.23
  104.5 3.0 %copy-start.14 = (f32[96,896]{1,0:T(8,128)S(1)}, f32[96,896]{1,0:T(8,128)}, u32[]{:S(2)}) copy-start(f32[96,896]{1,0:T(8,128)} %copy-done.13) | copy-start | bytes 1032196
  104.5 3.0 %copy-start.18 = (f32[96,896]{1,0:T(8,128)S(1)}, f32[96,896]{1,0:T(8,128)}, u32[]{:S(2)}) copy-start(f32[96,896]{1,0:T(8,128)} %copy-done.17) | copy-start | bytes 1032196
  105.8 9.5 %copy-start.12 = (f32[96,896]{1,0:T(8,128)S(1)}, f32[96,896]{1,0:T(8,128)}, u32[]{:S(2)}) copy-start(f32[96,896]{1,0:T(8,128)} %copy-done.11) | copy-start | bytes 1032196
  105.8 9.5 %copy-start.16 = (f32[96,896]{1,0:T(8,128)S(1)}, f32[96,896]{1,0:T(8,128)}, u32[]{:S(2)}) copy-start(f32[96,896]{1,0:T(8,128)} %copy-done.15) | copy-start | bytes 1032196
  105.8 9.5 %collective-permute-start.23 = (f32[8,384]{1,0:T(8,128)S(1)}, f32[8,384]{1,0:T(8,128)S(1)}, u32[]{:S(2)}, u32[]{:S(2)}) collective-permute-start(f32[8,384]{1,0:T(8,128)S(1)} %copy-done.23), channel_id=1, source_target_pairs={{0,8},{1,9},{2,10},{3,11},{4,12},{5,13},{6,14},{7,15},{8,0},{9,1},... | collective-permute-start | bytes 36872 | tf_op jit(solution)/shard_map/ppermute | solution.py:261
  115.3 8.4 %copy-start.5 = (f32[96,896]{1,0:T(8,128)S(1)}, f32[96,896]{1,0:T(8,128)}, u32[]{:S(2)}) copy-start(f32[96,896]{1,0:T(8,128)} %copy-done.3) | copy-start | bytes 1032196
  116.6 6.0 %collective-permute-start.25 = (f32[48,896]{1,0:T(8,128)S(1)}, f32[48,896]{1,0:T(8,128)S(1)}, u32[]{:S(2)}, u32[]{:S(2)}) collective-permute-start(f32[48,896]{1,0:T(8,128)S(1)} %slice.12), channel_id=1, source_target_pairs={{0,16},{1,17},{2,18},{3,19},{4,20},{5,21},{6,22},{7,23},{8,24},{9,... | collective-permute-start | bytes 516104 | tf_op jit(solution)/shard_map/ppermute | solution.py:261
  118.0 5.6 %collective-permute-start.26 = (f32[48,896]{1,0:T(8,128)S(1)}, f32[48,896]{1,0:T(8,128)S(1)}, u32[]{:S(2)}, u32[]{:S(2)}) collective-permute-start(f32[48,896]{1,0:T(8,128)S(1)} %slice.13), channel_id=1, source_target_pairs={{0,8},{1,9},{2,10},{3,11},{4,12},{5,13},{6,14},{7,15},{8,0},{9,1},... | collective-permute-start | bytes 516104 | tf_op jit(solution)/shard_map/ppermute | solution.py:261
  118.6 10.2 %collective-permute-start.27 = (f32[8,384]{1,0:T(8,128)S(1)}, f32[8,384]{1,0:T(8,128)S(1)}, u32[]{:S(2)}, u32[]{:S(2)}) collective-permute-start(f32[8,384]{1,0:T(8,128)S(1)} %add.111), channel_id=1, source_target_pairs={{0,16},{1,17},{2,18},{3,19},{4,20},{5,21},{6,22},{7,23},{8,24},{9,... | collective-permute-start | bytes 36872 | tf_op jit(solution)/shard_map/ppermute | solution.py:261
  125.6 10.3 %all-to-all-start = ((f32[32,1,128]{2,1,0:T(1,128)}), f32[32,1,128]{2,1,0:T(1,128)S(1)}, u32[]{:S(2)}, u32[]{:S(2)}) async-start(f32[32,1,128]{2,1,0:T(1,128)} %bitcast.3), calls=%async_computation | async-start | bytes 32768 | tf_op jit(solution)/shard_map/all_to_all | solution.py:428
  (5 other events, 3.8 us)

commit v3 on v2

--- a/solution.py
+++ b/solution.py
@@ -11,28 +11,38 @@
 BLOCK = 128
 VMEM = 56 * 1024 * 1024
 EARLY = 20_000_000_000
-
-
-def add_products(parts, pieces, here, there, total, rows, devices=0):
-    depth = 2 * rows
+LITTLE = 1_000_000_000
+STACK_VMEM = 1024 * 1024
+
+
+def add_products(parts, pieces, factors, total, rows, devices=0, token=None):
     share = parts[0].shape[-1]
-    hidden_share = here.shape[1]
+    hidden_share = factors[0].shape[1]
+    low = pieces[0][3]
+    high = pieces[-1][3] + pieces[-1][2]
+    last = () if token is None else (token,)
+    n_parts, n_factors = len(parts), len(factors)
 
     def kernel(*refs):
-        part_refs, (here_ref, there_ref, total_ref, out_ref) = refs[: len(parts)], refs[len(parts) : len(parts) + 4]
+        part_refs, factor_refs = refs[:n_parts], refs[n_parts : n_parts + n_factors]
+        total_ref, out_ref = refs[n_parts + n_factors], refs[n_parts + n_factors + 1 + len(last)]
         left, right = refs[-2:]
         for part, first, amount, spot in pieces:
-            left[spot : spot + amount, :] = part_refs[part][first : first + amount, :].astype(jnp.bfloat16)
-        for side, factor_ref in enumerate((here_ref, there_ref)):
+            left[spot - low : spot - low + amount, :] = part_refs[part][first : first + amount, :].astype(jnp.bfloat16)
+        for side, factor_ref in enumerate(factor_refs):
             marks = factor_ref[rows:, :].T
             for first in range(0, rows, hidden_share):
                 amount = min(hidden_share, rows - first)
                 line = first // hidden_share
-                mark = marks[:amount, line : line + 1]
-                weight = factor_ref[first : first + amount, :]
-                spot = side * rows + first
+                begin = max(first, low - side * rows)
+                end = min(first + amount, high - side * rows)
+                if begin >= end:
+                    continue
+                mark = marks[begin - first : end - first, line : line + 1]
+                weight = factor_ref[begin:end, :]
+                spot = side * rows + begin - low
                 for expert in range(EXPERTS):
-                    right[spot : spot + amount, expert * hidden_share : (expert + 1) * hidden_share] = jnp.where(
+                    right[spot : spot + end - begin, expert * hidden_share : (expert + 1) * hidden_share] = jnp.where(
                         mark == float(expert), weight, 0.0
                     ).astype(jnp.bfloat16)
         weights = right[...]
@@ -55,13 +65,15 @@
                 sums = jnp.where(lane == expert, jnp.sum(own, axis=1, keepdims=True), sums)
             refs[-3][...] = sums
 
+    depth = high - low
     out_shape = [jax.ShapeDtypeStruct(total.shape, jnp.float32)]
     if devices:
         out_shape.append(jax.ShapeDtypeStruct((devices, 128), jnp.float32))
     results = pl.pallas_call(
         kernel,
         out_shape=out_shape,
-        in_specs=[pl.BlockSpec(memory_space=pltpu.VMEM)] * (len(parts) + 3),
+        in_specs=[pl.BlockSpec(memory_space=pltpu.VMEM)] * (n_parts + n_factors + 1)
+        + [pl.BlockSpec(memory_space=pl.ANY)] * len(last),
         out_specs=[pl.BlockSpec(memory_space=pltpu.VMEM)] * len(out_shape),
         scratch_shapes=[
             pltpu.VMEM((depth, share), jnp.bfloat16),
@@ -73,7 +85,7 @@
             bytes_accessed=4 * depth * (share + hidden_share) + 8 * share * EXPERTS * hidden_share,
             transcendentals=0,
         ),
-    )(*parts, here, there, total)
+    )(*parts, *factors, total, *last)
     return results if devices else results[0]
 
 
@@ -107,6 +119,20 @@
     )(*arrays)
 
 
+def marker(values, flops):
+    def kernel(*refs):
+        refs[-1][...] = jnp.zeros_like(refs[-1])
+
+    return pl.pallas_call(
+        kernel,
+        out_shape=jax.ShapeDtypeStruct((8, 128), jnp.float32),
+        in_specs=[pl.BlockSpec(memory_space=pl.ANY)] * len(values),
+        out_specs=pl.BlockSpec(memory_space=pltpu.VMEM),
+        compiler_params=pltpu.CompilerParams(vmem_limit_bytes=1024 * 1024),
+        cost_estimate=pl.CostEstimate(flops=flops, bytes_accessed=8192, transcendentals=0),
+    )(*values)
+
+
 def project(upstream, weights):
     rows, width = upstream.shape
     hidden_share = weights.shape[2]
@@ -132,7 +158,7 @@
             pl.BlockSpec((EXPERTS, block, hidden_share), lambda i: (0, i, 0)),
         ],
         out_specs=pl.BlockSpec((EXPERTS, rows, hidden_share), lambda i: (0, 0, 0)),
-        compiler_params=pltpu.CompilerParams(vmem_limit_bytes=VMEM),
+        compiler_params=pltpu.CompilerParams(vmem_limit_bytes=16 * 1024 * 1024),
         cost_estimate=pl.CostEstimate(
             flops=2 * rows * width * EXPERTS * hidden_share,
             bytes_accessed=2 * width * (rows + EXPERTS * hidden_share),
@@ -228,7 +254,7 @@
         ],
         in_specs=[smem] + [vmem] * 5,
         out_specs=[vmem] * 3,
-        compiler_params=pltpu.CompilerParams(vmem_limit_bytes=VMEM),
+        compiler_params=pltpu.CompilerParams(vmem_limit_bytes=16 * 1024 * 1024),
         cost_estimate=pl.CostEstimate(flops=6 * rows * rows * hidden_share, bytes_accessed=20 * rows * hidden_share, transcendentals=0),
     )(block_expert, both, gate_pre, up_pre, gate_prob, row_token)
 
@@ -287,9 +313,11 @@
 
     near_0 = sent((1, 0), piece_for((1, 0), blk_index))
     skip_0 = sent((2, 0), piece_for((2, 0), blk_index))
-    (spread,) = stack_rows([[(near_0, 0, quarter), (skip_0, 0, quarter)]], EARLY)
-
+    piece_11 = piece_for((1, 1), blk_index)
     factor = factor_of_tokens(gate_pre, up_pre, gate_prob, row_token, block_expert, blk_index, columns)
+    factor_near = outer_swap(factor)
+    mid_own = middle_swap(factor)
+    other_factor = across(factor)
 
     def own_columns(of_core, index):
         first_column = share * (2 * chip + of_core)
@@ -299,129 +327,149 @@
         ]
         return jnp.concatenate(parts, axis=0).astype(jnp.float32)
 
-    factor_near = outer_swap(factor)
-    mid_own = middle_swap(factor)
-    down_weight, _ = together(down_weight, factor)
-    spread, index = together(spread, blk_index)
+    down_weight, index, _ = together(down_weight, blk_index, factor)
     weights = jnp.transpose(down_weight, (1, 0, 2))
-    pieces = [piece_for(key, index) for key in ((1, 1), (2, 1), (3, 0), (3, 1))]
+
+    token = block_expert
+
+    def arrive(*values, marked=(), flops=0):
+        nonlocal token
+        if marked:
+            token = marker(marked + (token,), flops)
+        *values, token = together(*values, token)
+        return values
+
+    half = quarter // 2
+
+    near_0, skip_0, index, weights, piece_11 = arrive(near_0, skip_0, index, weights, piece_11)
+    near_1 = sent((1, 1), piece_11)
+    (spread,) = stack_rows([[(near_0, 0, quarter), (skip_0, 0, quarter)]], EARLY)
+    x_0, y_0 = along_x(spread), along_y(spread)
+    piece_21, piece_30, piece_31 = [piece_for(key, index) for key in ((2, 1), (3, 0), (3, 1))]
     own_tokens, other_tokens = own_columns(core, index), own_columns(1 - core, index)
-    other_factor = across(factor)
-
-    spread, factor_near, mid_own, other_factor, weights, pieces, other_tokens = together(
-        spread, factor_near, mid_own, other_factor, weights, pieces, other_tokens
-    )
-    piece_11, piece_21, piece_30, piece_31 = pieces
-    near_1 = sent((1, 1), piece_11)
+
+    factor_near, mid_own, piece_21, piece_30, piece_31, other_tokens, other_factor = arrive(
+        factor_near, mid_own, piece_21, piece_30, piece_31, other_tokens, other_factor,
+        marked=(factor_near, mid_own, spread), flops=EARLY,
+    )
     skip_1 = sent((2, 1), piece_21)
-    x_0, y_0 = along_x(spread), along_y(spread)
-    (pair,) = stack_rows([[(near_1, 0, quarter), (skip_1, 0, quarter)]], EARLY)
-    both = project(upstream, weights)
-    other_tokens = across(other_tokens)
-
-    (
-        pair, x_0, y_0, both, factor_near, mid_own, other_tokens, piece_30, piece_31, gate_pre
-    ) = together(
-        pair, x_0, y_0, both, factor_near, mid_own, other_tokens, piece_30, piece_31, gate_pre
-    )
-    far_0 = sent((3, 0), piece_30)
-    (far_0,) = stack_rows([[(far_0, 0, quarter)]], EARLY)
-    mid_near = middle_swap(factor_near)
+
+    x_0, y_0, near_1, mid_own = arrive(x_0, y_0, near_1, mid_own)
     to_x, to_y = stack_rows(
         [
-            [(pair, 0, 2 * quarter), (y_0, quarter, quarter)],
-            [(pair, 0, 2 * quarter), (x_0, 0, quarter)],
-        ]
+            [(near_1, 0, quarter), (y_0, quarter, quarter)],
+            [(near_1, 0, quarter), (x_0, 0, quarter)],
+        ],
+        EARLY,
     )
     x_1, y_1 = along_x(to_x), along_y(to_y)
     out_own = outer_swap(mid_own)
 
-    up_grad, gate_grad, partial_value = row_gradients(both, gate_pre, up_pre, gate_prob, row_token, block_expert)
-
-    far_0, mid_near, x_1, y_1, out_own, partial_value, up_grad, gate_grad, piece_31, factor_near = together(
-        far_0, mid_near, x_1, y_1, out_own, partial_value, up_grad, gate_grad, piece_31, factor_near
-    )
-    far_1 = sent((3, 1), piece_31)
-    (far_1,) = stack_rows([[(far_1, 0, quarter)]], EARLY)
+    skip_1, piece_30 = arrive(skip_1, piece_30, marked=(skip_1, to_x), flops=EARLY)
+    far_0 = sent((3, 0), piece_30)
+
+    x_1, y_1, other_tokens = arrive(x_1, y_1, other_tokens)
     to_x, to_y = stack_rows(
         [
-            [(far_0, 0, quarter), (y_1, quarter, quarter)],
-            [(far_0, 0, quarter), (x_1, 0, quarter)],
-        ]
+            [(skip_1, 0, quarter), (y_1, half, half)],
+            [(skip_1, 0, quarter), (x_1, 0, half)],
+        ],
+        EARLY,
     )
     x_2, y_2 = along_x(to_x), along_y(to_y)
+    other_tokens = across(other_tokens)
+
+    far_0, piece_31, weights = arrive(far_0, piece_31, weights, marked=(far_0, to_x), flops=EARLY)
+    far_1 = sent((3, 1), piece_31)
+    both = project(upstream, weights)
+
+    x_2, y_2, factor_near, both, out_own, gate_pre = arrive(x_2, y_2, factor_near, both, out_own, gate_pre)
+    to_x, to_y = stack_rows(
+        [
+            [(far_0, 0, quarter), (y_2, half, half)],
+            [(far_0, 0, quarter), (x_2, 0, half)],
+        ],
+        EARLY,
+    )
+    x_3, y_3 = along_x(to_x), along_y(to_y)
+    near_factor = across(factor_near)
+    up_grad, gate_grad, partial_value = row_gradients(both, gate_pre, up_pre, gate_prob, row_token, block_expert)
+
+    far_1, factor_near, partial_value, up_grad, gate_grad = arrive(
+        far_1, factor_near, partial_value, up_grad, gate_grad, marked=(far_1, to_x), flops=EARLY
+    )
+    mid_near = middle_swap(factor_near)
+
+    x_3, y_3, near_factor, partial_value, other_tokens = arrive(x_3, y_3, near_factor, partial_value, other_tokens)
+    to_x, to_y = stack_rows(
+        [
+            [(far_1, 0, quarter), (y_3, half, half)],
+            [(far_1, 0, quarter), (x_3, 0, half)],
+        ],
+        EARLY,
+    )
+    x_4, y_4 = along_x(to_x), along_y(to_y)
+    partial_value = partial_value + along_x(partial_value)
+
+    mid_near, mid_own, out_own = arrive(mid_near, mid_own, out_own, marked=(mid_near, to_x), flops=EARLY)
     out_near = outer_swap(mid_near)
     outer = (chip == 0) | (chip == chips - 1)
     factor_skip = jnp.where(outer, out_own, mid_near)
-    near_factor = across(factor_near)
-
-    far_1, x_2, y_2, out_near, near_factor, partial_value, factor_skip = together(
-        far_1, x_2, y_2, out_near, near_factor, partial_value, factor_skip
-    )
-    to_x, to_y = stack_rows(
-        [
-            [(far_1, 0, quarter), (y_2, quarter // 2, quarter // 2)],
-            [(far_1, 0, quarter), (x_2, 0, quarter // 2)],
-        ]
-    )
-    x_3, y_3 = along_x(to_x), along_y(to_y)
-    factor_far = jnp.where(outer, out_near, mid_own)
     skip_factor = across(factor_skip)
-    far_factor = across(factor_far)
-    partial_value = partial_value + along_x(partial_value)
+
+    def hopped(own, x_hop, y_hop, row, diagonal):
+        parts = [own, x_hop, y_hop] + [hop for hop, _, _ in diagonal]
+        pieces = [(0, 0, quarter, 0), (1, row, quarter, quarter), (2, row, quarter, 2 * quarter)]
+        spot = 3 * quarter
+        for index, (_, first, amount) in enumerate(diagonal):
+            pieces.append((3 + index, first, amount, spot))
+            spot += amount
+        return parts, pieces
+
+    def both_sides(one, two):
+        shift = len(one[0])
+        pieces = one[1] + [(part + shift, first, amount, spot + rows) for part, first, amount, spot in two[1]]
+        return tuple(one[0] + two[0]), tuple(pieces)
 
     total = add_products(
         (own_tokens, other_tokens),
         ((0, 0, rows, 0), (1, 0, rows, rows)),
-        factor,
-        other_factor,
+        (factor, other_factor),
         jnp.zeros((share, EXPERTS * hidden_share), jnp.float32),
         rows,
     )
-
-    def gathered(pairs, near, far, running, devices=0):
-        parts, pieces = [], []
-        for side, (own, x_hop, y_hop, row, diagonal) in enumerate(pairs):
-            spot = side * rows
-            base = len(parts)
-            parts += [own, x_hop, y_hop] + [hop for hop, _, _ in diagonal]
-            pieces += [
-                (base, 0, quarter, spot),
-                (base + 1, row, quarter, spot + quarter),
-                (base + 2, row, quarter, spot + 2 * quarter),
-            ]
-            spot += 3 * quarter
-            for index, (_, first, amount) in enumerate(diagonal):
-                pieces.append((base + 3 + index, first, amount, spot))
-                spot += amount
-        return add_products(tuple(parts), tuple(pieces), near, far, running, rows, devices)
-
-    half = quarter // 2
-    total = gathered(
-        (
-            (near_0, x_0, y_0, 0, ((y_1, 2 * quarter, quarter),)),
-            (near_1, x_1, y_1, 0, ((y_2, quarter, quarter),)),
+    total = add_products(
+        *both_sides(
+            hopped(near_0, x_0, y_0, 0, ((y_1, quarter, quarter),)),
+            hopped(near_1, x_1, y_1, 0, ((y_2, quarter, half), (x_2, quarter, half))),
         ),
-        factor_near, near_factor, total,
-    )
-    total = gathered(
-        (
-            (skip_0, x_0, y_0, quarter, ((x_1, 2 * quarter, quarter),)),
-            (skip_1, x_1, y_1, quarter, ((x_2, quarter, quarter),)),
+        (factor_near, near_factor), total, rows,
+    )
+    total = add_products(
+        *both_sides(
+            hopped(skip_0, x_0, y_0, quarter, ((x_1, quarter, quarter),)),
+            hopped(skip_1, x_2, y_2, 0, ((y_3, quarter, half), (x_3, quarter, half))),
         ),
-        factor_skip, skip_factor, total,
-    )
-
-    x_3, y_3, total, partial_value, far_factor = together(x_3, y_3, total, partial_value, far_factor)
+        (factor_skip, skip_factor), total, rows,
+    )
+
+    x_4, y_4, partial_value = arrive(x_4, y_4, partial_value)
+    to_x, to_y = stack_rows([[(y_4, half, half)], [(x_4, 0, half)]], LITTLE)
+    x_5, y_5 = along_x(to_x), along_y(to_y)
     prob_grad = (partial_value + along_y(partial_value))[0]
-    x_4, y_4 = along_x(y_3[half:quarter]), along_y(x_3[:half])
+    factor_far = jnp.where(outer, out_near, mid_own)
+    far_factor = across(factor_far)
+    parts, pieces = both_sides(
+        hopped(far_0, x_3, y_3, 0, ((y_4, quarter, half), (x_4, quarter, half))),
+        hopped(far_1, x_4, y_4, 0, ()),
+    )
+    total = add_products(parts, pieces, (factor_far, far_factor), total, rows)
+    x_5, y_5 = arrive(x_5, y_5, marked=(x_5, y_5), flops=EARLY)
     devices = columns * wide
-    total, sums = gathered(
-        (
-            (far_0, x_2, y_2, 0, ((y_3, quarter, half), (x_3, quarter, half))),
-            (far_1, x_3, y_3, 0, ((y_4, 0, half), (x_4, 0, half))),
-        ),
-        factor_far, far_factor, total, devices,
+    total, sums = add_products(
+        (y_5, x_5),
+        ((0, 0, half, 3 * quarter), (1, 0, half, 3 * quarter + half)),
+        (far_factor,), total, rows, devices, token,
     )
 
     down_grad = total.reshape(share, EXPERTS, hidden_share)

time: 137 us -> 126 us (0.920)
  waiting for transfers between devices: 59.9 us -> 49.2 us
  starting transfers between devices: 31.2 us -> 39.2 us
  Pallas kernels: 22.5 us -> 16.4 us
    ppermute x28 -> x30, waiting for transfers between devices: 55.7 us -> 45 us  [moved(): return lax.ppermute(value, ('blk', 'wide'), pairs)]
    ppermute x28 -> x30, starting transfers between devices: 28 us -> 34.3 us  [moved(): return lax.ppermute(value, ('blk', 'wide'), pairs)]
    pallas_call x1, Pallas kernels: 9.29 us -> 5.03 us  [project(): pl.pallas_call(kernel, out_shape=jax.ShapeDtypeStruct((EXPERTS, rows, hid...]
    pallas_call x7 -> x6, Pallas kernels: 2.38 us -> 0.36 us  [stack_rows(): pl.pallas_call(kernel, out_shape=[jax.ShapeDtypeStruct((height, share), j...]
    all_to_all x1, starting transfers between devices: 3.15 us -> 4.93 us  [factors_body(): spread = lax.all_to_all(sums, ('blk', 'wide'), 0, 0, tiled=True)]
    unnamed x48 -> x34, local copies, waits for them, and re-layouts: 6.05 us -> 4.94 us
    pallas_call x4 -> x5, Pallas kernels: 5.68 us -> 6.62 us  [add_products(): pl.pallas_call(kernel, out_shape=out_shape, in_specs=[pl.BlockSpec(memory...]
  transfers between devices with their start and end apart: 29 -> 31, of which waited for: 15 -> 13; matrix products, arithmetic and copies ran while one was open for 10% -> 10% of each run, Pallas kernels for 17% -> 13%
where the time goes in v3:
time: 126 us; the launch traced here: 125 us
  waiting for transfers between devices  49.2 us (39%)
  starting transfers between devices  39.2 us (31%)
  Pallas kernels  16.4 us (13%)
  local copies, waits for them, and re-layouts  14.4 us (11%)
  other arithmetic  5.12 us (4%)
    ppermute x30, waiting for transfers between devices, moved(): return lax.ppermute(value, ('blk', 'wide'), pairs)  45 us
    ppermute x30, starting transfers between devices, moved(): return lax.ppermute(value, ('blk', 'wide'), pairs)  34.3 us
    optimization_barrier x1, local copies, waits for them, and re-layouts, together(): return lax.optimization_barrier(values)  6.92 us
    pallas_call x5, Pallas kernels, add_products(): pl.pallas_call(kernel, out_shape=out_shape, in_specs=[pl.BlockSpec(memory...  6.62 us
    pallas_call x1, Pallas kernels, project(): pl.pallas_call(kernel, out_shape=jax.ShapeDtypeStruct((EXPERTS, rows, hid...  5.03 us
    unnamed x34, local copies, waits for them, and re-layouts  4.94 us
    all_to_all x1, starting transfers between devices, factors_body(): spread = lax.all_to_all(sums, ('blk', 'wide'), 0, 0, tiled=True)  4.93 us
    all_to_all x1, waiting for transfers between devices, factors_body(): spread = lax.all_to_all(sums, ('blk', 'wide'), 0, 0, tiled=True)  4.17 us
  transfers between devices with their start and end apart: 31, of which 13 were waited for; matrix products, arithmetic and copies ran while one was open for 10% of the time, Pallas kernels for 13%

profile of v3, /device:TPU:0, one launch (start us, length us, event | category | flops | bytes accessed | tf_op | source)
XLA Modules:
  0.0 125.4 jit_solution(7392741897108234297)
XLA Ops:
  0.7 1.9 %dynamic-slice_convert_fusion.3 = (f32[96,896]{1,0:T(8,128)}, f32[96,896]{1,0:T(8,128)S(1)}, f32[96,896]{1,0:T(8,128)S(1)}) fusion(bf16[384,7168]{1,0:T(8,128)(2,1)} %upstream_ref.1, s32[]{:T(128)S(6)} %select_n.77, s32[]{:T(128)S(6)} %select_n.82, s32[]{:T(128)S(6)} %select_n.81, s32[]{:T(128)S(6)} %select_n.80), kind=kLoop, calls=%fused_computation.8 | loop fusion | flops 258048 | bytes 1548304 | tf_op jit(solution)/shard_map/convert_element_type | solution.py:308
  2.6 3.0 %collective-permute-start.2 = (f32[96,896]{1,0:T(8,128)S(1)}, f32[96,896]{1,0:T(8,128)S(1)}, u32[]{:S(2)}, u32[]{:S(2)}) collective-permute-start(f32[96,896]{1,0:T(8,128)S(1)} %get-tuple-element.172), channel_id=1, source_target_pairs={{0,2},{1,3},{2,0},{3,1},{4,6},{5,7},{6,4},{7,5},{8,10},{9,11},{10,... | collective-permute-start | bytes 1032200 | tf_op jit(solution)/shard_map/ppermute | solution.py:287
  5.6 2.6 %collective-permute-start.3 = (f32[96,896]{1,0:T(8,128)S(1)}, f32[96,896]{1,0:T(8,128)S(1)}, u32[]{:S(2)}, u32[]{:S(2)}) collective-permute-start(f32[96,896]{1,0:T(8,128)S(1)} %get-tuple-element.171), channel_id=1, source_target_pairs={{0,4},{1,5},{2,6},{3,7},{4,0},{5,1},{6,2},{7,3},{8,12},{9,13},{10,... | collective-permute-start | bytes 1032200 | tf_op jit(solution)/shard_map/ppermute | solution.py:287
  8.2 2.3 %shard_map.110.refs_2_ = f32[392,256]{1,0:T(8,128)} custom-call(s32[3]{0:T(128)} %expert_ref.3, s32[1]{0:T(128)} %bitcast.index_ref, bf16[384,256]{1,0:T(8,128)(2,1)} %gate_ref.2, bf16[384,256]{1,0:T(8,128)(2,1)} %up_ref.3, f32[384]{0:T(512)} %prob_ref.3, s32[384]{0:T(512)} %token_ref.3), custom_call_target="tpu_custom_call" | custom-call | flops 75497472 | bytes 1179648 | tf_op jit(solution)/shard_map/pallas_call | solution.py:206
  11.5 6.9 %copy.16 = bf16[7168,2,256]{2,0,1:T(8,128)(2,1)} copy(bf16[7168,2,256]{2,1,0:T(2,128)(2,1)} %param.10) | data formatting | bytes 14680064 | tf_op jit(solution)/shard_map/optimization_barrier | solution.py:263
  18.4 2.7 %collective-permute-done.2.refs_0_ = f32[96,896]{1,0:T(8,128)S(1)} collective-permute-done((f32[96,896]{1,0:T(8,128)S(1)}, f32[96,896]{1,0:T(8,128)S(1)}, u32[]{:S(2)}, u32[]{:S(2)}) %collective-permute-start.2) | collective-permute-done | bytes 344096 | tf_op jit(solution)/shard_map/ppermute | solution.py:287
  21.1 3.8 %collective-permute-done.3.refs_1_.refs_0_ = f32[96,896]{1,0:T(8,128)S(1)} collective-permute-done((f32[96,896]{1,0:T(8,128)S(1)}, f32[96,896]{1,0:T(8,128)S(1)}, u32[]{:S(2)}, u32[]{:S(2)}) %collective-permute-start.3) | collective-permute-done | bytes 344096 | tf_op jit(solution)/shard_map/ppermute | solution.py:287
  24.9 0.8 copy-done.3
  25.7 0.8 copy-done.5
  26.5 1.5 %collective-permute-start.6 = (f32[192,896]{1,0:T(8,128)S(1)}, f32[192,896]{1,0:T(8,128)S(1)}, u32[]{:S(2)}, u32[]{:S(2)}) collective-permute-start(f32[192,896]{1,0:T(8,128)S(1)} %shard_map.111.refs_2_), channel_id=1, source_target_pairs={{0,8},{1,9},{2,10},{3,11},{4,12},{5,13},{6,14},{7,15},{8,0},{9,1},... | collective-permute-start | bytes 2064392 | tf_op jit(solution)/shard_map/ppermute | solution.py:287
  28.0 1.5 %collective-permute-start.7 = (f32[192,896]{1,0:T(8,128)S(1)}, f32[192,896]{1,0:T(8,128)S(1)}, u32[]{:S(2)}, u32[]{:S(2)}) collective-permute-start(f32[192,896]{1,0:T(8,128)S(1)} %shard_map.111.refs_2_), channel_id=1, source_target_pairs={{0,16},{1,17},{2,18},{3,19},{4,20},{5,21},{6,22},{7,23},{8,24},{9,... | collective-permute-start | bytes 2064392 | tf_op jit(solution)/shard_map/ppermute | solution.py:287
  29.5 1.7 %fusion.1 = (bf16[96,896]{1,0:T(8,128)(2,1)S(1)}, bf16[96,896]{1,0:T(8,128)(2,1)S(1)}, bf16[96,896]{1,0:T(8,128)(2,1)S(1)}, bf16[96,896]{1,0:T(8,128)(2,1)S(1)},...) fusion(bf16[384,7168]{1,0:T(8,128)(2,1)} %upstream_ref.1, ...), kind=kLoop, calls=%fused_computation.14 | loop fusion | flops 258048 | bytes 4300836 | tf_op jit(solution)/shard_map/dynamic_slice | solution.py:325
  31.5 0.8 copy-done.12
  32.3 2.8 %collective-permute-start.5 = (f32[96,896]{1,0:T(8,128)S(1)}, f32[96,896]{1,0:T(8,128)S(1)}, u32[]{:S(2)}, u32[]{:S(2)}) collective-permute-start(f32[96,896]{1,0:T(8,128)S(1)} %get-tuple-element.88), channel_id=1, source_target_pairs={{0,5},{1,4},{2,7},{3,6},{4,1},{5,0},{6,3},{7,2},{8,13},{9,12},{10,... | collective-permute-start | bytes 1032200 | tf_op jit(solution)/shard_map/ppermute | solution.py:287
  35.1 12.1 %collective-permute-done.8.refs_0_.refs_4_ = f32[96,896]{1,0:T(8,128)S(1)} collective-permute-done((f32[96,896]{1,0:T(8,128)S(1)}, f32[96,896]{1,0:T(8,128)S(1)}, u32[]{:S(2)}, u32[]{:S(2)}) %collective-permute-start.8) | collective-permute-done | bytes 344096 | tf_op jit(solution)/shard_map/ppermute | solution.py:287
  47.4 0.6 copy-done.7
  48.0 1.5 %collective-permute-start.10 = (f32[192,896]{1,0:T(8,128)S(1)}, f32[192,896]{1,0:T(8,128)S(1)}, u32[]{:S(2)}, u32[]{:S(2)}) collective-permute-start(f32[192,896]{1,0:T(8,128)S(1)} %get-tuple-element.96.refs_1_), channel_id=1, source_target_pairs={{0,8},{1,9},{2,10},{3,11},{4,12},{5,13},{6,14},{7,15},{8,0},{9,1},... | collective-permute-start | bytes 2064392 | tf_op jit(solution)/shard_map/ppermute | solution.py:287
  49.5 1.9 %collective-permute-start.11 = (f32[192,896]{1,0:T(8,128)S(1)}, f32[192,896]{1,0:T(8,128)S(1)}, u32[]{:S(2)}, u32[]{:S(2)}) collective-permute-start(f32[192,896]{1,0:T(8,128)S(1)} %get-tuple-element.102), channel_id=1, source_target_pairs={{0,16},{1,17},{2,18},{3,19},{4,20},{5,21},{6,22},{7,23},{8,24},{9,... | collective-permute-start | bytes 2064392 | tf_op jit(solution)/shard_map/ppermute | solution.py:287
  51.4 1.6 %collective-permute-start.9 = (f32[96,896]{1,0:T(8,128)S(1)}, f32[96,896]{1,0:T(8,128)S(1)}, u32[]{:S(2)}, u32[]{:S(2)}) collective-permute-start(f32[96,896]{1,0:T(8,128)S(1)} %get-tuple-element.98), channel_id=1, source_target_pairs={{0,6},{1,7},{2,4},{3,5},{4,2},{5,3},{6,0},{7,1},{8,14},{9,15},{10,... | collective-permute-start | bytes 1032200 | tf_op jit(solution)/shard_map/ppermute | solution.py:287
  53.0 11.1 %collective-permute-done.10.refs_2_.refs_5_.refs_3_ = f32[192,896]{1,0:T(8,128)S(1)} collective-permute-done((f32[192,896]{1,0:T(8,128)S(1)}, f32[192,896]{1,0:T(8,128)S(1)}, u32[]{:S(2)}, u32[]{:S(2)}) %collective-permute-start.10) | collective-permute-done | bytes 688160 | tf_op jit(solution)/shard_map/ppermute | solution.py:287
  64.1 2.5 %collective-permute-done.11.refs_1_.refs_3_.refs_6_ = f32[192,896]{1,0:T(8,128)S(1)} collective-permute-done((f32[192,896]{1,0:T(8,128)S(1)}, f32[192,896]{1,0:T(8,128)S(1)}, u32[]{:S(2)}, u32[]{:S(2)}) %collective-permute-start.11) | collective-permute-done | bytes 688160 | tf_op jit(solution)/shard_map/ppermute | solution.py:287
  67.0 1.7 %collective-permute-start.14 = (f32[144,896]{1,0:T(8,128)S(1)}, f32[144,896]{1,0:T(8,128)S(1)}, u32[]{:S(2)}, u32[]{:S(2)}) collective-permute-start(f32[144,896]{1,0:T(8,128)S(1)} %get-tuple-element.110), channel_id=1, source_target_pairs={{0,16},{1,17},{2,18},{3,19},{4,20},{5,21},{6,22},{7,23},{8,24},{9,... | collective-permute-start | bytes 1548296 | tf_op jit(solution)/shard_map/ppermute | solution.py:287
  68.8 0.6 collective-permute-start.19
  69.4 0.7 slice-done.2
  70.0 0.9 slice-done.1
  71.2 5.0 %shard_map.117.both_ref = f32[2,384,256]{2,1,0:T(8,128)S(1)} custom-call(bf16[384,7168]{1,0:T(8,128)(2,1)S(1)} %bitcast.11, bf16[2,7168,256]{2,1,0:T(8,128)(2,1)S(1)} %bitcast.9), custom_call_target="tpu_custom_call" | custom-call | flops 2818572288 | bytes 12845056 | tf_op jit(solution)/shard_map/pallas_call | solution.py:152
  76.3 2.9 %collective-permute-done.13.refs_2_.refs_8_.refs_5_ = f32[144,896]{1,0:T(8,128)S(1)} collective-permute-done((f32[144,896]{1,0:T(8,128)S(1)}, f32[144,896]{1,0:T(8,128)S(1)}, u32[]{:S(2)}, u32[]{:S(2)}) %collective-permute-start.13) | collective-permute-done | bytes 516128 | tf_op jit(solution)/shard_map/ppermute | solution.py:287
  79.4 1.6 %collective-permute-start.16 = (f32[144,896]{1,0:T(8,128)S(1)}, f32[144,896]{1,0:T(8,128)S(1)}, u32[]{:S(2)}, u32[]{:S(2)}) collective-permute-start(f32[144,896]{1,0:T(8,128)S(1)} %get-tuple-element.124.refs_1_), channel_id=1, source_target_pairs={{0,8},{1,9},{2,10},{3,11},{4,12},{5,13},{6,14},{7,15},{8,0},{9,1},... | collective-permute-start | bytes 1548296 | tf_op jit(solution)/shard_map/ppermute | solution.py:287
  81.1 1.6 %collective-permute-start.17 = (f32[144,896]{1,0:T(8,128)S(1)}, f32[144,896]{1,0:T(8,128)S(1)}, u32[]{:S(2)}, u32[]{:S(2)}) collective-permute-start(f32[144,896]{1,0:T(8,128)S(1)} %get-tuple-element.127), channel_id=1, source_target_pairs={{0,16},{1,17},{2,18},{3,19},{4,20},{5,21},{6,22},{7,23},{8,24},{9,... | collective-permute-start | bytes 1548296 | tf_op jit(solution)/shard_map/ppermute | solution.py:287
  82.8 2.1 %shard_map.118 = (bf16[384,256]{1,0:T(8,128)(2,1)}, bf16[384,256]{1,0:T(8,128)(2,1)}, f32[8,384]{1,0:T(8,128)S(1)}) custom-call(s32[3]{0:T(128)S(1)} %copy-done.11, f32[2,384,256]{2,1,0:T(8,128)S(1)} %shard_map.117.both_ref, bf16[384,256]{1,0:T(8,128)(2,1)S(1)} %copy-done.1, bf16[384,256]{1,0:T(8,128)(2,1)S(1)} %copy-done.2, f32[384]{0:T(512)S(1)} %copy-done.9, ...), custom_call_target="tpu_custom_call" | custom-call | flops 226492416 | bytes 1966080 | tf_op jit(solution)/shard_map/pallas_call | solution.py:248
  85.4 5.5 %collective-permute-done.16.refs_2_.refs_8_.refs_1_ = f32[144,896]{1,0:T(8,128)S(1)} collective-permute-done((f32[144,896]{1,0:T(8,128)S(1)}, f32[144,896]{1,0:T(8,128)S(1)}, u32[]{:S(2)}, u32[]{:S(2)}) %collective-permute-start.16) | collective-permute-done | bytes 516128 | tf_op jit(solution)/shard_map/ppermute | solution.py:287
  90.9 1.5 %collective-permute-done.17.refs_1_.refs_7_.refs_2_ = f32[144,896]{1,0:T(8,128)S(1)} collective-permute-done((f32[144,896]{1,0:T(8,128)S(1)}, f32[144,896]{1,0:T(8,128)S(1)}, u32[]{:S(2)}, u32[]{:S(2)}) %collective-permute-start.17) | collective-permute-done | bytes 516128 | tf_op jit(solution)/shard_map/ppermute | solution.py:287
  92.9 1.9 %collective-permute-start.21 = (f32[144,896]{1,0:T(8,128)S(1)}, f32[144,896]{1,0:T(8,128)S(1)}, u32[]{:S(2)}, u32[]{:S(2)}) collective-permute-start(f32[144,896]{1,0:T(8,128)S(1)} %get-tuple-element.134), channel_id=1, source_target_pairs={{0,16},{1,17},{2,18},{3,19},{4,20},{5,21},{6,22},{7,23},{8,24},{9,... | collective-permute-start | bytes 1548296 | tf_op jit(solution)/shard_map/ppermute | solution.py:287
  94.8 1.0 collective-permute-start.22
  95.8 4.1 %collective-permute-start.26 = (f32[392,256]{1,0:T(8,128)S(1)}, f32[392,256]{1,0:T(8,128)S(1)}, u32[]{:S(2)}, u32[]{:S(2)}) collective-permute-start(f32[392,256]{1,0:T(8,128)S(1)} %collective-permute-done.23.refs_0_), channel_id=1, source_target_pairs={{0,2},{1,3},{2,0},{3,1},{4,6},{5,7},{6,4},{7,5},{8,10},{9,11},{10,... | collective-permute-start | bytes 1204232 | tf_op jit(solution)/shard_map/ppermute | solution.py:287
  100.2 1.3 %shard_map.125.refs_11_ = f32[896,512]{1,0:T(8,128)S(1)} custom-call(f32[384,896]{1,0:T(8,128)S(1)} %maximum_convert_fusion.1.refs_0_, f32[384,896]{1,0:T(8,128)S(1)} %collective-permute-done.19.refs_1_, f32[392,256]{1,0:T(8,128)S(1)} %copy-done, f32[392,256]{1,0:T(8,128)S(1)} %collective-permute-done.4.refs_3_, f32[896,512]{1,0:T(8,128)S(1)} %broadcast_in_dim.3.refs_4_), custom_call_target="tpu_custom_call" | custom-call | flops 704643072 | bytes 7208960 | tf_op jit(solution)/shard_map/pallas_call | solution.py:72
  101.6 1.3 %shard_map.126.refs_11_ = f32[896,512]{1,0:T(8,128)S(1)} custom-call(f32[96,896]{1,0:T(8,128)S(1)} %copy-done.6, f32[192,896]{1,0:T(8,128)S(1)} %collective-permute-done.6.refs_2_.refs_1_, f32[192,896]{1,0:T(8,128)S(1)} %collective-permute-done.7.refs_1_.refs_2_, f32[192,896]{1,0:T(8,128)S(1)} %collective-permute-done.11.refs_1_.refs_3_.refs_6_, ...), custom_call_target="tpu_custom_call" | custom-call | flops 704643072 | bytes 7208960 | tf_op jit(solution)/shard_map/pallas_call | solution.py:72
  103.3 1.0 collective-permute-start.24
  104.2 1.4 %collective-permute-start.25 = (f32[48,896]{1,0:T(8,128)S(1)}, f32[48,896]{1,0:T(8,128)S(1)}, u32[]{:S(2)}, u32[]{:S(2)}) collective-permute-start(f32[48,896]{1,0:T(8,128)S(1)} %get-tuple-element.143), channel_id=1, source_target_pairs={{0,16},{1,17},{2,18},{3,19},{4,20},{5,21},{6,22},{7,23},{8,24},{9,... | collective-permute-start | bytes 516104 | tf_op jit(solution)/shard_map/ppermute | solution.py:287
  105.7 2.3 %collective-permute-done.26 = f32[392,256]{1,0:T(8,128)S(1)} collective-permute-done((f32[392,256]{1,0:T(8,128)S(1)}, f32[392,256]{1,0:T(8,128)S(1)}, u32[]{:S(2)}, u32[]{:S(2)}) %collective-permute-start.26) | collective-permute-done | bytes 401440 | tf_op jit(solution)/shard_map/ppermute | solution.py:287
  108.2 1.3 %shard_map.127.refs_10_ = f32[896,512]{1,0:T(8,128)S(1)} custom-call(f32[96,896]{1,0:T(8,128)S(1)} %copy-done.4, f32[192,896]{1,0:T(8,128)S(1)} %collective-permute-done.6.refs_2_.refs_1_, f32[192,896]{1,0:T(8,128)S(1)} %collective-permute-done.7.refs_1_.refs_2_, f32[192,896]{1,0:T(8,128)S(1)} %collective-permute-done.10.refs_2_.refs_5_.refs_3_, ...), custom_call_target="tpu_custom_call" | custom-call | flops 704643072 | bytes 7208960 | tf_op jit(solution)/shard_map/pallas_call | solution.py:72
  109.5 0.6 collective-permute-start.29
  110.1 1.4 %shard_map.128.refs_3_ = f32[896,512]{1,0:T(8,128)S(1)} custom-call(f32[96,896]{1,0:T(8,128)S(1)} %collective-permute-done.9.refs_0_, f32[144,896]{1,0:T(8,128)S(1)} %collective-permute-done.16.refs_2_.refs_8_.refs_1_, f32[144,896]{1,0:T(8,128)S(1)} %collective-permute-done.17.refs_1_.refs_7_.refs_2_, ...), custom_call_target="tpu_custom_call" | custom-call | flops 616562688 | bytes 6766592 | tf_op jit(solution)/shard_map/pallas_call | solution.py:72
  111.5 1.3 %shard_map.129 = (f32[896,512]{1,0:T(8,128)S(1)}, f32[32,128]{1,0:T(8,128)}) custom-call(f32[48,896]{1,0:T(8,128)S(1)} %collective-permute-done.25.refs_1_.refs_0_, f32[48,896]{1,0:T(8,128)S(1)} %collective-permute-done.24.refs_0_.refs_1_, f32[392,256]{1,0:T(8,128)S(1)} %collective-permute-done.27.refs_9_.refs_2_, f32[896,512]{1,0:T(8,128)S(1)} %shard_map.128.refs_3_, ...), custom_call_target="tpu_custom_call" | custom-call | flops 88080384 | bytes 4112384 | tf_op jit(solution)/shard_map/pallas_call | solution.py:72
  112.8 4.9 %all-to-all-start = ((f32[32,1,128]{2,1,0:T(1,128)}), f32[32,1,128]{2,1,0:T(1,128)S(1)}, u32[]{:S(2)}, u32[]{:S(2)}) async-start(f32[32,1,128]{2,1,0:T(1,128)} %bitcast.3), calls=%async_computation | async-start | bytes 32768 | tf_op jit(solution)/shard_map/all_to_all | solution.py:476
  117.7 0.6 fusion
  118.3 2.4 %reshape.19 = f32[896,2,256]{2,1,0:T(2,128)} reshape(f32[896,512]{1,0:T(8,128)S(1)} %get-tuple-element.154) | data formatting | bytes 3670016 | tf_op jit(solution)/shard_map/reshape | solution.py:475
  120.7 4.2 %all-to-all-done = f32[32,1,128]{2,1,0:T(1,128)S(1)} async-done(((f32[32,1,128]{2,1,0:T(1,128)}), f32[32,1,128]{2,1,0:T(1,128)S(1)}, u32[]{:S(2)}, u32[]{:S(2)}) %all-to-all-start) | async-done | bytes 16416 | tf_op jit(solution)/shard_map/all_to_all | solution.py:476
  (83 shorter events, 4.7 us)
Async XLA Ops:
  2.6 18.5 %collective-permute-start.2 = (f32[96,896]{1,0:T(8,128)S(1)}, f32[96,896]{1,0:T(8,128)S(1)}, u32[]{:S(2)}, u32[]{:S(2)}) collective-permute-start(f32[96,896]{1,0:T(8,128)S(1)} %get-tuple-element.172), channel_id=1, source_target_pairs={{0,2},{1,3},{2,0},{3,1},{4,6},{5,7},{6,4},{7,5},{8,10},{9,11},{10,... | collective-permute-start | bytes 1032200 | tf_op jit(solution)/shard_map/ppermute | solution.py:287
  5.6 19.3 %collective-permute-start.3 = (f32[96,896]{1,0:T(8,128)S(1)}, f32[96,896]{1,0:T(8,128)S(1)}, u32[]{:S(2)}, u32[]{:S(2)}) collective-permute-start(f32[96,896]{1,0:T(8,128)S(1)} %get-tuple-element.171), channel_id=1, source_target_pairs={{0,4},{1,5},{2,6},{3,7},{4,0},{5,1},{6,2},{7,3},{8,12},{9,13},{10,... | collective-permute-start | bytes 1032200 | tf_op jit(solution)/shard_map/ppermute | solution.py:287
  10.5 20.9 %collective-permute-start = (f32[392,256]{1,0:T(8,128)}, f32[392,256]{1,0:T(8,128)S(1)}, u32[]{:S(2)}, u32[]{:S(2)}) collective-permute-start(f32[392,256]{1,0:T(8,128)} %shard_map.110.refs_2_), channel_id=1, source_target_pairs={{0,2},{1,3},{2,0},{3,1},{4,6},{5,7},{6,4},{7,5},{8,10},{9,11},{10,... | collective-permute-start | bytes 1204232 | tf_op jit(solution)/shard_map/ppermute | solution.py:287
  11.0 21.4 %collective-permute-start.1 = (f32[392,256]{1,0:T(8,128)}, f32[392,256]{1,0:T(8,128)S(1)}, u32[]{:S(2)}, u32[]{:S(2)}) collective-permute-start(f32[392,256]{1,0:T(8,128)} %shard_map.110.refs_2_), channel_id=1, source_target_pairs={{0,1},{1,0},{2,4},{3,5},{4,2},{5,3},{6,7},{7,6},{8,9},{9,8},{10,12... | collective-permute-start | bytes 1204232 | tf_op jit(solution)/shard_map/ppermute | solution.py:287
  11.0 21.4 %collective-permute-start.4 = (f32[392,256]{1,0:T(8,128)}, f32[392,256]{1,0:T(8,128)S(1)}, u32[]{:S(2)}, u32[]{:S(2)}) collective-permute-start(f32[392,256]{1,0:T(8,128)} %shard_map.110.refs_2_), channel_id=1, source_target_pairs={{0,1},{1,0},{2,3},{3,2},{4,5},{5,4},{6,7},{7,6},{8,9},{9,8},{10,11... | collective-permute-start | bytes 1204232 | tf_op jit(solution)/shard_map/ppermute | solution.py:287
  24.9 0.8 copy-start.3
  25.7 0.8 copy-start.5
  26.5 20.8 %collective-permute-start.6 = (f32[192,896]{1,0:T(8,128)S(1)}, f32[192,896]{1,0:T(8,128)S(1)}, u32[]{:S(2)}, u32[]{:S(2)}) collective-permute-start(f32[192,896]{1,0:T(8,128)S(1)} %shard_map.111.refs_2_), channel_id=1, source_target_pairs={{0,8},{1,9},{2,10},{3,11},{4,12},{5,13},{6,14},{7,15},{8,0},{9,1},... | collective-permute-start | bytes 2064392 | tf_op jit(solution)/shard_map/ppermute | solution.py:287
  28.0 19.3 %collective-permute-start.7 = (f32[192,896]{1,0:T(8,128)S(1)}, f32[192,896]{1,0:T(8,128)S(1)}, u32[]{:S(2)}, u32[]{:S(2)}) collective-permute-start(f32[192,896]{1,0:T(8,128)S(1)} %shard_map.111.refs_2_), channel_id=1, source_target_pairs={{0,16},{1,17},{2,18},{3,19},{4,20},{5,21},{6,22},{7,23},{8,24},{9,... | collective-permute-start | bytes 2064392 | tf_op jit(solution)/shard_map/ppermute | solution.py:287
  31.3 1.0 copy-start.12
  31.3 1.0 copy-start.11
  32.3 14.9 %collective-permute-start.8 = (f32[96,896]{1,0:T(8,128)S(1)}, f32[96,896]{1,0:T(8,128)S(1)}, u32[]{:S(2)}, u32[]{:S(2)}) collective-permute-start(f32[96,896]{1,0:T(8,128)S(1)} %copy-done.12), channel_id=1, source_target_pairs={{0,3},{1,2},{2,1},{3,0},{4,7},{5,6},{6,5},{7,4},{8,11},{9,10},{10,... | collective-permute-start | bytes 1032200 | tf_op jit(solution)/shard_map/ppermute | solution.py:287
  32.3 19.0 %collective-permute-start.5 = (f32[96,896]{1,0:T(8,128)S(1)}, f32[96,896]{1,0:T(8,128)S(1)}, u32[]{:S(2)}, u32[]{:S(2)}) collective-permute-start(f32[96,896]{1,0:T(8,128)S(1)} %get-tuple-element.88), channel_id=1, source_target_pairs={{0,5},{1,4},{2,7},{3,6},{4,1},{5,0},{6,3},{7,2},{8,13},{9,12},{10,... | collective-permute-start | bytes 1032200 | tf_op jit(solution)/shard_map/ppermute | solution.py:287
  47.3 0.7 copy-start.7
  48.0 16.1 %collective-permute-start.10 = (f32[192,896]{1,0:T(8,128)S(1)}, f32[192,896]{1,0:T(8,128)S(1)}, u32[]{:S(2)}, u32[]{:S(2)}) collective-permute-start(f32[192,896]{1,0:T(8,128)S(1)} %get-tuple-element.96.refs_1_), channel_id=1, source_target_pairs={{0,8},{1,9},{2,10},{3,11},{4,12},{5,13},{6,14},{7,15},{8,0},{9,1},... | collective-permute-start | bytes 2064392 | tf_op jit(solution)/shard_map/ppermute | solution.py:287
  49.5 17.1 %collective-permute-start.11 = (f32[192,896]{1,0:T(8,128)S(1)}, f32[192,896]{1,0:T(8,128)S(1)}, u32[]{:S(2)}, u32[]{:S(2)}) collective-permute-start(f32[192,896]{1,0:T(8,128)S(1)} %get-tuple-element.102), channel_id=1, source_target_pairs={{0,16},{1,17},{2,18},{3,19},{4,20},{5,21},{6,22},{7,23},{8,24},{9,... | collective-permute-start | bytes 2064392 | tf_op jit(solution)/shard_map/ppermute | solution.py:287
  51.4 17.4 %collective-permute-start.9 = (f32[96,896]{1,0:T(8,128)S(1)}, f32[96,896]{1,0:T(8,128)S(1)}, u32[]{:S(2)}, u32[]{:S(2)}) collective-permute-start(f32[96,896]{1,0:T(8,128)S(1)} %get-tuple-element.98), channel_id=1, source_target_pairs={{0,6},{1,7},{2,4},{3,5},{4,2},{5,3},{6,0},{7,1},{8,14},{9,15},{10,... | collective-permute-start | bytes 1032200 | tf_op jit(solution)/shard_map/ppermute | solution.py:287
  53.0 23.3 %collective-permute-start.15 = (f32[392,256]{1,0:T(8,128)S(1)}, f32[392,256]{1,0:T(8,128)S(1)}, u32[]{:S(2)}, u32[]{:S(2)}) collective-permute-start(f32[392,256]{1,0:T(8,128)S(1)} %collective-permute-done.1.refs_1_), channel_id=1, source_target_pairs={{0,2},{1,3},{2,0},{3,1},{4,6},{5,7},{6,4},{7,5},{8,10},{9,11},{10,... | collective-permute-start | bytes 1204232 | tf_op jit(solution)/shard_map/ppermute | solution.py:287
  66.6 2.8 %slice-start = ((s8[7340032]{0:T(1024)(128)(4,1)}), s8[4194304]{0:T(1024)(128)(4,1)S(1)}, s32[]{:S(2)}) async-start(s8[7340032]{0:T(1024)(128)(4,1)} %bitcast.7), calls=%async_computation.1 | async-start | bytes 8388608
  66.6 3.5 %slice-start.2 = ((s8[5505024]{0:T(1024)(128)(4,1)}), s8[4194304]{0:T(1024)(128)(4,1)S(1)}, s32[]{:S(2)}) async-start(s8[5505024]{0:T(1024)(128)(4,1)} %bitcast.10), calls=%async_computation.3 | async-start | bytes 8388608
  66.6 4.3 %slice-start.1 = ((s8[7340032]{0:T(1024)(128)(4,1)}), s8[3145728]{0:T(1024)(128)(4,1)S(1)}, s32[]{:S(2)}) async-start(s8[7340032]{0:T(1024)(128)(4,1)} %bitcast.7), calls=%async_computation.2 | async-start | bytes 6291456
  66.6 4.6 %slice-start.3 = ((s8[5505024]{0:T(1024)(128)(4,1)}), s8[1310720]{0:T(1024)(128)(4,1)S(1)}, s32[]{:S(2)}) async-start(s8[5505024]{0:T(1024)(128)(4,1)} %bitcast.10), calls=%async_computation.4 | async-start | bytes 2621440
  66.7 12.6 %collective-permute-start.13 = (f32[144,896]{1,0:T(8,128)S(1)}, f32[144,896]{1,0:T(8,128)S(1)}, u32[]{:S(2)}, u32[]{:S(2)}) collective-permute-start(f32[144,896]{1,0:T(8,128)S(1)} %get-tuple-element.107.refs_1_), channel_id=1, source_target_pairs={{0,8},{1,9},{2,10},{3,11},{4,12},{5,13},{6,14},{7,15},{8,0},{9,1},... | collective-permute-start | bytes 1548296 | tf_op jit(solution)/shard_map/ppermute | solution.py:287
  67.0 12.4 %collective-permute-start.14 = (f32[144,896]{1,0:T(8,128)S(1)}, f32[144,896]{1,0:T(8,128)S(1)}, u32[]{:S(2)}, u32[]{:S(2)}) collective-permute-start(f32[144,896]{1,0:T(8,128)S(1)} %get-tuple-element.110), channel_id=1, source_target_pairs={{0,16},{1,17},{2,18},{3,19},{4,20},{5,21},{6,22},{7,23},{8,24},{9,... | collective-permute-start | bytes 1548296 | tf_op jit(solution)/shard_map/ppermute | solution.py:287
  68.8 14.0 %collective-permute-start.12 = (f32[96,896]{1,0:T(8,128)S(1)}, f32[96,896]{1,0:T(8,128)S(1)}, u32[]{:S(2)}, u32[]{:S(2)}) collective-permute-start(f32[96,896]{1,0:T(8,128)S(1)} %get-tuple-element.109), channel_id=1, source_target_pairs={{0,7},{1,6},{2,5},{3,4},{4,3},{5,2},{6,1},{7,0},{8,15},{9,14},{10,... | collective-permute-start | bytes 1032200 | tf_op jit(solution)/shard_map/ppermute | solution.py:287
  68.8 23.7 %collective-permute-start.19 = (f32[384,896]{1,0:T(8,128)S(1)}, f32[384,896]{1,0:T(8,128)S(1)}, u32[]{:S(2)}, u32[]{:S(2)}) collective-permute-start(f32[384,896]{1,0:T(8,128)S(1)} %maximum_convert_fusion), channel_id=1, source_target_pairs={{0,1},{1,0},{2,3},{3,2},{4,5},{5,4},{6,7},{7,6},{8,9},{9,8},{10,11... | collective-permute-start | bytes 4128776 | tf_op jit(solution)/shard_map/ppermute | solution.py:287
  79.4 11.5 %collective-permute-start.16 = (f32[144,896]{1,0:T(8,128)S(1)}, f32[144,896]{1,0:T(8,128)S(1)}, u32[]{:S(2)}, u32[]{:S(2)}) collective-permute-start(f32[144,896]{1,0:T(8,128)S(1)} %get-tuple-element.124.refs_1_), channel_id=1, source_target_pairs={{0,8},{1,9},{2,10},{3,11},{4,12},{5,13},{6,14},{7,15},{8,0},{9,1},... | collective-permute-start | bytes 1548296 | tf_op jit(solution)/shard_map/ppermute | solution.py:287
  81.1 1.7 %copy-start.1 = (bf16[384,256]{1,0:T(8,128)(2,1)S(1)}, bf16[384,256]{1,0:T(8,128)(2,1)}, u32[]{:S(2)}) copy-start(bf16[384,256]{1,0:T(8,128)(2,1)} %gate_ref.2) | copy-start | bytes 589828
  81.1 1.7 %copy-start.2 = (bf16[384,256]{1,0:T(8,128)(2,1)S(1)}, bf16[384,256]{1,0:T(8,128)(2,1)}, u32[]{:S(2)}) copy-start(bf16[384,256]{1,0:T(8,128)(2,1)} %up_ref.3) | copy-start | bytes 589828
  81.1 1.7 %copy-start.9 = (f32[384]{0:T(512)S(1)}, f32[384]{0:T(512)}, u32[]{:S(2)}) copy-start(f32[384]{0:T(512)} %prob_ref.3) | copy-start | bytes 4612
  81.1 1.7 %copy-start.10 = (s32[384]{0:T(512)S(1)}, s32[384]{0:T(512)}, u32[]{:S(2)}) copy-start(s32[384]{0:T(512)} %token_ref.3) | copy-start | bytes 4612
  81.1 11.3 %collective-permute-start.17 = (f32[144,896]{1,0:T(8,128)S(1)}, f32[144,896]{1,0:T(8,128)S(1)}, u32[]{:S(2)}, u32[]{:S(2)}) collective-permute-start(f32[144,896]{1,0:T(8,128)S(1)} %get-tuple-element.127), channel_id=1, source_target_pairs={{0,16},{1,17},{2,18},{3,19},{4,20},{5,21},{6,22},{7,23},{8,24},{9,... | collective-permute-start | bytes 1548296 | tf_op jit(solution)/shard_map/ppermute | solution.py:287
  82.7 2.7 %collective-permute-start.18 = (f32[392,256]{1,0:T(8,128)S(1)}, f32[392,256]{1,0:T(8,128)S(1)}, u32[]{:S(2)}, u32[]{:S(2)}) collective-permute-start(f32[392,256]{1,0:T(8,128)S(1)} %collective-permute-done.refs_0_.refs_9_), channel_id=1, source_target_pairs={{0,1},{1,0},{2,3},{3,2},{4,5},{5,4},{6,7},{7,6},{8,9},{9,8},{10,11... | collective-permute-start | bytes 1204232 | tf_op jit(solution)/shard_map/ppermute | solution.py:287
  84.9 9.9 %collective-permute-start.23 = (f32[392,256]{1,0:T(8,128)S(1)}, f32[392,256]{1,0:T(8,128)S(1)}, u32[]{:S(2)}, u32[]{:S(2)}) collective-permute-start(f32[392,256]{1,0:T(8,128)S(1)} %collective-permute-done.refs_0_.refs_9_), channel_id=1, source_target_pairs={{0,1},{1,0},{2,4},{3,5},{4,2},{5,3},{6,7},{7,6},{8,9},{9,8},{10,12... | collective-permute-start | bytes 1204232 | tf_op jit(solution)/shard_map/ppermute | solution.py:287
  92.5 10.4 %collective-permute-start.20 = (f32[144,896]{1,0:T(8,128)S(1)}, f32[144,896]{1,0:T(8,128)S(1)}, u32[]{:S(2)}, u32[]{:S(2)}) collective-permute-start(f32[144,896]{1,0:T(8,128)S(1)} %get-tuple-element.133.refs_1_), channel_id=1, source_target_pairs={{0,8},{1,9},{2,10},{3,11},{4,12},{5,13},{6,14},{7,15},{8,0},{9,1},... | collective-permute-start | bytes 1548296 | tf_op jit(solution)/shard_map/ppermute | solution.py:287
  92.9 10.3 %collective-permute-start.21 = (f32[144,896]{1,0:T(8,128)S(1)}, f32[144,896]{1,0:T(8,128)S(1)}, u32[]{:S(2)}, u32[]{:S(2)}) collective-permute-start(f32[144,896]{1,0:T(8,128)S(1)} %get-tuple-element.134), channel_id=1, source_target_pairs={{0,16},{1,17},{2,18},{3,19},{4,20},{5,21},{6,22},{7,23},{8,24},{9,... | collective-permute-start | bytes 1548296 | tf_op jit(solution)/shard_map/ppermute | solution.py:287
  94.8 5.4 %copy-start = (f32[392,256]{1,0:T(8,128)S(1)}, f32[392,256]{1,0:T(8,128)}, u32[]{:S(2)}) copy-start(f32[392,256]{1,0:T(8,128)} %shard_map.110.refs_2_) | copy-start | bytes 1204228
  94.8 8.1 %collective-permute-start.22 = (f32[8,384]{1,0:T(8,128)S(1)}, f32[8,384]{1,0:T(8,128)S(1)}, u32[]{:S(2)}, u32[]{:S(2)}) collective-permute-start(f32[8,384]{1,0:T(8,128)S(1)} %get-tuple-element.135), channel_id=1, source_target_pairs={{0,8},{1,9},{2,10},{3,11},{4,12},{5,13},{6,14},{7,15},{8,0},{9,1},... | collective-permute-start | bytes 36872 | tf_op jit(solution)/shard_map/ppermute | solution.py:287
  95.8 12.2 %collective-permute-start.26 = (f32[392,256]{1,0:T(8,128)S(1)}, f32[392,256]{1,0:T(8,128)S(1)}, u32[]{:S(2)}, u32[]{:S(2)}) collective-permute-start(f32[392,256]{1,0:T(8,128)S(1)} %collective-permute-done.23.refs_0_), channel_id=1, source_target_pairs={{0,2},{1,3},{2,0},{3,1},{4,6},{5,7},{6,4},{7,5},{8,10},{9,11},{10,... | collective-permute-start | bytes 1204232 | tf_op jit(solution)/shard_map/ppermute | solution.py:287
  99.9 8.2 %collective-permute-start.28 = (f32[392,256]{1,0:T(8,128)S(1)}, f32[392,256]{1,0:T(8,128)S(1)}, u32[]{:S(2)}, u32[]{:S(2)}) collective-permute-start(f32[392,256]{1,0:T(8,128)S(1)} %broadcast_select_fusion.refs_9_), channel_id=1, source_target_pairs={{0,1},{1,0},{2,3},{3,2},{4,5},{5,4},{6,7},{7,6},{8,9},{9,8},{10,11... | collective-permute-start | bytes 1204232 | tf_op jit(solution)/shard_map/ppermute | solution.py:287
  100.2 1.4 %copy-start.6 = (f32[96,896]{1,0:T(8,128)S(1)}, f32[96,896]{1,0:T(8,128)}, u32[]{:S(2)}) copy-start(f32[96,896]{1,0:T(8,128)} %copy-done.5) | copy-start | bytes 1032196
  100.2 1.4 %copy-start.8 = (f32[96,896]{1,0:T(8,128)S(1)}, f32[96,896]{1,0:T(8,128)}, u32[]{:S(2)}) copy-start(f32[96,896]{1,0:T(8,128)} %copy-done.7) | copy-start | bytes 1032196
  103.3 4.9 %copy-start.4 = (f32[96,896]{1,0:T(8,128)S(1)}, f32[96,896]{1,0:T(8,128)}, u32[]{:S(2)}) copy-start(f32[96,896]{1,0:T(8,128)} %copy-done.3) | copy-start | bytes 1032196
  103.3 6.8 %collective-permute-start.24 = (f32[48,896]{1,0:T(8,128)S(1)}, f32[48,896]{1,0:T(8,128)S(1)}, u32[]{:S(2)}, u32[]{:S(2)}) collective-permute-start(f32[48,896]{1,0:T(8,128)S(1)} %get-tuple-element.142), channel_id=1, source_target_pairs={{0,8},{1,9},{2,10},{3,11},{4,12},{5,13},{6,14},{7,15},{8,0},{9,1},... | collective-permute-start | bytes 516104 | tf_op jit(solution)/shard_map/ppermute | solution.py:287
  104.2 5.9 %collective-permute-start.25 = (f32[48,896]{1,0:T(8,128)S(1)}, f32[48,896]{1,0:T(8,128)S(1)}, u32[]{:S(2)}, u32[]{:S(2)}) collective-permute-start(f32[48,896]{1,0:T(8,128)S(1)} %get-tuple-element.143), channel_id=1, source_target_pairs={{0,16},{1,17},{2,18},{3,19},{4,20},{5,21},{6,22},{7,23},{8,24},{9,... | collective-permute-start | bytes 516104 | tf_op jit(solution)/shard_map/ppermute | solution.py:287
  108.1 2.1 %collective-permute-start.27 = (f32[392,256]{1,0:T(8,128)S(1)}, f32[392,256]{1,0:T(8,128)S(1)}, u32[]{:S(2)}, u32[]{:S(2)}) collective-permute-start(f32[392,256]{1,0:T(8,128)S(1)} %broadcast_select_fusion.1.refs_8_), channel_id=1, source_target_pairs={{0,1},{1,0},{2,3},{3,2},{4,5},{5,4},{6,7},{7,6},{8,9},{9,8},{10,11... | collective-permute-start | bytes 1204232 | tf_op jit(solution)/shard_map/ppermute | solution.py:287
  109.5 8.2 %collective-permute-start.29 = (f32[8,384]{1,0:T(8,128)S(1)}, f32[8,384]{1,0:T(8,128)S(1)}, u32[]{:S(2)}, u32[]{:S(2)}) collective-permute-start(f32[8,384]{1,0:T(8,128)S(1)} %add.109), channel_id=1, source_target_pairs={{0,16},{1,17},{2,18},{3,19},{4,20},{5,21},{6,22},{7,23},{8,24},{9,... | collective-permute-start | bytes 36872 | tf_op jit(solution)/shard_map/ppermute | solution.py:287
  112.8 12.1 %all-to-all-start = ((f32[32,1,128]{2,1,0:T(1,128)}), f32[32,1,128]{2,1,0:T(1,128)S(1)}, u32[]{:S(2)}, u32[]{:S(2)}) async-start(f32[32,1,128]{2,1,0:T(1,128)} %bitcast.3), calls=%async_computation | async-start | bytes 32768 | tf_op jit(solution)/shard_map/all_to_all | solution.py:476

commit v4 on v3

--- a/solution.py
+++ b/solution.py
@@ -313,9 +313,8 @@
 
     near_0 = sent((1, 0), piece_for((1, 0), blk_index))
     skip_0 = sent((2, 0), piece_for((2, 0), blk_index))
-    piece_11 = piece_for((1, 1), blk_index)
+    piece_11, piece_21 = piece_for((1, 1), blk_index), piece_for((2, 1), blk_index)
     factor = factor_of_tokens(gate_pre, up_pre, gate_prob, row_token, block_expert, blk_index, columns)
-    factor_near = outer_swap(factor)
     mid_own = middle_swap(factor)
     other_factor = across(factor)
 
@@ -330,12 +329,14 @@
     down_weight, index, _ = together(down_weight, blk_index, factor)
     weights = jnp.transpose(down_weight, (1, 0, 2))
 
-    token = block_expert
+    token = None
 
     def arrive(*values, marked=(), flops=0):
         nonlocal token
         if marked:
-            token = marker(marked + (token,), flops)
+            token = marker(marked + (() if token is None else (token,)), flops)
+        if token is None:
+            return together(*values) if len(values) > 1 else values
         *values, token = together(*values, token)
         return values
 
@@ -344,17 +345,19 @@
     near_0, skip_0, index, weights, piece_11 = arrive(near_0, skip_0, index, weights, piece_11)
     near_1 = sent((1, 1), piece_11)
     (spread,) = stack_rows([[(near_0, 0, quarter), (skip_0, 0, quarter)]], EARLY)
+    sent_0 = spread
     x_0, y_0 = along_x(spread), along_y(spread)
-    piece_21, piece_30, piece_31 = [piece_for(key, index) for key in ((2, 1), (3, 0), (3, 1))]
+
+    mid_own, factor, piece_21, other_factor, index = arrive(
+        mid_own, factor, piece_21, other_factor, index, marked=(mid_own, spread), flops=EARLY
+    )
+    piece_30, piece_31 = [piece_for(key, index) for key in ((3, 0), (3, 1))]
     own_tokens, other_tokens = own_columns(core, index), own_columns(1 - core, index)
-
-    factor_near, mid_own, piece_21, piece_30, piece_31, other_tokens, other_factor = arrive(
-        factor_near, mid_own, piece_21, piece_30, piece_31, other_tokens, other_factor,
-        marked=(factor_near, mid_own, spread), flops=EARLY,
-    )
     skip_1 = sent((2, 1), piece_21)
 
-    x_0, y_0, near_1, mid_own = arrive(x_0, y_0, near_1, mid_own)
+    x_0, y_0, near_1, piece_30, piece_31, other_tokens, own_tokens = arrive(
+        x_0, y_0, near_1, piece_30, piece_31, other_tokens, own_tokens
+    )
     to_x, to_y = stack_rows(
         [
             [(near_1, 0, quarter), (y_0, quarter, quarter)],
@@ -362,13 +365,17 @@
         ],
         EARLY,
     )
+    sent_1 = to_x
     x_1, y_1 = along_x(to_x), along_y(to_y)
-    out_own = outer_swap(mid_own)
-
-    skip_1, piece_30 = arrive(skip_1, piece_30, marked=(skip_1, to_x), flops=EARLY)
+
+    skip_1, piece_30, factor, weights = arrive(
+        skip_1, piece_30, factor, weights, marked=(skip_1, to_x), flops=EARLY
+    )
     far_0 = sent((3, 0), piece_30)
-
-    x_1, y_1, other_tokens = arrive(x_1, y_1, other_tokens)
+    both = project(upstream, weights)
+
+    x_1, y_1, other_tokens, both, factor = arrive(x_1, y_1, other_tokens, both, factor)
+    factor_near = outer_swap(factor)
     to_x, to_y = stack_rows(
         [
             [(skip_1, 0, quarter), (y_1, half, half)],
@@ -376,14 +383,15 @@
         ],
         EARLY,
     )
+    sent_2 = to_x
     x_2, y_2 = along_x(to_x), along_y(to_y)
     other_tokens = across(other_tokens)
 
-    far_0, piece_31, weights = arrive(far_0, piece_31, weights, marked=(far_0, to_x), flops=EARLY)
+    far_0, piece_31, mid_own = arrive(far_0, piece_31, mid_own, marked=(far_0, to_x), flops=EARLY)
     far_1 = sent((3, 1), piece_31)
-    both = project(upstream, weights)
-
-    x_2, y_2, factor_near, both, out_own, gate_pre = arrive(x_2, y_2, factor_near, both, out_own, gate_pre)
+    out_own = outer_swap(mid_own)
+
+    x_2, y_2, factor_near, other_tokens = arrive(x_2, y_2, factor_near, other_tokens)
     to_x, to_y = stack_rows(
         [
             [(far_0, 0, quarter), (y_2, half, half)],
@@ -391,16 +399,17 @@
         ],
         EARLY,
     )
+    sent_3 = to_x
     x_3, y_3 = along_x(to_x), along_y(to_y)
     near_factor = across(factor_near)
+
+    far_1, factor_near, gate_pre = arrive(far_1, factor_near, gate_pre, marked=(far_1, to_x), flops=EARLY)
+    mid_near = middle_swap(factor_near)
     up_grad, gate_grad, partial_value = row_gradients(both, gate_pre, up_pre, gate_prob, row_token, block_expert)
 
-    far_1, factor_near, partial_value, up_grad, gate_grad = arrive(
-        far_1, factor_near, partial_value, up_grad, gate_grad, marked=(far_1, to_x), flops=EARLY
-    )
-    mid_near = middle_swap(factor_near)
-
-    x_3, y_3, near_factor, partial_value, other_tokens = arrive(x_3, y_3, near_factor, partial_value, other_tokens)
+    x_3, y_3, near_factor, partial_value, up_grad, gate_grad = arrive(
+        x_3, y_3, near_factor, partial_value, up_grad, gate_grad
+    )
     to_x, to_y = stack_rows(
         [
             [(far_1, 0, quarter), (y_3, half, half)],
@@ -408,6 +417,7 @@
         ],
         EARLY,
     )
+    sent_4 = to_x
     x_4, y_4 = along_x(to_x), along_y(to_y)
     partial_value = partial_value + along_x(partial_value)
 
@@ -417,9 +427,9 @@
     factor_skip = jnp.where(outer, out_own, mid_near)
     skip_factor = across(factor_skip)
 
-    def hopped(own, x_hop, y_hop, row, diagonal):
+    def hopped(own, own_row, x_hop, y_hop, row, diagonal):
         parts = [own, x_hop, y_hop] + [hop for hop, _, _ in diagonal]
-        pieces = [(0, 0, quarter, 0), (1, row, quarter, quarter), (2, row, quarter, 2 * quarter)]
+        pieces = [(0, own_row, quarter, 0), (1, row, quarter, quarter), (2, row, quarter, 2 * quarter)]
         spot = 3 * quarter
         for index, (_, first, amount) in enumerate(diagonal):
             pieces.append((3 + index, first, amount, spot))
@@ -440,15 +450,15 @@
     )
     total = add_products(
         *both_sides(
-            hopped(near_0, x_0, y_0, 0, ((y_1, quarter, quarter),)),
-            hopped(near_1, x_1, y_1, 0, ((y_2, quarter, half), (x_2, quarter, half))),
+            hopped(sent_0, 0, x_0, y_0, 0, ((y_1, quarter, quarter),)),
+            hopped(sent_1, 0, x_1, y_1, 0, ((y_2, quarter, half), (x_2, quarter, half))),
         ),
         (factor_near, near_factor), total, rows,
     )
     total = add_products(
         *both_sides(
-            hopped(skip_0, x_0, y_0, quarter, ((x_1, quarter, quarter),)),
-            hopped(skip_1, x_2, y_2, 0, ((y_3, quarter, half), (x_3, quarter, half))),
+            hopped(sent_0, quarter, x_0, y_0, quarter, ((x_1, quarter, quarter),)),
+            hopped(sent_2, 0, x_2, y_2, 0, ((y_3, quarter, half), (x_3, quarter, half))),
         ),
         (factor_skip, skip_factor), total, rows,
     )
@@ -460,8 +470,8 @@
     factor_far = jnp.where(outer, out_near, mid_own)
     far_factor = across(factor_far)
     parts, pieces = both_sides(
-        hopped(far_0, x_3, y_3, 0, ((y_4, quarter, half), (x_4, quarter, half))),
-        hopped(far_1, x_4, y_4, 0, ()),
+        hopped(sent_3, 0, x_3, y_3, 0, ((y_4, quarter, half), (x_4, quarter, half))),
+        hopped(sent_4, 0, x_4, y_4, 0, ()),
     )
     total = add_products(parts, pieces, (factor_far, far_factor), total, rows)
     x_5, y_5 = arrive(x_5, y_5, marked=(x_5, y_5), flops=EARLY)

time: 126 us -> 120 us (0.952)
  local copies, waits for them, and re-layouts: 14.4 us -> 10.1 us
    unnamed x34 -> x24, local copies, waits for them, and re-layouts: 4.94 us -> 0.64 us
  transfers between devices with their start and end apart: 31 -> 31, of which waited for: 13 -> 16; matrix products, arithmetic and copies ran while one was open for 10% -> 10% of each run, Pallas kernels for 13% -> 14%
where the time goes in v4:
time: 120 us
  waiting for transfers between devices  48.7 us (41%)
  starting transfers between devices  38.4 us (32%)
  Pallas kernels  16.4 us (14%)
  local copies, waits for them, and re-layouts  10.1 us (8%)
  other arithmetic  5.33 us (4%)
    ppermute x30, waiting for transfers between devices, moved(): return lax.ppermute(value, ('blk', 'wide'), pairs)  44.5 us
    ppermute x30, starting transfers between devices, moved(): return lax.ppermute(value, ('blk', 'wide'), pairs)  34.5 us
    optimization_barrier x1, local copies, waits for them, and re-layouts, together(): return lax.optimization_barrier(values)  6.92 us
    pallas_call x5, Pallas kernels, add_products(): pl.pallas_call(kernel, out_shape=out_shape, in_specs=[pl.BlockSpec(memory...  6.54 us
    pallas_call x1, Pallas kernels, project(): pl.pallas_call(kernel, out_shape=jax.ShapeDtypeStruct((EXPERTS, rows, hid...  5.05 us
    all_to_all x1, waiting for transfers between devices, factors_body(): spread = lax.all_to_all(sums, ('blk', 'wide'), 0, 0, tiled=True)  4.16 us
    all_to_all x1, starting transfers between devices, factors_body(): spread = lax.all_to_all(sums, ('blk', 'wide'), 0, 0, tiled=True)  3.96 us
  transfers between devices with their start and end apart: 31, of which 16 were waited for; matrix products, arithmetic and copies ran while one was open for 10% of the time, Pallas kernels for 14%

profile of v4, /device:TPU:0, one launch (start us, length us, event | category | flops | bytes accessed | tf_op | source)
XLA Modules:
  0.0 119.9 jit_solution(8032674377022266986)
XLA Ops:
  0.7 2.2 %dynamic-slice_convert_fusion.2 = (f32[96,896]{1,0:T(8,128)}, f32[96,896]{1,0:T(8,128)S(1)}, f32[96,896]{1,0:T(8,128)S(1)}, f32[96,896]{1,0:T(8,128)}) fusion(bf16[384,7168]{1,0:T(8,128)(2,1)} %upstream_ref.1, s32[]{:T(128)S(6)} %select_n.77, s32[]{:T(128)S(6)} %select_n.83, s32[]{:T(128)S(6)} %select_n.82, s32[]{:T(128)S(6)} %select_n.81, s32[]{:T(128)S(6)} %select_n.80), kind=kLoop, calls=%fused_computation.7 | loop fusion | flops 344064 | bytes 2064404 | tf_op jit(solution)/shard_map/convert_element_type | solution.py:308
  2.9 3.0 %collective-permute-start.2 = (f32[96,896]{1,0:T(8,128)S(1)}, f32[96,896]{1,0:T(8,128)S(1)}, u32[]{:S(2)}, u32[]{:S(2)}) collective-permute-start(f32[96,896]{1,0:T(8,128)S(1)} %get-tuple-element.173), channel_id=1, source_target_pairs={{0,2},{1,3},{2,0},{3,1},{4,6},{5,7},{6,4},{7,5},{8,10},{9,11},{10,... | collective-permute-start | bytes 1032200 | tf_op jit(solution)/shard_map/ppermute | solution.py:287
  5.9 2.6 %collective-permute-start.3 = (f32[96,896]{1,0:T(8,128)S(1)}, f32[96,896]{1,0:T(8,128)S(1)}, u32[]{:S(2)}, u32[]{:S(2)}) collective-permute-start(f32[96,896]{1,0:T(8,128)S(1)} %get-tuple-element.172), channel_id=1, source_target_pairs={{0,4},{1,5},{2,6},{3,7},{4,0},{5,1},{6,2},{7,3},{8,12},{9,13},{10,... | collective-permute-start | bytes 1032200 | tf_op jit(solution)/shard_map/ppermute | solution.py:287
  8.5 2.3 %shard_map.110.refs_2_ = f32[392,256]{1,0:T(8,128)} custom-call(s32[3]{0:T(128)} %expert_ref.3, s32[1]{0:T(128)} %bitcast.index_ref, bf16[384,256]{1,0:T(8,128)(2,1)} %gate_ref.2, bf16[384,256]{1,0:T(8,128)(2,1)} %up_ref.3, f32[384]{0:T(512)} %prob_ref.3, s32[384]{0:T(512)} %token_ref.3), custom_call_target="tpu_custom_call" | custom-call | flops 75497472 | bytes 1179648 | tf_op jit(solution)/shard_map/pallas_call | solution.py:206
  10.8 0.5 collective-permute-start.1
  11.3 6.9 %copy.16 = bf16[7168,2,256]{2,0,1:T(8,128)(2,1)} copy(bf16[7168,2,256]{2,1,0:T(2,128)(2,1)} %param.10) | data formatting | bytes 14680064 | tf_op jit(solution)/shard_map/optimization_barrier | solution.py:263
  18.2 2.3 %collective-permute-done.2.refs_0_ = f32[96,896]{1,0:T(8,128)S(1)} collective-permute-done((f32[96,896]{1,0:T(8,128)S(1)}, f32[96,896]{1,0:T(8,128)S(1)}, u32[]{:S(2)}, u32[]{:S(2)}) %collective-permute-start.2) | collective-permute-done | bytes 344096 | tf_op jit(solution)/shard_map/ppermute | solution.py:287
  20.6 4.6 %collective-permute-done.3.refs_1_ = f32[96,896]{1,0:T(8,128)S(1)} collective-permute-done((f32[96,896]{1,0:T(8,128)S(1)}, f32[96,896]{1,0:T(8,128)S(1)}, u32[]{:S(2)}, u32[]{:S(2)}) %collective-permute-start.3) | collective-permute-done | bytes 344096 | tf_op jit(solution)/shard_map/ppermute | solution.py:287
  25.2 1.6 %collective-permute-start.5 = (f32[192,896]{1,0:T(8,128)S(1)}, f32[192,896]{1,0:T(8,128)S(1)}, u32[]{:S(2)}, u32[]{:S(2)}) collective-permute-start(f32[192,896]{1,0:T(8,128)S(1)} %shard_map.111.refs_1_.refs_0_), channel_id=1, source_target_pairs={{0,8},{1,9},{2,10},{3,11},{4,12},{5,13},{6,14},{7,15},{8,0},{9,1},... | collective-permute-start | bytes 2064392 | tf_op jit(solution)/shard_map/ppermute | solution.py:287
  26.8 1.5 %collective-permute-start.6 = (f32[192,896]{1,0:T(8,128)S(1)}, f32[192,896]{1,0:T(8,128)S(1)}, u32[]{:S(2)}, u32[]{:S(2)}) collective-permute-start(f32[192,896]{1,0:T(8,128)S(1)} %shard_map.111.refs_1_.refs_0_), channel_id=1, source_target_pairs={{0,16},{1,17},{2,18},{3,19},{4,20},{5,21},{6,22},{7,23},{8,24},{9,... | collective-permute-start | bytes 2064392 | tf_op jit(solution)/shard_map/ppermute | solution.py:287
  28.3 0.6 copy-done.6
  28.9 3.9 %collective-permute-start.4 = (f32[96,896]{1,0:T(8,128)}, f32[96,896]{1,0:T(8,128)S(1)}, u32[]{:S(2)}, u32[]{:S(2)}) collective-permute-start(f32[96,896]{1,0:T(8,128)} %get-tuple-element.88), channel_id=1, source_target_pairs={{0,5},{1,4},{2,7},{3,6},{4,1},{5,0},{6,3},{7,2},{8,13},{9,12},{10,... | collective-permute-start | bytes 1032200 | tf_op jit(solution)/shard_map/ppermute | solution.py:287
  32.8 1.7 %fusion.1 = (bf16[96,896]{1,0:T(8,128)(2,1)S(1)}, bf16[96,896]{1,0:T(8,128)(2,1)S(1)}, bf16[96,896]{1,0:T(8,128)(2,1)S(1)}, bf16[96,896]{1,0:T(8,128)(2,1)S(1)},...) fusion(bf16[384,7168]{1,0:T(8,128)(2,1)} %upstream_ref.1, ...), kind=kLoop, calls=%fused_computation.14 | loop fusion | flops 172032 | bytes 3784736 | tf_op jit(solution)/shard_map/dynamic_slice | solution.py:324
  34.7 6.0 %collective-permute-done.7.refs_0_ = f32[96,896]{1,0:T(8,128)S(1)} collective-permute-done((f32[96,896]{1,0:T(8,128)}, f32[96,896]{1,0:T(8,128)S(1)}, u32[]{:S(2)}, u32[]{:S(2)}) %collective-permute-start.7) | collective-permute-done | bytes 344096 | tf_op jit(solution)/shard_map/ppermute | solution.py:287
  41.0 6.0 %collective-permute-done.4.refs_0_ = f32[96,896]{1,0:T(8,128)S(1)} collective-permute-done((f32[96,896]{1,0:T(8,128)}, f32[96,896]{1,0:T(8,128)S(1)}, u32[]{:S(2)}, u32[]{:S(2)}) %collective-permute-start.4) | collective-permute-done | bytes 344096 | tf_op jit(solution)/shard_map/ppermute | solution.py:287
  47.0 1.4 %collective-permute-start.8 = (f32[96,896]{1,0:T(8,128)S(1)}, f32[96,896]{1,0:T(8,128)S(1)}, u32[]{:S(2)}, u32[]{:S(2)}) collective-permute-start(f32[96,896]{1,0:T(8,128)S(1)} %get-tuple-element.100), channel_id=1, source_target_pairs={{0,6},{1,7},{2,4},{3,5},{4,2},{5,3},{6,0},{7,1},{8,14},{9,15},{10,... | collective-permute-start | bytes 1032200 | tf_op jit(solution)/shard_map/ppermute | solution.py:287
  48.4 5.0 %shard_map.115.both_ref = f32[2,384,256]{2,1,0:T(8,128)S(1)} custom-call(bf16[384,7168]{1,0:T(8,128)(2,1)S(1)} %bitcast.11, bf16[2,7168,256]{2,1,0:T(8,128)(2,1)S(1)} %bitcast.9), custom_call_target="tpu_custom_call" | custom-call | flops 2818572288 | bytes 12845056 | tf_op jit(solution)/shard_map/pallas_call | solution.py:152
  53.5 3.0 %collective-permute-done.10.refs_1_.refs_3_.refs_6_ = f32[192,896]{1,0:T(8,128)S(1)} collective-permute-done((f32[192,896]{1,0:T(8,128)S(1)}, f32[192,896]{1,0:T(8,128)S(1)}, u32[]{:S(2)}, u32[]{:S(2)}) %collective-permute-start.10) | collective-permute-done | bytes 688160 | tf_op jit(solution)/shard_map/ppermute | solution.py:287
  57.0 1.7 %collective-permute-start.13 = (f32[144,896]{1,0:T(8,128)S(1)}, f32[144,896]{1,0:T(8,128)S(1)}, u32[]{:S(2)}, u32[]{:S(2)}) collective-permute-start(f32[144,896]{1,0:T(8,128)S(1)} %get-tuple-element.114), channel_id=1, source_target_pairs={{0,16},{1,17},{2,18},{3,19},{4,20},{5,21},{6,22},{7,23},{8,24},{9,... | collective-permute-start | bytes 1548296 | tf_op jit(solution)/shard_map/ppermute | solution.py:287
  58.7 1.5 %collective-permute-start.14 = (f32[392,256]{1,0:T(8,128)S(1)}, f32[392,256]{1,0:T(8,128)S(1)}, u32[]{:S(2)}, u32[]{:S(2)}) collective-permute-start(f32[392,256]{1,0:T(8,128)S(1)} %copy-done), channel_id=1, source_target_pairs={{0,2},{1,3},{2,0},{3,1},{4,6},{5,7},{6,4},{7,5},{8,10},{9,11},{10,... | collective-permute-start | bytes 1204232 | tf_op jit(solution)/shard_map/ppermute | solution.py:287
  60.2 2.3 %collective-permute-start.11 = (f32[96,896]{1,0:T(8,128)S(1)}, f32[96,896]{1,0:T(8,128)S(1)}, u32[]{:S(2)}, u32[]{:S(2)}) collective-permute-start(f32[96,896]{1,0:T(8,128)S(1)} %get-tuple-element.113), channel_id=1, source_target_pairs={{0,7},{1,6},{2,5},{3,4},{4,3},{5,2},{6,1},{7,0},{8,15},{9,14},{10,... | collective-permute-start | bytes 1032200 | tf_op jit(solution)/shard_map/ppermute | solution.py:287
  62.5 7.9 %collective-permute-done.14.refs_9_ = f32[392,256]{1,0:T(8,128)S(1)} collective-permute-done((f32[392,256]{1,0:T(8,128)S(1)}, f32[392,256]{1,0:T(8,128)S(1)}, u32[]{:S(2)}, u32[]{:S(2)}) %collective-permute-start.14) | collective-permute-done | bytes 401440 | tf_op jit(solution)/shard_map/ppermute | solution.py:287
  70.4 1.9 %collective-permute-start.23 = (f32[392,256]{1,0:T(8,128)S(1)}, f32[392,256]{1,0:T(8,128)S(1)}, u32[]{:S(2)}, u32[]{:S(2)}) collective-permute-start(f32[392,256]{1,0:T(8,128)S(1)} %collective-permute-done.refs_0_), channel_id=1, source_target_pairs={{0,2},{1,3},{2,0},{3,1},{4,6},{5,7},{6,4},{7,5},{8,10},{9,11},{10,... | collective-permute-start | bytes 1204232 | tf_op jit(solution)/shard_map/ppermute | solution.py:287
  72.4 1.8 %collective-permute-start.16 = (f32[144,896]{1,0:T(8,128)S(1)}, f32[144,896]{1,0:T(8,128)S(1)}, u32[]{:S(2)}, u32[]{:S(2)}) collective-permute-start(f32[144,896]{1,0:T(8,128)S(1)} %get-tuple-element.122.refs_1_.refs_0_), channel_id=1, source_target_pairs={{0,8},{1,9},{2,10},{3,11},{4,12},{5,13},{6,14},{7,15},{8,0},{9,1},... | collective-permute-start | bytes 1548296 | tf_op jit(solution)/shard_map/ppermute | solution.py:287
  74.2 0.4 collective-permute-start.17
  74.6 4.9 %collective-permute-done.11.refs_0_ = f32[96,896]{1,0:T(8,128)S(1)} collective-permute-done((f32[96,896]{1,0:T(8,128)S(1)}, f32[96,896]{1,0:T(8,128)S(1)}, u32[]{:S(2)}, u32[]{:S(2)}) %collective-permute-start.11) | collective-permute-done | bytes 344096 | tf_op jit(solution)/shard_map/ppermute | solution.py:287
  79.5 0.5 collective-permute-start.22
  80.0 2.1 %shard_map.120 = (bf16[384,256]{1,0:T(8,128)(2,1)}, bf16[384,256]{1,0:T(8,128)(2,1)}, f32[8,384]{1,0:T(8,128)S(1)}) custom-call(s32[3]{0:T(128)S(1)} %copy-done.5, f32[2,384,256]{2,1,0:T(8,128)S(1)} %shard_map.115.both_ref, bf16[384,256]{1,0:T(8,128)(2,1)S(1)} %copy-done.1, bf16[384,256]{1,0:T(8,128)(2,1)S(1)} %copy-done.2, f32[384]{0:T(512)S(1)} %copy-done.3, ...), custom_call_target="tpu_custom_call" | custom-call | flops 226492416 | bytes 1966080 | tf_op jit(solution)/shard_map/pallas_call | solution.py:248
  82.3 1.3 %shard_map.125.refs_11_ = f32[896,512]{1,0:T(8,128)S(1)} custom-call(f32[384,896]{1,0:T(8,128)S(1)} %get-tuple-element.152.refs_0_, f32[384,896]{1,0:T(8,128)S(1)} %collective-permute-done.15.refs_1_, f32[392,256]{1,0:T(8,128)S(1)} %copy-done, f32[392,256]{1,0:T(8,128)S(1)} %collective-permute-done.1.refs_3_, f32[896,512]{1,0:T(8,128)S(1)} %broadcast_in_dim.3.refs_4_), custom_call_target="tpu_custom_call" | custom-call | flops 704643072 | bytes 7208960 | tf_op jit(solution)/shard_map/pallas_call | solution.py:72
  83.7 1.5 %collective-permute-done.16.refs_2_.refs_8_.refs_1_ = f32[144,896]{1,0:T(8,128)S(1)} collective-permute-done((f32[144,896]{1,0:T(8,128)S(1)}, f32[144,896]{1,0:T(8,128)S(1)}, u32[]{:S(2)}, u32[]{:S(2)}) %collective-permute-start.16) | collective-permute-done | bytes 516128 | tf_op jit(solution)/shard_map/ppermute | solution.py:287
  85.2 1.5 %collective-permute-done.17.refs_1_.refs_7_.refs_2_ = f32[144,896]{1,0:T(8,128)S(1)} collective-permute-done((f32[144,896]{1,0:T(8,128)S(1)}, f32[144,896]{1,0:T(8,128)S(1)}, u32[]{:S(2)}, u32[]{:S(2)}) %collective-permute-start.17) | collective-permute-done | bytes 516128 | tf_op jit(solution)/shard_map/ppermute | solution.py:287
  87.5 0.8 collective-permute-done.23
  88.3 1.7 %collective-permute-start.21 = (f32[8,384]{1,0:T(8,128)S(1)}, f32[8,384]{1,0:T(8,128)S(1)}, u32[]{:S(2)}, u32[]{:S(2)}) collective-permute-start(f32[8,384]{1,0:T(8,128)S(1)} %get-tuple-element.136), channel_id=1, source_target_pairs={{0,8},{1,9},{2,10},{3,11},{4,12},{5,13},{6,14},{7,15},{8,0},{9,1},... | collective-permute-start | bytes 36872 | tf_op jit(solution)/shard_map/ppermute | solution.py:287
  90.1 3.6 %collective-permute-start.26 = (f32[392,256]{1,0:T(8,128)S(1)}, f32[392,256]{1,0:T(8,128)S(1)}, u32[]{:S(2)}, u32[]{:S(2)}) collective-permute-start(f32[392,256]{1,0:T(8,128)S(1)} %collective-permute-done.22.refs_0_), channel_id=1, source_target_pairs={{0,2},{1,3},{2,0},{3,1},{4,6},{5,7},{6,4},{7,5},{8,10},{9,11},{10,... | collective-permute-start | bytes 1204232 | tf_op jit(solution)/shard_map/ppermute | solution.py:287
  93.8 1.3 %shard_map.126.refs_11_ = f32[896,512]{1,0:T(8,128)S(1)} custom-call(f32[192,896]{1,0:T(8,128)S(1)} %shard_map.111.refs_1_.refs_0_, f32[192,896]{1,0:T(8,128)S(1)} %collective-permute-done.5.refs_2_.refs_1_, f32[192,896]{1,0:T(8,128)S(1)} %collective-permute-done.6.refs_1_.refs_2_, f32[192,896]{1,0:T(8,128)S(1)} %collective-permute-done.10.refs_1_.refs_3_.refs_6_, ...), custom_call_target="tpu_custom_call" | custom-call | flops 704643072 | bytes 7208960 | tf_op jit(solution)/shard_map/pallas_call | solution.py:72
  95.1 3.5 %collective-permute-done.21 = f32[8,384]{1,0:T(8,128)S(1)} collective-permute-done((f32[8,384]{1,0:T(8,128)S(1)}, f32[8,384]{1,0:T(8,128)S(1)}, u32[]{:S(2)}, u32[]{:S(2)}) %collective-permute-start.21) | collective-permute-done | bytes 12320 | tf_op jit(solution)/shard_map/ppermute | solution.py:287
  99.0 1.2 collective-permute-start.24
  100.6 1.2 collective-permute-done.26
  101.9 1.3 %shard_map.127.refs_10_ = f32[896,512]{1,0:T(8,128)S(1)} custom-call(f32[192,896]{1,0:T(8,128)S(1)} %shard_map.111.refs_1_.refs_0_, f32[192,896]{1,0:T(8,128)S(1)} %collective-permute-done.5.refs_2_.refs_1_, f32[192,896]{1,0:T(8,128)S(1)} %collective-permute-done.6.refs_1_.refs_2_, f32[192,896]{1,0:T(8,128)S(1)} %collective-permute-done.9.refs_2_.refs_5_.refs_3_, ...), custom_call_target="tpu_custom_call" | custom-call | flops 704643072 | bytes 7208960 | tf_op jit(solution)/shard_map/pallas_call | solution.py:72
  103.2 1.6 %collective-permute-start.29 = (f32[8,384]{1,0:T(8,128)S(1)}, f32[8,384]{1,0:T(8,128)S(1)}, u32[]{:S(2)}, u32[]{:S(2)}) collective-permute-start(f32[8,384]{1,0:T(8,128)S(1)} %add.111), channel_id=1, source_target_pairs={{0,16},{1,17},{2,18},{3,19},{4,20},{5,21},{6,22},{7,23},{8,24},{9,... | collective-permute-start | bytes 36872 | tf_op jit(solution)/shard_map/ppermute | solution.py:287
  104.8 0.8 collective-permute-done.25.refs_1_.refs_0_
  105.6 1.4 %shard_map.128.refs_3_ = f32[896,512]{1,0:T(8,128)S(1)} custom-call(f32[144,896]{1,0:T(8,128)S(1)} %get-tuple-element.122.refs_1_.refs_0_, f32[144,896]{1,0:T(8,128)S(1)} %collective-permute-done.16.refs_2_.refs_8_.refs_1_, f32[144,896]{1,0:T(8,128)S(1)} %collective-permute-done.17.refs_1_.refs_7_.refs_2_, ...), custom_call_target="tpu_custom_call" | custom-call | flops 616562688 | bytes 6766592 | tf_op jit(solution)/shard_map/pallas_call | solution.py:72
  107.0 1.3 %shard_map.129 = (f32[896,512]{1,0:T(8,128)S(1)}, f32[32,128]{1,0:T(8,128)}) custom-call(f32[48,896]{1,0:T(8,128)S(1)} %collective-permute-done.25.refs_1_.refs_0_, f32[48,896]{1,0:T(8,128)S(1)} %collective-permute-done.24.refs_0_.refs_1_, f32[392,256]{1,0:T(8,128)S(1)} %collective-permute-done.27.refs_9_.refs_2_, f32[896,512]{1,0:T(8,128)S(1)} %shard_map.128.refs_3_, ...), custom_call_target="tpu_custom_call" | custom-call | flops 88080384 | bytes 4112384 | tf_op jit(solution)/shard_map/pallas_call | solution.py:72
  108.2 4.0 %all-to-all-start = ((f32[32,1,128]{2,1,0:T(1,128)}), f32[32,1,128]{2,1,0:T(1,128)S(1)}, u32[]{:S(2)}, u32[]{:S(2)}) async-start(f32[32,1,128]{2,1,0:T(1,128)} %bitcast.3), calls=%async_computation | async-start | bytes 32768 | tf_op jit(solution)/shard_map/all_to_all | solution.py:486
  112.2 0.6 fusion
  112.8 2.4 %reshape.19 = f32[896,2,256]{2,1,0:T(2,128)} reshape(f32[896,512]{1,0:T(8,128)S(1)} %get-tuple-element.156) | data formatting | bytes 3670016 | tf_op jit(solution)/shard_map/reshape | solution.py:485
  115.2 4.2 %all-to-all-done = f32[32,1,128]{2,1,0:T(1,128)S(1)} async-done(((f32[32,1,128]{2,1,0:T(1,128)}), f32[32,1,128]{2,1,0:T(1,128)S(1)}, u32[]{:S(2)}, u32[]{:S(2)}) %all-to-all-start) | async-done | bytes 16416 | tf_op jit(solution)/shard_map/all_to_all | solution.py:486
  119.4 0.5 multiply_sqrt_fusion
  (72 shorter events, 3.2 us)
Async XLA Ops:
  2.9 17.7 %collective-permute-start.2 = (f32[96,896]{1,0:T(8,128)S(1)}, f32[96,896]{1,0:T(8,128)S(1)}, u32[]{:S(2)}, u32[]{:S(2)}) collective-permute-start(f32[96,896]{1,0:T(8,128)S(1)} %get-tuple-element.173), channel_id=1, source_target_pairs={{0,2},{1,3},{2,0},{3,1},{4,6},{5,7},{6,4},{7,5},{8,10},{9,11},{10,... | collective-permute-start | bytes 1032200 | tf_op jit(solution)/shard_map/ppermute | solution.py:287
  5.9 19.3 %collective-permute-start.3 = (f32[96,896]{1,0:T(8,128)S(1)}, f32[96,896]{1,0:T(8,128)S(1)}, u32[]{:S(2)}, u32[]{:S(2)}) collective-permute-start(f32[96,896]{1,0:T(8,128)S(1)} %get-tuple-element.172), channel_id=1, source_target_pairs={{0,4},{1,5},{2,6},{3,7},{4,0},{5,1},{6,2},{7,3},{8,12},{9,13},{10,... | collective-permute-start | bytes 1032200 | tf_op jit(solution)/shard_map/ppermute | solution.py:287
  10.8 17.5 %collective-permute-start = (f32[392,256]{1,0:T(8,128)}, f32[392,256]{1,0:T(8,128)S(1)}, u32[]{:S(2)}, u32[]{:S(2)}) collective-permute-start(f32[392,256]{1,0:T(8,128)} %shard_map.110.refs_2_), channel_id=1, source_target_pairs={{0,1},{1,0},{2,4},{3,5},{4,2},{5,3},{6,7},{7,6},{8,9},{9,8},{10,12... | collective-permute-start | bytes 1204232 | tf_op jit(solution)/shard_map/ppermute | solution.py:287
  10.8 18.1 %collective-permute-start.1 = (f32[392,256]{1,0:T(8,128)}, f32[392,256]{1,0:T(8,128)S(1)}, u32[]{:S(2)}, u32[]{:S(2)}) collective-permute-start(f32[392,256]{1,0:T(8,128)} %shard_map.110.refs_2_), channel_id=1, source_target_pairs={{0,1},{1,0},{2,3},{3,2},{4,5},{5,4},{6,7},{7,6},{8,9},{9,8},{10,11... | collective-permute-start | bytes 1204232 | tf_op jit(solution)/shard_map/ppermute | solution.py:287
  25.2 15.5 %collective-permute-start.5 = (f32[192,896]{1,0:T(8,128)S(1)}, f32[192,896]{1,0:T(8,128)S(1)}, u32[]{:S(2)}, u32[]{:S(2)}) collective-permute-start(f32[192,896]{1,0:T(8,128)S(1)} %shard_map.111.refs_1_.refs_0_), channel_id=1, source_target_pairs={{0,8},{1,9},{2,10},{3,11},{4,12},{5,13},{6,14},{7,15},{8,0},{9,1},... | collective-permute-start | bytes 2064392 | tf_op jit(solution)/shard_map/ppermute | solution.py:287
  26.8 13.9 %collective-permute-start.6 = (f32[192,896]{1,0:T(8,128)S(1)}, f32[192,896]{1,0:T(8,128)S(1)}, u32[]{:S(2)}, u32[]{:S(2)}) collective-permute-start(f32[192,896]{1,0:T(8,128)S(1)} %shard_map.111.refs_1_.refs_0_), channel_id=1, source_target_pairs={{0,16},{1,17},{2,18},{3,19},{4,20},{5,21},{6,22},{7,23},{8,24},{9,... | collective-permute-start | bytes 2064392 | tf_op jit(solution)/shard_map/ppermute | solution.py:287
  28.3 12.4 %collective-permute-start.7 = (f32[96,896]{1,0:T(8,128)}, f32[96,896]{1,0:T(8,128)S(1)}, u32[]{:S(2)}, u32[]{:S(2)}) collective-permute-start(f32[96,896]{1,0:T(8,128)} %get-tuple-element.89), channel_id=1, source_target_pairs={{0,3},{1,2},{2,1},{3,0},{4,7},{5,6},{6,5},{7,4},{8,11},{9,10},{10,... | collective-permute-start | bytes 1032200 | tf_op jit(solution)/shard_map/ppermute | solution.py:287
  28.3 0.6 copy-start.6
  28.9 18.1 %collective-permute-start.4 = (f32[96,896]{1,0:T(8,128)}, f32[96,896]{1,0:T(8,128)S(1)}, u32[]{:S(2)}, u32[]{:S(2)}) collective-permute-start(f32[96,896]{1,0:T(8,128)} %get-tuple-element.88), channel_id=1, source_target_pairs={{0,5},{1,4},{2,7},{3,6},{4,1},{5,0},{6,3},{7,2},{8,13},{9,12},{10,... | collective-permute-start | bytes 1032200 | tf_op jit(solution)/shard_map/ppermute | solution.py:287
  40.7 6.3 %copy-start.7 = (f32[8,128]{1,0:T(8,128)S(1)}, f32[8,128]{1,0:T(8,128)}, u32[]{:S(2)}) copy-start(f32[8,128]{1,0:T(8,128)} %copy-done.6) | copy-start | bytes 12292
  40.7 7.7 %slice-start = ((s8[7340032]{0:T(1024)(128)(4,1)}), s8[4194304]{0:T(1024)(128)(4,1)S(1)}, s32[]{:S(2)}) async-start(s8[7340032]{0:T(1024)(128)(4,1)} %bitcast.7), calls=%async_computation.1 | async-start | bytes 8388608
  40.7 7.7 %slice-start.2 = ((s8[5505024]{0:T(1024)(128)(4,1)}), s8[4194304]{0:T(1024)(128)(4,1)S(1)}, s32[]{:S(2)}) async-start(s8[5505024]{0:T(1024)(128)(4,1)} %bitcast.10), calls=%async_computation.3 | async-start | bytes 8388608
  40.8 7.6 %slice-start.1 = ((s8[7340032]{0:T(1024)(128)(4,1)}), s8[3145728]{0:T(1024)(128)(4,1)S(1)}, s32[]{:S(2)}) async-start(s8[7340032]{0:T(1024)(128)(4,1)} %bitcast.7), calls=%async_computation.2 | async-start | bytes 6291456
  40.8 7.6 %slice-start.3 = ((s8[5505024]{0:T(1024)(128)(4,1)}), s8[1310720]{0:T(1024)(128)(4,1)S(1)}, s32[]{:S(2)}) async-start(s8[5505024]{0:T(1024)(128)(4,1)} %bitcast.10), calls=%async_computation.4 | async-start | bytes 2621440
  40.9 15.7 %collective-permute-start.10 = (f32[192,896]{1,0:T(8,128)S(1)}, f32[192,896]{1,0:T(8,128)S(1)}, u32[]{:S(2)}, u32[]{:S(2)}) collective-permute-start(f32[192,896]{1,0:T(8,128)S(1)} %get-tuple-element.104), channel_id=1, source_target_pairs={{0,16},{1,17},{2,18},{3,19},{4,20},{5,21},{6,22},{7,23},{8,24},{9,... | collective-permute-start | bytes 2064392 | tf_op jit(solution)/shard_map/ppermute | solution.py:287
  40.9 15.7 %collective-permute-start.9 = (f32[192,896]{1,0:T(8,128)S(1)}, f32[192,896]{1,0:T(8,128)S(1)}, u32[]{:S(2)}, u32[]{:S(2)}) collective-permute-start(f32[192,896]{1,0:T(8,128)S(1)} %get-tuple-element.98.refs_1_.refs_4_), channel_id=1, source_target_pairs={{0,8},{1,9},{2,10},{3,11},{4,12},{5,13},{6,14},{7,15},{8,0},{9,1},... | collective-permute-start | bytes 2064392 | tf_op jit(solution)/shard_map/ppermute | solution.py:287
  47.0 13.2 %collective-permute-start.8 = (f32[96,896]{1,0:T(8,128)S(1)}, f32[96,896]{1,0:T(8,128)S(1)}, u32[]{:S(2)}, u32[]{:S(2)}) collective-permute-start(f32[96,896]{1,0:T(8,128)S(1)} %get-tuple-element.100), channel_id=1, source_target_pairs={{0,6},{1,7},{2,4},{3,5},{4,2},{5,3},{6,0},{7,1},{8,14},{9,15},{10,... | collective-permute-start | bytes 1032200 | tf_op jit(solution)/shard_map/ppermute | solution.py:287
  53.5 5.2 %copy-start = (f32[392,256]{1,0:T(8,128)S(1)}, f32[392,256]{1,0:T(8,128)}, u32[]{:S(2)}) copy-start(f32[392,256]{1,0:T(8,128)} %shard_map.110.refs_2_) | copy-start | bytes 1204228
  56.7 15.6 %collective-permute-start.12 = (f32[144,896]{1,0:T(8,128)S(1)}, f32[144,896]{1,0:T(8,128)S(1)}, u32[]{:S(2)}, u32[]{:S(2)}) collective-permute-start(f32[144,896]{1,0:T(8,128)S(1)} %get-tuple-element.111.refs_1_.refs_4_), channel_id=1, source_target_pairs={{0,8},{1,9},{2,10},{3,11},{4,12},{5,13},{6,14},{7,15},{8,0},{9,1},... | collective-permute-start | bytes 1548296 | tf_op jit(solution)/shard_map/ppermute | solution.py:287
  57.0 15.3 %collective-permute-start.13 = (f32[144,896]{1,0:T(8,128)S(1)}, f32[144,896]{1,0:T(8,128)S(1)}, u32[]{:S(2)}, u32[]{:S(2)}) collective-permute-start(f32[144,896]{1,0:T(8,128)S(1)} %get-tuple-element.114), channel_id=1, source_target_pairs={{0,16},{1,17},{2,18},{3,19},{4,20},{5,21},{6,22},{7,23},{8,24},{9,... | collective-permute-start | bytes 1548296 | tf_op jit(solution)/shard_map/ppermute | solution.py:287
  58.7 13.6 %collective-permute-start.15 = (f32[384,896]{1,0:T(8,128)S(1)}, f32[384,896]{1,0:T(8,128)S(1)}, u32[]{:S(2)}, u32[]{:S(2)}) collective-permute-start(f32[384,896]{1,0:T(8,128)S(1)} %get-tuple-element.116), channel_id=1, source_target_pairs={{0,1},{1,0},{2,3},{3,2},{4,5},{5,4},{6,7},{7,6},{8,9},{9,8},{10,11... | collective-permute-start | bytes 4128776 | tf_op jit(solution)/shard_map/ppermute | solution.py:287
  58.7 11.7 %collective-permute-start.14 = (f32[392,256]{1,0:T(8,128)S(1)}, f32[392,256]{1,0:T(8,128)S(1)}, u32[]{:S(2)}, u32[]{:S(2)}) collective-permute-start(f32[392,256]{1,0:T(8,128)S(1)} %copy-done), channel_id=1, source_target_pairs={{0,2},{1,3},{2,0},{3,1},{4,6},{5,7},{6,4},{7,5},{8,10},{9,11},{10,... | collective-permute-start | bytes 1204232 | tf_op jit(solution)/shard_map/ppermute | solution.py:287
  60.2 19.3 %collective-permute-start.11 = (f32[96,896]{1,0:T(8,128)S(1)}, f32[96,896]{1,0:T(8,128)S(1)}, u32[]{:S(2)}, u32[]{:S(2)}) collective-permute-start(f32[96,896]{1,0:T(8,128)S(1)} %get-tuple-element.113), channel_id=1, source_target_pairs={{0,7},{1,6},{2,5},{3,4},{4,3},{5,2},{6,1},{7,0},{8,15},{9,14},{10,... | collective-permute-start | bytes 1032200 | tf_op jit(solution)/shard_map/ppermute | solution.py:287
  70.4 17.9 %collective-permute-start.23 = (f32[392,256]{1,0:T(8,128)S(1)}, f32[392,256]{1,0:T(8,128)S(1)}, u32[]{:S(2)}, u32[]{:S(2)}) collective-permute-start(f32[392,256]{1,0:T(8,128)S(1)} %collective-permute-done.refs_0_), channel_id=1, source_target_pairs={{0,2},{1,3},{2,0},{3,1},{4,6},{5,7},{6,4},{7,5},{8,10},{9,11},{10,... | collective-permute-start | bytes 1204232 | tf_op jit(solution)/shard_map/ppermute | solution.py:287
  72.4 12.8 %collective-permute-start.16 = (f32[144,896]{1,0:T(8,128)S(1)}, f32[144,896]{1,0:T(8,128)S(1)}, u32[]{:S(2)}, u32[]{:S(2)}) collective-permute-start(f32[144,896]{1,0:T(8,128)S(1)} %get-tuple-element.122.refs_1_.refs_0_), channel_id=1, source_target_pairs={{0,8},{1,9},{2,10},{3,11},{4,12},{5,13},{6,14},{7,15},{8,0},{9,1},... | collective-permute-start | bytes 1548296 | tf_op jit(solution)/shard_map/ppermute | solution.py:287
  74.2 5.8 %copy-start.1 = (bf16[384,256]{1,0:T(8,128)(2,1)S(1)}, bf16[384,256]{1,0:T(8,128)(2,1)}, u32[]{:S(2)}) copy-start(bf16[384,256]{1,0:T(8,128)(2,1)} %gate_ref.2) | copy-start | bytes 589828
  74.2 5.8 %copy-start.2 = (bf16[384,256]{1,0:T(8,128)(2,1)S(1)}, bf16[384,256]{1,0:T(8,128)(2,1)}, u32[]{:S(2)}) copy-start(bf16[384,256]{1,0:T(8,128)(2,1)} %up_ref.3) | copy-start | bytes 589828
  74.2 5.8 %copy-start.3 = (f32[384]{0:T(512)S(1)}, f32[384]{0:T(512)}, u32[]{:S(2)}) copy-start(f32[384]{0:T(512)} %prob_ref.3) | copy-start | bytes 4612
  74.2 5.8 %copy-start.4 = (s32[384]{0:T(512)S(1)}, s32[384]{0:T(512)}, u32[]{:S(2)}) copy-start(s32[384]{0:T(512)} %token_ref.3) | copy-start | bytes 4612
  74.2 5.8 %copy-start.5 = (s32[3]{0:T(128)S(1)}, s32[3]{0:T(128)}, u32[]{:S(2)}) copy-start(s32[3]{0:T(128)} %expert_ref.3) | copy-start | bytes 40
  74.2 12.5 %collective-permute-start.17 = (f32[144,896]{1,0:T(8,128)S(1)}, f32[144,896]{1,0:T(8,128)S(1)}, u32[]{:S(2)}, u32[]{:S(2)}) collective-permute-start(f32[144,896]{1,0:T(8,128)S(1)} %get-tuple-element.125), channel_id=1, source_target_pairs={{0,16},{1,17},{2,18},{3,19},{4,20},{5,21},{6,22},{7,23},{8,24},{9,... | collective-permute-start | bytes 1548296 | tf_op jit(solution)/shard_map/ppermute | solution.py:287
  74.6 9.0 %collective-permute-start.18 = (f32[392,256]{1,0:T(8,128)S(1)}, f32[392,256]{1,0:T(8,128)S(1)}, u32[]{:S(2)}, u32[]{:S(2)}) collective-permute-start(f32[392,256]{1,0:T(8,128)S(1)} %collective-permute-done.14.refs_9_), channel_id=1, source_target_pairs={{0,1},{1,0},{2,3},{3,2},{4,5},{5,4},{6,7},{7,6},{8,9},{9,8},{10,11... | collective-permute-start | bytes 1204232 | tf_op jit(solution)/shard_map/ppermute | solution.py:287
  79.5 8.0 %collective-permute-start.22 = (f32[392,256]{1,0:T(8,128)S(1)}, f32[392,256]{1,0:T(8,128)S(1)}, u32[]{:S(2)}, u32[]{:S(2)}) collective-permute-start(f32[392,256]{1,0:T(8,128)S(1)} %collective-permute-done.14.refs_9_), channel_id=1, source_target_pairs={{0,1},{1,0},{2,4},{3,5},{4,2},{5,3},{6,7},{7,6},{8,9},{9,8},{10,12... | collective-permute-start | bytes 1204232 | tf_op jit(solution)/shard_map/ppermute | solution.py:287
  86.8 11.8 %collective-permute-start.19 = (f32[144,896]{1,0:T(8,128)S(1)}, f32[144,896]{1,0:T(8,128)S(1)}, u32[]{:S(2)}, u32[]{:S(2)}) collective-permute-start(f32[144,896]{1,0:T(8,128)S(1)} %get-tuple-element.134.refs_1_.refs_5_), channel_id=1, source_target_pairs={{0,8},{1,9},{2,10},{3,11},{4,12},{5,13},{6,14},{7,15},{8,0},{9,1},... | collective-permute-start | bytes 1548296 | tf_op jit(solution)/shard_map/ppermute | solution.py:287
  87.2 11.8 %collective-permute-start.20 = (f32[144,896]{1,0:T(8,128)S(1)}, f32[144,896]{1,0:T(8,128)S(1)}, u32[]{:S(2)}, u32[]{:S(2)}) collective-permute-start(f32[144,896]{1,0:T(8,128)S(1)} %get-tuple-element.135), channel_id=1, source_target_pairs={{0,16},{1,17},{2,18},{3,19},{4,20},{5,21},{6,22},{7,23},{8,24},{9,... | collective-permute-start | bytes 1548296 | tf_op jit(solution)/shard_map/ppermute | solution.py:287
  88.3 10.3 %collective-permute-start.21 = (f32[8,384]{1,0:T(8,128)S(1)}, f32[8,384]{1,0:T(8,128)S(1)}, u32[]{:S(2)}, u32[]{:S(2)}) collective-permute-start(f32[8,384]{1,0:T(8,128)S(1)} %get-tuple-element.136), channel_id=1, source_target_pairs={{0,8},{1,9},{2,10},{3,11},{4,12},{5,13},{6,14},{7,15},{8,0},{9,1},... | collective-permute-start | bytes 36872 | tf_op jit(solution)/shard_map/ppermute | solution.py:287
  90.1 11.7 %collective-permute-start.26 = (f32[392,256]{1,0:T(8,128)S(1)}, f32[392,256]{1,0:T(8,128)S(1)}, u32[]{:S(2)}, u32[]{:S(2)}) collective-permute-start(f32[392,256]{1,0:T(8,128)S(1)} %collective-permute-done.22.refs_0_), channel_id=1, source_target_pairs={{0,2},{1,3},{2,0},{3,1},{4,6},{5,7},{6,4},{7,5},{8,10},{9,11},{10,... | collective-permute-start | bytes 1204232 | tf_op jit(solution)/shard_map/ppermute | solution.py:287
  93.7 8.2 %collective-permute-start.28 = (f32[392,256]{1,0:T(8,128)S(1)}, f32[392,256]{1,0:T(8,128)S(1)}, u32[]{:S(2)}, u32[]{:S(2)}) collective-permute-start(f32[392,256]{1,0:T(8,128)S(1)} %broadcast_select_fusion.refs_9_), channel_id=1, source_target_pairs={{0,1},{1,0},{2,3},{3,2},{4,5},{5,4},{6,7},{7,6},{8,9},{9,8},{10,11... | collective-permute-start | bytes 1204232 | tf_op jit(solution)/shard_map/ppermute | solution.py:287
  99.0 5.8 %collective-permute-start.24 = (f32[48,896]{1,0:T(8,128)S(1)}, f32[48,896]{1,0:T(8,128)S(1)}, u32[]{:S(2)}, u32[]{:S(2)}) collective-permute-start(f32[48,896]{1,0:T(8,128)S(1)} %get-tuple-element.143), channel_id=1, source_target_pairs={{0,8},{1,9},{2,10},{3,11},{4,12},{5,13},{6,14},{7,15},{8,0},{9,1},... | collective-permute-start | bytes 516104 | tf_op jit(solution)/shard_map/ppermute | solution.py:287
  100.2 5.4 %collective-permute-start.25 = (f32[48,896]{1,0:T(8,128)S(1)}, f32[48,896]{1,0:T(8,128)S(1)}, u32[]{:S(2)}, u32[]{:S(2)}) collective-permute-start(f32[48,896]{1,0:T(8,128)S(1)} %get-tuple-element.144), channel_id=1, source_target_pairs={{0,16},{1,17},{2,18},{3,19},{4,20},{5,21},{6,22},{7,23},{8,24},{9,... | collective-permute-start | bytes 516104 | tf_op jit(solution)/shard_map/ppermute | solution.py:287
  101.8 3.8 %collective-permute-start.27 = (f32[392,256]{1,0:T(8,128)S(1)}, f32[392,256]{1,0:T(8,128)S(1)}, u32[]{:S(2)}, u32[]{:S(2)}) collective-permute-start(f32[392,256]{1,0:T(8,128)S(1)} %broadcast_select_fusion.1.refs_8_), channel_id=1, source_target_pairs={{0,1},{1,0},{2,3},{3,2},{4,5},{5,4},{6,7},{7,6},{8,9},{9,8},{10,11... | collective-permute-start | bytes 1204232 | tf_op jit(solution)/shard_map/ppermute | solution.py:287
  103.2 9.0 %collective-permute-start.29 = (f32[8,384]{1,0:T(8,128)S(1)}, f32[8,384]{1,0:T(8,128)S(1)}, u32[]{:S(2)}, u32[]{:S(2)}) collective-permute-start(f32[8,384]{1,0:T(8,128)S(1)} %add.111), channel_id=1, source_target_pairs={{0,16},{1,17},{2,18},{3,19},{4,20},{5,21},{6,22},{7,23},{8,24},{9,... | collective-permute-start | bytes 36872 | tf_op jit(solution)/shard_map/ppermute | solution.py:287
  108.2 11.1 %all-to-all-start = ((f32[32,1,128]{2,1,0:T(1,128)}), f32[32,1,128]{2,1,0:T(1,128)S(1)}, u32[]{:S(2)}, u32[]{:S(2)}) async-start(f32[32,1,128]{2,1,0:T(1,128)} %bitcast.3), calls=%async_computation | async-start | bytes 32768 | tf_op jit(solution)/shard_map/all_to_all | solution.py:486

commit v5 on v4

--- a/solution.py
+++ b/solution.py
@@ -136,7 +136,7 @@
 def project(upstream, weights):
     rows, width = upstream.shape
     hidden_share = weights.shape[2]
-    steps = 7 if width % (7 * 128) == 0 else 1
+    steps = 4 if width % (4 * 128) == 0 else 1
     block = width // steps
 
     def kernel(upstream_ref, weights_ref, out_ref):
@@ -407,8 +407,8 @@
     mid_near = middle_swap(factor_near)
     up_grad, gate_grad, partial_value = row_gradients(both, gate_pre, up_pre, gate_prob, row_token, block_expert)
 
-    x_3, y_3, near_factor, partial_value, up_grad, gate_grad = arrive(
-        x_3, y_3, near_factor, partial_value, up_grad, gate_grad
+    x_3, y_3, near_factor, partial_value, up_grad, gate_grad, own_tokens = arrive(
+        x_3, y_3, near_factor, partial_value, up_grad, gate_grad, own_tokens
     )
     to_x, to_y = stack_rows(
         [

time: 120 us -> 119 us (level)
  transfers between devices with their start and end apart: 31 -> 31, of which waited for: 16 -> 15; matrix products, arithmetic and copies ran while one was open for 10% -> 10% of each run, Pallas kernels for 14% -> 13%
where the time goes in v5:
time: 119 us
  waiting for transfers between devices  49 us (41%)
  starting transfers between devices  37.9 us (32%)
  Pallas kernels  15.7 us (13%)
  local copies, waits for them, and re-layouts  10.1 us (8%)
  other arithmetic  5.33 us (4%)
    ppermute x30, waiting for transfers between devices, moved(): return lax.ppermute(value, ('blk', 'wide'), pairs)  44.8 us
    ppermute x30, starting transfers between devices, moved(): return lax.ppermute(value, ('blk', 'wide'), pairs)  34.8 us
    optimization_barrier x1, local copies, waits for them, and re-layouts, together(): return lax.optimization_barrier(values)  6.92 us
    pallas_call x5, Pallas kernels, add_products(): pl.pallas_call(kernel, out_shape=out_shape, in_specs=[pl.BlockSpec(memory...  6.45 us
    pallas_call x1, Pallas kernels, project(): pl.pallas_call(kernel, out_shape=jax.ShapeDtypeStruct((EXPERTS, rows, hid...  4.49 us
    all_to_all x1, waiting for transfers between devices, factors_body(): spread = lax.all_to_all(sums, ('blk', 'wide'), 0, 0, tiled=True)  4.16 us
    all_to_all x1, starting transfers between devices, factors_body(): spread = lax.all_to_all(sums, ('blk', 'wide'), 0, 0, tiled=True)  3.17 us
  transfers between devices with their start and end apart: 31, of which 15 were waited for; matrix products, arithmetic and copies ran while one was open for 10% of the time, Pallas kernels for 13%

profile of v5, /device:TPU:0, one launch (start us, length us, event | category | flops | bytes accessed | tf_op | source)
XLA Modules:
  0.0 119.1 jit_solution(11745842825620689912)
XLA Ops:
  0.7 2.2 %dynamic-slice_convert_fusion.2 = (f32[96,896]{1,0:T(8,128)}, f32[96,896]{1,0:T(8,128)S(1)}, f32[96,896]{1,0:T(8,128)S(1)}, f32[96,896]{1,0:T(8,128)}) fusion(bf16[384,7168]{1,0:T(8,128)(2,1)} %upstream_ref.1, s32[]{:T(128)S(6)} %select_n.77, s32[]{:T(128)S(6)} %select_n.83, s32[]{:T(128)S(6)} %select_n.82, s32[]{:T(128)S(6)} %select_n.81, s32[]{:T(128)S(6)} %select_n.80), kind=kLoop, calls=%fused_computation.7 | loop fusion | flops 344064 | bytes 2064404 | tf_op jit(solution)/shard_map/convert_element_type | solution.py:308
  2.9 3.0 %collective-permute-start.2 = (f32[96,896]{1,0:T(8,128)S(1)}, f32[96,896]{1,0:T(8,128)S(1)}, u32[]{:S(2)}, u32[]{:S(2)}) collective-permute-start(f32[96,896]{1,0:T(8,128)S(1)} %get-tuple-element.175), channel_id=1, source_target_pairs={{0,2},{1,3},{2,0},{3,1},{4,6},{5,7},{6,4},{7,5},{8,10},{9,11},{10,... | collective-permute-start | bytes 1032200 | tf_op jit(solution)/shard_map/ppermute | solution.py:287
  5.9 2.6 %collective-permute-start.3 = (f32[96,896]{1,0:T(8,128)S(1)}, f32[96,896]{1,0:T(8,128)S(1)}, u32[]{:S(2)}, u32[]{:S(2)}) collective-permute-start(f32[96,896]{1,0:T(8,128)S(1)} %get-tuple-element.174), channel_id=1, source_target_pairs={{0,4},{1,5},{2,6},{3,7},{4,0},{5,1},{6,2},{7,3},{8,12},{9,13},{10,... | collective-permute-start | bytes 1032200 | tf_op jit(solution)/shard_map/ppermute | solution.py:287
  8.5 2.3 %shard_map.110.refs_2_ = f32[392,256]{1,0:T(8,128)} custom-call(s32[3]{0:T(128)} %expert_ref.3, s32[1]{0:T(128)} %bitcast.index_ref, bf16[384,256]{1,0:T(8,128)(2,1)} %gate_ref.2, bf16[384,256]{1,0:T(8,128)(2,1)} %up_ref.3, f32[384]{0:T(512)} %prob_ref.3, s32[384]{0:T(512)} %token_ref.3), custom_call_target="tpu_custom_call" | custom-call | flops 75497472 | bytes 1179648 | tf_op jit(solution)/shard_map/pallas_call | solution.py:206
  10.8 0.5 collective-permute-start.1
  11.3 6.9 %copy.16 = bf16[7168,2,256]{2,0,1:T(8,128)(2,1)} copy(bf16[7168,2,256]{2,1,0:T(2,128)(2,1)} %param.10) | data formatting | bytes 14680064 | tf_op jit(solution)/shard_map/optimization_barrier | solution.py:263
  18.2 2.3 %collective-permute-done.2.refs_0_ = f32[96,896]{1,0:T(8,128)S(1)} collective-permute-done((f32[96,896]{1,0:T(8,128)S(1)}, f32[96,896]{1,0:T(8,128)S(1)}, u32[]{:S(2)}, u32[]{:S(2)}) %collective-permute-start.2) | collective-permute-done | bytes 344096 | tf_op jit(solution)/shard_map/ppermute | solution.py:287
  20.6 4.6 %collective-permute-done.3.refs_1_ = f32[96,896]{1,0:T(8,128)S(1)} collective-permute-done((f32[96,896]{1,0:T(8,128)S(1)}, f32[96,896]{1,0:T(8,128)S(1)}, u32[]{:S(2)}, u32[]{:S(2)}) %collective-permute-start.3) | collective-permute-done | bytes 344096 | tf_op jit(solution)/shard_map/ppermute | solution.py:287
  25.2 1.6 %collective-permute-start.5 = (f32[192,896]{1,0:T(8,128)S(1)}, f32[192,896]{1,0:T(8,128)S(1)}, u32[]{:S(2)}, u32[]{:S(2)}) collective-permute-start(f32[192,896]{1,0:T(8,128)S(1)} %shard_map.111.refs_1_.refs_0_), channel_id=1, source_target_pairs={{0,8},{1,9},{2,10},{3,11},{4,12},{5,13},{6,14},{7,15},{8,0},{9,1},... | collective-permute-start | bytes 2064392 | tf_op jit(solution)/shard_map/ppermute | solution.py:287
  26.8 1.5 %collective-permute-start.6 = (f32[192,896]{1,0:T(8,128)S(1)}, f32[192,896]{1,0:T(8,128)S(1)}, u32[]{:S(2)}, u32[]{:S(2)}) collective-permute-start(f32[192,896]{1,0:T(8,128)S(1)} %shard_map.111.refs_1_.refs_0_), channel_id=1, source_target_pairs={{0,16},{1,17},{2,18},{3,19},{4,20},{5,21},{6,22},{7,23},{8,24},{9,... | collective-permute-start | bytes 2064392 | tf_op jit(solution)/shard_map/ppermute | solution.py:287
  28.3 0.6 copy-done.6
  28.9 3.9 %collective-permute-start.4 = (f32[96,896]{1,0:T(8,128)}, f32[96,896]{1,0:T(8,128)S(1)}, u32[]{:S(2)}, u32[]{:S(2)}) collective-permute-start(f32[96,896]{1,0:T(8,128)} %get-tuple-element.89), channel_id=1, source_target_pairs={{0,5},{1,4},{2,7},{3,6},{4,1},{5,0},{6,3},{7,2},{8,13},{9,12},{10,... | collective-permute-start | bytes 1032200 | tf_op jit(solution)/shard_map/ppermute | solution.py:287
  32.8 1.7 %fusion.1 = (bf16[96,896]{1,0:T(8,128)(2,1)S(1)}, bf16[96,896]{1,0:T(8,128)(2,1)S(1)}, bf16[96,896]{1,0:T(8,128)(2,1)S(1)}, bf16[96,896]{1,0:T(8,128)(2,1)S(1)},...) fusion(bf16[384,7168]{1,0:T(8,128)(2,1)} %upstream_ref.1, ...), kind=kLoop, calls=%fused_computation.14 | loop fusion | flops 172032 | bytes 3784736 | tf_op jit(solution)/shard_map/dynamic_slice | solution.py:324
  34.7 6.0 %collective-permute-done.7.refs_0_ = f32[96,896]{1,0:T(8,128)S(1)} collective-permute-done((f32[96,896]{1,0:T(8,128)}, f32[96,896]{1,0:T(8,128)S(1)}, u32[]{:S(2)}, u32[]{:S(2)}) %collective-permute-start.7) | collective-permute-done | bytes 344096 | tf_op jit(solution)/shard_map/ppermute | solution.py:287
  41.0 6.0 %collective-permute-done.4.refs_0_ = f32[96,896]{1,0:T(8,128)S(1)} collective-permute-done((f32[96,896]{1,0:T(8,128)}, f32[96,896]{1,0:T(8,128)S(1)}, u32[]{:S(2)}, u32[]{:S(2)}) %collective-permute-start.4) | collective-permute-done | bytes 344096 | tf_op jit(solution)/shard_map/ppermute | solution.py:287
  47.0 1.4 %collective-permute-start.8 = (f32[96,896]{1,0:T(8,128)S(1)}, f32[96,896]{1,0:T(8,128)S(1)}, u32[]{:S(2)}, u32[]{:S(2)}) collective-permute-start(f32[96,896]{1,0:T(8,128)S(1)} %get-tuple-element.101), channel_id=1, source_target_pairs={{0,6},{1,7},{2,4},{3,5},{4,2},{5,3},{6,0},{7,1},{8,14},{9,15},{10,... | collective-permute-start | bytes 1032200 | tf_op jit(solution)/shard_map/ppermute | solution.py:287
  48.4 4.5 %shard_map.115.both_ref = f32[2,384,256]{2,1,0:T(8,128)S(1)} custom-call(bf16[384,7168]{1,0:T(8,128)(2,1)S(1)} %bitcast.11, bf16[2,7168,256]{2,1,0:T(8,128)(2,1)S(1)} %bitcast.9), custom_call_target="tpu_custom_call" | custom-call | flops 2818572288 | bytes 12845056 | tf_op jit(solution)/shard_map/pallas_call | solution.py:152
  52.9 3.6 %collective-permute-done.10.refs_1_.refs_3_.refs_6_ = f32[192,896]{1,0:T(8,128)S(1)} collective-permute-done((f32[192,896]{1,0:T(8,128)S(1)}, f32[192,896]{1,0:T(8,128)S(1)}, u32[]{:S(2)}, u32[]{:S(2)}) %collective-permute-start.10) | collective-permute-done | bytes 688160 | tf_op jit(solution)/shard_map/ppermute | solution.py:287
  57.0 1.7 %collective-permute-start.13 = (f32[144,896]{1,0:T(8,128)S(1)}, f32[144,896]{1,0:T(8,128)S(1)}, u32[]{:S(2)}, u32[]{:S(2)}) collective-permute-start(f32[144,896]{1,0:T(8,128)S(1)} %get-tuple-element.115), channel_id=1, source_target_pairs={{0,16},{1,17},{2,18},{3,19},{4,20},{5,21},{6,22},{7,23},{8,24},{9,... | collective-permute-start | bytes 1548296 | tf_op jit(solution)/shard_map/ppermute | solution.py:287
  58.7 1.5 %collective-permute-start.14 = (f32[392,256]{1,0:T(8,128)S(1)}, f32[392,256]{1,0:T(8,128)S(1)}, u32[]{:S(2)}, u32[]{:S(2)}) collective-permute-start(f32[392,256]{1,0:T(8,128)S(1)} %copy-done), channel_id=1, source_target_pairs={{0,2},{1,3},{2,0},{3,1},{4,6},{5,7},{6,4},{7,5},{8,10},{9,11},{10,... | collective-permute-start | bytes 1204232 | tf_op jit(solution)/shard_map/ppermute | solution.py:287
  60.2 2.3 %collective-permute-start.11 = (f32[96,896]{1,0:T(8,128)S(1)}, f32[96,896]{1,0:T(8,128)S(1)}, u32[]{:S(2)}, u32[]{:S(2)}) collective-permute-start(f32[96,896]{1,0:T(8,128)S(1)} %get-tuple-element.114), channel_id=1, source_target_pairs={{0,7},{1,6},{2,5},{3,4},{4,3},{5,2},{6,1},{7,0},{8,15},{9,14},{10,... | collective-permute-start | bytes 1032200 | tf_op jit(solution)/shard_map/ppermute | solution.py:287
  62.5 7.9 %collective-permute-done.14.refs_9_ = f32[392,256]{1,0:T(8,128)S(1)} collective-permute-done((f32[392,256]{1,0:T(8,128)S(1)}, f32[392,256]{1,0:T(8,128)S(1)}, u32[]{:S(2)}, u32[]{:S(2)}) %collective-permute-start.14) | collective-permute-done | bytes 401440 | tf_op jit(solution)/shard_map/ppermute | solution.py:287
  70.4 1.9 %collective-permute-start.23 = (f32[392,256]{1,0:T(8,128)S(1)}, f32[392,256]{1,0:T(8,128)S(1)}, u32[]{:S(2)}, u32[]{:S(2)}) collective-permute-start(f32[392,256]{1,0:T(8,128)S(1)} %collective-permute-done.refs_0_), channel_id=1, source_target_pairs={{0,2},{1,3},{2,0},{3,1},{4,6},{5,7},{6,4},{7,5},{8,10},{9,11},{10,... | collective-permute-start | bytes 1204232 | tf_op jit(solution)/shard_map/ppermute | solution.py:287
  72.4 1.8 %collective-permute-start.16 = (f32[144,896]{1,0:T(8,128)S(1)}, f32[144,896]{1,0:T(8,128)S(1)}, u32[]{:S(2)}, u32[]{:S(2)}) collective-permute-start(f32[144,896]{1,0:T(8,128)S(1)} %get-tuple-element.123.refs_1_.refs_0_), channel_id=1, source_target_pairs={{0,8},{1,9},{2,10},{3,11},{4,12},{5,13},{6,14},{7,15},{8,0},{9,1},... | collective-permute-start | bytes 1548296 | tf_op jit(solution)/shard_map/ppermute | solution.py:287
  74.2 0.4 collective-permute-start.17
  74.6 4.9 %collective-permute-done.11.refs_0_ = f32[96,896]{1,0:T(8,128)S(1)} collective-permute-done((f32[96,896]{1,0:T(8,128)S(1)}, f32[96,896]{1,0:T(8,128)S(1)}, u32[]{:S(2)}, u32[]{:S(2)}) %collective-permute-start.11) | collective-permute-done | bytes 344096 | tf_op jit(solution)/shard_map/ppermute | solution.py:287
  79.5 0.5 collective-permute-start.22
  80.0 2.1 %shard_map.120 = (bf16[384,256]{1,0:T(8,128)(2,1)}, bf16[384,256]{1,0:T(8,128)(2,1)}, f32[8,384]{1,0:T(8,128)S(1)}) custom-call(s32[3]{0:T(128)S(1)} %copy-done.5, f32[2,384,256]{2,1,0:T(8,128)S(1)} %shard_map.115.both_ref, bf16[384,256]{1,0:T(8,128)(2,1)S(1)} %copy-done.1, bf16[384,256]{1,0:T(8,128)(2,1)S(1)} %copy-done.2, f32[384]{0:T(512)S(1)} %copy-done.3, ...), custom_call_target="tpu_custom_call" | custom-call | flops 226492416 | bytes 1966080 | tf_op jit(solution)/shard_map/pallas_call | solution.py:248
  82.1 3.1 %collective-permute-done.16.refs_2_.refs_8_.refs_1_ = f32[144,896]{1,0:T(8,128)S(1)} collective-permute-done((f32[144,896]{1,0:T(8,128)S(1)}, f32[144,896]{1,0:T(8,128)S(1)}, u32[]{:S(2)}, u32[]{:S(2)}) %collective-permute-start.16) | collective-permute-done | bytes 516128 | tf_op jit(solution)/shard_map/ppermute | solution.py:287
  85.2 1.5 %collective-permute-done.17.refs_1_.refs_7_.refs_2_ = f32[144,896]{1,0:T(8,128)S(1)} collective-permute-done((f32[144,896]{1,0:T(8,128)S(1)}, f32[144,896]{1,0:T(8,128)S(1)}, u32[]{:S(2)}, u32[]{:S(2)}) %collective-permute-start.17) | collective-permute-done | bytes 516128 | tf_op jit(solution)/shard_map/ppermute | solution.py:287
  87.5 0.8 collective-permute-done.23
  88.3 1.7 %collective-permute-start.21 = (f32[8,384]{1,0:T(8,128)S(1)}, f32[8,384]{1,0:T(8,128)S(1)}, u32[]{:S(2)}, u32[]{:S(2)}) collective-permute-start(f32[8,384]{1,0:T(8,128)S(1)} %get-tuple-element.138), channel_id=1, source_target_pairs={{0,8},{1,9},{2,10},{3,11},{4,12},{5,13},{6,14},{7,15},{8,0},{9,1},... | collective-permute-start | bytes 36872 | tf_op jit(solution)/shard_map/ppermute | solution.py:287
  90.1 3.6 %collective-permute-start.26 = (f32[392,256]{1,0:T(8,128)S(1)}, f32[392,256]{1,0:T(8,128)S(1)}, u32[]{:S(2)}, u32[]{:S(2)}) collective-permute-start(f32[392,256]{1,0:T(8,128)S(1)} %collective-permute-done.22.refs_0_), channel_id=1, source_target_pairs={{0,2},{1,3},{2,0},{3,1},{4,6},{5,7},{6,4},{7,5},{8,10},{9,11},{10,... | collective-permute-start | bytes 1204232 | tf_op jit(solution)/shard_map/ppermute | solution.py:287
  94.0 1.3 %shard_map.125.refs_11_ = f32[896,512]{1,0:T(8,128)S(1)} custom-call(f32[384,896]{1,0:T(8,128)S(1)} %get-tuple-element.154.refs_0_, f32[384,896]{1,0:T(8,128)S(1)} %collective-permute-done.15.refs_1_, f32[392,256]{1,0:T(8,128)S(1)} %copy-done, f32[392,256]{1,0:T(8,128)S(1)} %collective-permute-done.1.refs_3_, f32[896,512]{1,0:T(8,128)S(1)} %broadcast_in_dim.3.refs_4_), custom_call_target="tpu_custom_call" | custom-call | flops 704643072 | bytes 7208960 | tf_op jit(solution)/shard_map/pallas_call | solution.py:72
  95.3 1.3 %shard_map.126.refs_11_ = f32[896,512]{1,0:T(8,128)S(1)} custom-call(f32[192,896]{1,0:T(8,128)S(1)} %shard_map.111.refs_1_.refs_0_, f32[192,896]{1,0:T(8,128)S(1)} %collective-permute-done.5.refs_2_.refs_1_, f32[192,896]{1,0:T(8,128)S(1)} %collective-permute-done.6.refs_1_.refs_2_, f32[192,896]{1,0:T(8,128)S(1)} %collective-permute-done.10.refs_1_.refs_3_.refs_6_, ...), custom_call_target="tpu_custom_call" | custom-call | flops 704643072 | bytes 7208960 | tf_op jit(solution)/shard_map/pallas_call | solution.py:72
  96.6 2.0 %collective-permute-done.21 = f32[8,384]{1,0:T(8,128)S(1)} collective-permute-done((f32[8,384]{1,0:T(8,128)S(1)}, f32[8,384]{1,0:T(8,128)S(1)}, u32[]{:S(2)}, u32[]{:S(2)}) %collective-permute-start.21) | collective-permute-done | bytes 12320 | tf_op jit(solution)/shard_map/ppermute | solution.py:287
  98.7 1.5 %collective-permute-start.24 = (f32[48,896]{1,0:T(8,128)S(1)}, f32[48,896]{1,0:T(8,128)S(1)}, u32[]{:S(2)}, u32[]{:S(2)}) collective-permute-start(f32[48,896]{1,0:T(8,128)S(1)} %get-tuple-element.145), channel_id=1, source_target_pairs={{0,8},{1,9},{2,10},{3,11},{4,12},{5,13},{6,14},{7,15},{8,0},{9,1},... | collective-permute-start | bytes 516104 | tf_op jit(solution)/shard_map/ppermute | solution.py:287
  100.6 1.2 %collective-permute-done.26 = f32[392,256]{1,0:T(8,128)S(1)} collective-permute-done((f32[392,256]{1,0:T(8,128)S(1)}, f32[392,256]{1,0:T(8,128)S(1)}, u32[]{:S(2)}, u32[]{:S(2)}) %collective-permute-start.26) | collective-permute-done | bytes 401440 | tf_op jit(solution)/shard_map/ppermute | solution.py:287
  101.9 1.3 %shard_map.127.refs_10_ = f32[896,512]{1,0:T(8,128)S(1)} custom-call(f32[192,896]{1,0:T(8,128)S(1)} %shard_map.111.refs_1_.refs_0_, f32[192,896]{1,0:T(8,128)S(1)} %collective-permute-done.5.refs_2_.refs_1_, f32[192,896]{1,0:T(8,128)S(1)} %collective-permute-done.6.refs_1_.refs_2_, f32[192,896]{1,0:T(8,128)S(1)} %collective-permute-done.9.refs_2_.refs_5_.refs_3_, ...), custom_call_target="tpu_custom_call" | custom-call | flops 704643072 | bytes 7208960 | tf_op jit(solution)/shard_map/pallas_call | solution.py:72
  103.2 1.6 %collective-permute-start.29 = (f32[8,384]{1,0:T(8,128)S(1)}, f32[8,384]{1,0:T(8,128)S(1)}, u32[]{:S(2)}, u32[]{:S(2)}) collective-permute-start(f32[8,384]{1,0:T(8,128)S(1)} %add.111), channel_id=1, source_target_pairs={{0,16},{1,17},{2,18},{3,19},{4,20},{5,21},{6,22},{7,23},{8,24},{9,... | collective-permute-start | bytes 36872 | tf_op jit(solution)/shard_map/ppermute | solution.py:287
  104.8 0.8 collective-permute-done.25.refs_1_.refs_0_
  105.6 1.3 %shard_map.128.refs_3_ = f32[896,512]{1,0:T(8,128)S(1)} custom-call(f32[144,896]{1,0:T(8,128)S(1)} %get-tuple-element.123.refs_1_.refs_0_, f32[144,896]{1,0:T(8,128)S(1)} %collective-permute-done.16.refs_2_.refs_8_.refs_1_, f32[144,896]{1,0:T(8,128)S(1)} %collective-permute-done.17.refs_1_.refs_7_.refs_2_, ...), custom_call_target="tpu_custom_call" | custom-call | flops 616562688 | bytes 6766592 | tf_op jit(solution)/shard_map/pallas_call | solution.py:72
  106.9 1.3 %shard_map.129 = (f32[896,512]{1,0:T(8,128)S(1)}, f32[32,128]{1,0:T(8,128)}) custom-call(f32[48,896]{1,0:T(8,128)S(1)} %collective-permute-done.25.refs_1_.refs_0_, f32[48,896]{1,0:T(8,128)S(1)} %collective-permute-done.24.refs_0_.refs_1_, f32[392,256]{1,0:T(8,128)S(1)} %collective-permute-done.27.refs_9_.refs_2_, f32[896,512]{1,0:T(8,128)S(1)} %shard_map.128.refs_3_, ...), custom_call_target="tpu_custom_call" | custom-call | flops 88080384 | bytes 4112384 | tf_op jit(solution)/shard_map/pallas_call | solution.py:72
  108.2 3.2 %all-to-all-start = ((f32[32,1,128]{2,1,0:T(1,128)}), f32[32,1,128]{2,1,0:T(1,128)S(1)}, u32[]{:S(2)}, u32[]{:S(2)}) async-start(f32[32,1,128]{2,1,0:T(1,128)} %bitcast.3), calls=%async_computation | async-start | bytes 32768 | tf_op jit(solution)/shard_map/all_to_all | solution.py:486
  111.4 0.6 fusion
  112.0 2.4 %reshape.19 = f32[896,2,256]{2,1,0:T(2,128)} reshape(f32[896,512]{1,0:T(8,128)S(1)} %get-tuple-element.158) | data formatting | bytes 3670016 | tf_op jit(solution)/shard_map/reshape | solution.py:485
  114.4 4.2 %all-to-all-done = f32[32,1,128]{2,1,0:T(1,128)S(1)} async-done(((f32[32,1,128]{2,1,0:T(1,128)}), f32[32,1,128]{2,1,0:T(1,128)S(1)}, u32[]{:S(2)}, u32[]{:S(2)}) %all-to-all-start) | async-done | bytes 16416 | tf_op jit(solution)/shard_map/all_to_all | solution.py:486
  118.6 0.5 multiply_sqrt_fusion
  (72 shorter events, 2.9 us)
Async XLA Ops:
  2.9 17.7 %collective-permute-start.2 = (f32[96,896]{1,0:T(8,128)S(1)}, f32[96,896]{1,0:T(8,128)S(1)}, u32[]{:S(2)}, u32[]{:S(2)}) collective-permute-start(f32[96,896]{1,0:T(8,128)S(1)} %get-tuple-element.175), channel_id=1, source_target_pairs={{0,2},{1,3},{2,0},{3,1},{4,6},{5,7},{6,4},{7,5},{8,10},{9,11},{10,... | collective-permute-start | bytes 1032200 | tf_op jit(solution)/shard_map/ppermute | solution.py:287
  5.9 19.3 %collective-permute-start.3 = (f32[96,896]{1,0:T(8,128)S(1)}, f32[96,896]{1,0:T(8,128)S(1)}, u32[]{:S(2)}, u32[]{:S(2)}) collective-permute-start(f32[96,896]{1,0:T(8,128)S(1)} %get-tuple-element.174), channel_id=1, source_target_pairs={{0,4},{1,5},{2,6},{3,7},{4,0},{5,1},{6,2},{7,3},{8,12},{9,13},{10,... | collective-permute-start | bytes 1032200 | tf_op jit(solution)/shard_map/ppermute | solution.py:287
  10.8 17.5 %collective-permute-start = (f32[392,256]{1,0:T(8,128)}, f32[392,256]{1,0:T(8,128)S(1)}, u32[]{:S(2)}, u32[]{:S(2)}) collective-permute-start(f32[392,256]{1,0:T(8,128)} %shard_map.110.refs_2_), channel_id=1, source_target_pairs={{0,1},{1,0},{2,4},{3,5},{4,2},{5,3},{6,7},{7,6},{8,9},{9,8},{10,12... | collective-permute-start | bytes 1204232 | tf_op jit(solution)/shard_map/ppermute | solution.py:287
  10.8 18.1 %collective-permute-start.1 = (f32[392,256]{1,0:T(8,128)}, f32[392,256]{1,0:T(8,128)S(1)}, u32[]{:S(2)}, u32[]{:S(2)}) collective-permute-start(f32[392,256]{1,0:T(8,128)} %shard_map.110.refs_2_), channel_id=1, source_target_pairs={{0,1},{1,0},{2,3},{3,2},{4,5},{5,4},{6,7},{7,6},{8,9},{9,8},{10,11... | collective-permute-start | bytes 1204232 | tf_op jit(solution)/shard_map/ppermute | solution.py:287
  25.2 15.5 %collective-permute-start.5 = (f32[192,896]{1,0:T(8,128)S(1)}, f32[192,896]{1,0:T(8,128)S(1)}, u32[]{:S(2)}, u32[]{:S(2)}) collective-permute-start(f32[192,896]{1,0:T(8,128)S(1)} %shard_map.111.refs_1_.refs_0_), channel_id=1, source_target_pairs={{0,8},{1,9},{2,10},{3,11},{4,12},{5,13},{6,14},{7,15},{8,0},{9,1},... | collective-permute-start | bytes 2064392 | tf_op jit(solution)/shard_map/ppermute | solution.py:287
  26.8 13.9 %collective-permute-start.6 = (f32[192,896]{1,0:T(8,128)S(1)}, f32[192,896]{1,0:T(8,128)S(1)}, u32[]{:S(2)}, u32[]{:S(2)}) collective-permute-start(f32[192,896]{1,0:T(8,128)S(1)} %shard_map.111.refs_1_.refs_0_), channel_id=1, source_target_pairs={{0,16},{1,17},{2,18},{3,19},{4,20},{5,21},{6,22},{7,23},{8,24},{9,... | collective-permute-start | bytes 2064392 | tf_op jit(solution)/shard_map/ppermute | solution.py:287
  28.3 12.4 %collective-permute-start.7 = (f32[96,896]{1,0:T(8,128)}, f32[96,896]{1,0:T(8,128)S(1)}, u32[]{:S(2)}, u32[]{:S(2)}) collective-permute-start(f32[96,896]{1,0:T(8,128)} %get-tuple-element.90), channel_id=1, source_target_pairs={{0,3},{1,2},{2,1},{3,0},{4,7},{5,6},{6,5},{7,4},{8,11},{9,10},{10,... | collective-permute-start | bytes 1032200 | tf_op jit(solution)/shard_map/ppermute | solution.py:287
  28.3 0.6 copy-start.6
  28.9 18.1 %collective-permute-start.4 = (f32[96,896]{1,0:T(8,128)}, f32[96,896]{1,0:T(8,128)S(1)}, u32[]{:S(2)}, u32[]{:S(2)}) collective-permute-start(f32[96,896]{1,0:T(8,128)} %get-tuple-element.89), channel_id=1, source_target_pairs={{0,5},{1,4},{2,7},{3,6},{4,1},{5,0},{6,3},{7,2},{8,13},{9,12},{10,... | collective-permute-start | bytes 1032200 | tf_op jit(solution)/shard_map/ppermute | solution.py:287
  40.7 6.3 %copy-start.7 = (f32[8,128]{1,0:T(8,128)S(1)}, f32[8,128]{1,0:T(8,128)}, u32[]{:S(2)}) copy-start(f32[8,128]{1,0:T(8,128)} %copy-done.6) | copy-start | bytes 12292
  40.7 7.7 %slice-start = ((s8[7340032]{0:T(1024)(128)(4,1)}), s8[4194304]{0:T(1024)(128)(4,1)S(1)}, s32[]{:S(2)}) async-start(s8[7340032]{0:T(1024)(128)(4,1)} %bitcast.7), calls=%async_computation.1 | async-start | bytes 8388608
  40.7 7.7 %slice-start.2 = ((s8[5505024]{0:T(1024)(128)(4,1)}), s8[4194304]{0:T(1024)(128)(4,1)S(1)}, s32[]{:S(2)}) async-start(s8[5505024]{0:T(1024)(128)(4,1)} %bitcast.10), calls=%async_computation.3 | async-start | bytes 8388608
  40.8 7.6 %slice-start.1 = ((s8[7340032]{0:T(1024)(128)(4,1)}), s8[3145728]{0:T(1024)(128)(4,1)S(1)}, s32[]{:S(2)}) async-start(s8[7340032]{0:T(1024)(128)(4,1)} %bitcast.7), calls=%async_computation.2 | async-start | bytes 6291456
  40.8 7.6 %slice-start.3 = ((s8[5505024]{0:T(1024)(128)(4,1)}), s8[1310720]{0:T(1024)(128)(4,1)S(1)}, s32[]{:S(2)}) async-start(s8[5505024]{0:T(1024)(128)(4,1)} %bitcast.10), calls=%async_computation.4 | async-start | bytes 2621440
  40.9 15.7 %collective-permute-start.10 = (f32[192,896]{1,0:T(8,128)S(1)}, f32[192,896]{1,0:T(8,128)S(1)}, u32[]{:S(2)}, u32[]{:S(2)}) collective-permute-start(f32[192,896]{1,0:T(8,128)S(1)} %get-tuple-element.105), channel_id=1, source_target_pairs={{0,16},{1,17},{2,18},{3,19},{4,20},{5,21},{6,22},{7,23},{8,24},{9,... | collective-permute-start | bytes 2064392 | tf_op jit(solution)/shard_map/ppermute | solution.py:287
  40.9 15.7 %collective-permute-start.9 = (f32[192,896]{1,0:T(8,128)S(1)}, f32[192,896]{1,0:T(8,128)S(1)}, u32[]{:S(2)}, u32[]{:S(2)}) collective-permute-start(f32[192,896]{1,0:T(8,128)S(1)} %get-tuple-element.99.refs_1_.refs_4_), channel_id=1, source_target_pairs={{0,8},{1,9},{2,10},{3,11},{4,12},{5,13},{6,14},{7,15},{8,0},{9,1},... | collective-permute-start | bytes 2064392 | tf_op jit(solution)/shard_map/ppermute | solution.py:287
  47.0 13.2 %collective-permute-start.8 = (f32[96,896]{1,0:T(8,128)S(1)}, f32[96,896]{1,0:T(8,128)S(1)}, u32[]{:S(2)}, u32[]{:S(2)}) collective-permute-start(f32[96,896]{1,0:T(8,128)S(1)} %get-tuple-element.101), channel_id=1, source_target_pairs={{0,6},{1,7},{2,4},{3,5},{4,2},{5,3},{6,0},{7,1},{8,14},{9,15},{10,... | collective-permute-start | bytes 1032200 | tf_op jit(solution)/shard_map/ppermute | solution.py:287
  52.9 5.8 %copy-start = (f32[392,256]{1,0:T(8,128)S(1)}, f32[392,256]{1,0:T(8,128)}, u32[]{:S(2)}) copy-start(f32[392,256]{1,0:T(8,128)} %shard_map.110.refs_2_) | copy-start | bytes 1204228
  56.7 15.6 %collective-permute-start.12 = (f32[144,896]{1,0:T(8,128)S(1)}, f32[144,896]{1,0:T(8,128)S(1)}, u32[]{:S(2)}, u32[]{:S(2)}) collective-permute-start(f32[144,896]{1,0:T(8,128)S(1)} %get-tuple-element.112.refs_1_.refs_4_), channel_id=1, source_target_pairs={{0,8},{1,9},{2,10},{3,11},{4,12},{5,13},{6,14},{7,15},{8,0},{9,1},... | collective-permute-start | bytes 1548296 | tf_op jit(solution)/shard_map/ppermute | solution.py:287
  57.0 15.3 %collective-permute-start.13 = (f32[144,896]{1,0:T(8,128)S(1)}, f32[144,896]{1,0:T(8,128)S(1)}, u32[]{:S(2)}, u32[]{:S(2)}) collective-permute-start(f32[144,896]{1,0:T(8,128)S(1)} %get-tuple-element.115), channel_id=1, source_target_pairs={{0,16},{1,17},{2,18},{3,19},{4,20},{5,21},{6,22},{7,23},{8,24},{9,... | collective-permute-start | bytes 1548296 | tf_op jit(solution)/shard_map/ppermute | solution.py:287
  58.7 13.6 %collective-permute-start.15 = (f32[384,896]{1,0:T(8,128)S(1)}, f32[384,896]{1,0:T(8,128)S(1)}, u32[]{:S(2)}, u32[]{:S(2)}) collective-permute-start(f32[384,896]{1,0:T(8,128)S(1)} %get-tuple-element.117), channel_id=1, source_target_pairs={{0,1},{1,0},{2,3},{3,2},{4,5},{5,4},{6,7},{7,6},{8,9},{9,8},{10,11... | collective-permute-start | bytes 4128776 | tf_op jit(solution)/shard_map/ppermute | solution.py:287
  58.7 11.7 %collective-permute-start.14 = (f32[392,256]{1,0:T(8,128)S(1)}, f32[392,256]{1,0:T(8,128)S(1)}, u32[]{:S(2)}, u32[]{:S(2)}) collective-permute-start(f32[392,256]{1,0:T(8,128)S(1)} %copy-done), channel_id=1, source_target_pairs={{0,2},{1,3},{2,0},{3,1},{4,6},{5,7},{6,4},{7,5},{8,10},{9,11},{10,... | collective-permute-start | bytes 1204232 | tf_op jit(solution)/shard_map/ppermute | solution.py:287
  60.2 19.3 %collective-permute-start.11 = (f32[96,896]{1,0:T(8,128)S(1)}, f32[96,896]{1,0:T(8,128)S(1)}, u32[]{:S(2)}, u32[]{:S(2)}) collective-permute-start(f32[96,896]{1,0:T(8,128)S(1)} %get-tuple-element.114), channel_id=1, source_target_pairs={{0,7},{1,6},{2,5},{3,4},{4,3},{5,2},{6,1},{7,0},{8,15},{9,14},{10,... | collective-permute-start | bytes 1032200 | tf_op jit(solution)/shard_map/ppermute | solution.py:287
  70.4 17.9 %collective-permute-start.23 = (f32[392,256]{1,0:T(8,128)S(1)}, f32[392,256]{1,0:T(8,128)S(1)}, u32[]{:S(2)}, u32[]{:S(2)}) collective-permute-start(f32[392,256]{1,0:T(8,128)S(1)} %collective-permute-done.refs_0_), channel_id=1, source_target_pairs={{0,2},{1,3},{2,0},{3,1},{4,6},{5,7},{6,4},{7,5},{8,10},{9,11},{10,... | collective-permute-start | bytes 1204232 | tf_op jit(solution)/shard_map/ppermute | solution.py:287
  72.4 12.8 %collective-permute-start.16 = (f32[144,896]{1,0:T(8,128)S(1)}, f32[144,896]{1,0:T(8,128)S(1)}, u32[]{:S(2)}, u32[]{:S(2)}) collective-permute-start(f32[144,896]{1,0:T(8,128)S(1)} %get-tuple-element.123.refs_1_.refs_0_), channel_id=1, source_target_pairs={{0,8},{1,9},{2,10},{3,11},{4,12},{5,13},{6,14},{7,15},{8,0},{9,1},... | collective-permute-start | bytes 1548296 | tf_op jit(solution)/shard_map/ppermute | solution.py:287
  74.2 5.8 %copy-start.1 = (bf16[384,256]{1,0:T(8,128)(2,1)S(1)}, bf16[384,256]{1,0:T(8,128)(2,1)}, u32[]{:S(2)}) copy-start(bf16[384,256]{1,0:T(8,128)(2,1)} %gate_ref.2) | copy-start | bytes 589828
  74.2 5.8 %copy-start.2 = (bf16[384,256]{1,0:T(8,128)(2,1)S(1)}, bf16[384,256]{1,0:T(8,128)(2,1)}, u32[]{:S(2)}) copy-start(bf16[384,256]{1,0:T(8,128)(2,1)} %up_ref.3) | copy-start | bytes 589828
  74.2 5.8 %copy-start.3 = (f32[384]{0:T(512)S(1)}, f32[384]{0:T(512)}, u32[]{:S(2)}) copy-start(f32[384]{0:T(512)} %prob_ref.3) | copy-start | bytes 4612
  74.2 5.8 %copy-start.4 = (s32[384]{0:T(512)S(1)}, s32[384]{0:T(512)}, u32[]{:S(2)}) copy-start(s32[384]{0:T(512)} %token_ref.3) | copy-start | bytes 4612
  74.2 5.8 %copy-start.5 = (s32[3]{0:T(128)S(1)}, s32[3]{0:T(128)}, u32[]{:S(2)}) copy-start(s32[3]{0:T(128)} %expert_ref.3) | copy-start | bytes 40
  74.2 12.5 %collective-permute-start.17 = (f32[144,896]{1,0:T(8,128)S(1)}, f32[144,896]{1,0:T(8,128)S(1)}, u32[]{:S(2)}, u32[]{:S(2)}) collective-permute-start(f32[144,896]{1,0:T(8,128)S(1)} %get-tuple-element.126), channel_id=1, source_target_pairs={{0,16},{1,17},{2,18},{3,19},{4,20},{5,21},{6,22},{7,23},{8,24},{9,... | collective-permute-start | bytes 1548296 | tf_op jit(solution)/shard_map/ppermute | solution.py:287
  74.6 7.5 %collective-permute-start.18 = (f32[392,256]{1,0:T(8,128)S(1)}, f32[392,256]{1,0:T(8,128)S(1)}, u32[]{:S(2)}, u32[]{:S(2)}) collective-permute-start(f32[392,256]{1,0:T(8,128)S(1)} %collective-permute-done.14.refs_9_), channel_id=1, source_target_pairs={{0,1},{1,0},{2,3},{3,2},{4,5},{5,4},{6,7},{7,6},{8,9},{9,8},{10,11... | collective-permute-start | bytes 1204232 | tf_op jit(solution)/shard_map/ppermute | solution.py:287
  79.5 8.0 %collective-permute-start.22 = (f32[392,256]{1,0:T(8,128)S(1)}, f32[392,256]{1,0:T(8,128)S(1)}, u32[]{:S(2)}, u32[]{:S(2)}) collective-permute-start(f32[392,256]{1,0:T(8,128)S(1)} %collective-permute-done.14.refs_9_), channel_id=1, source_target_pairs={{0,1},{1,0},{2,4},{3,5},{4,2},{5,3},{6,7},{7,6},{8,9},{9,8},{10,12... | collective-permute-start | bytes 1204232 | tf_op jit(solution)/shard_map/ppermute | solution.py:287
  86.8 11.8 %collective-permute-start.19 = (f32[144,896]{1,0:T(8,128)S(1)}, f32[144,896]{1,0:T(8,128)S(1)}, u32[]{:S(2)}, u32[]{:S(2)}) collective-permute-start(f32[144,896]{1,0:T(8,128)S(1)} %get-tuple-element.136.refs_1_.refs_5_), channel_id=1, source_target_pairs={{0,8},{1,9},{2,10},{3,11},{4,12},{5,13},{6,14},{7,15},{8,0},{9,1},... | collective-permute-start | bytes 1548296 | tf_op jit(solution)/shard_map/ppermute | solution.py:287
  87.2 11.5 %collective-permute-start.20 = (f32[144,896]{1,0:T(8,128)S(1)}, f32[144,896]{1,0:T(8,128)S(1)}, u32[]{:S(2)}, u32[]{:S(2)}) collective-permute-start(f32[144,896]{1,0:T(8,128)S(1)} %get-tuple-element.137), channel_id=1, source_target_pairs={{0,16},{1,17},{2,18},{3,19},{4,20},{5,21},{6,22},{7,23},{8,24},{9,... | collective-permute-start | bytes 1548296 | tf_op jit(solution)/shard_map/ppermute | solution.py:287
  88.3 10.3 %collective-permute-start.21 = (f32[8,384]{1,0:T(8,128)S(1)}, f32[8,384]{1,0:T(8,128)S(1)}, u32[]{:S(2)}, u32[]{:S(2)}) collective-permute-start(f32[8,384]{1,0:T(8,128)S(1)} %get-tuple-element.138), channel_id=1, source_target_pairs={{0,8},{1,9},{2,10},{3,11},{4,12},{5,13},{6,14},{7,15},{8,0},{9,1},... | collective-permute-start | bytes 36872 | tf_op jit(solution)/shard_map/ppermute | solution.py:287
  90.1 11.7 %collective-permute-start.26 = (f32[392,256]{1,0:T(8,128)S(1)}, f32[392,256]{1,0:T(8,128)S(1)}, u32[]{:S(2)}, u32[]{:S(2)}) collective-permute-start(f32[392,256]{1,0:T(8,128)S(1)} %collective-permute-done.22.refs_0_), channel_id=1, source_target_pairs={{0,2},{1,3},{2,0},{3,1},{4,6},{5,7},{6,4},{7,5},{8,10},{9,11},{10,... | collective-permute-start | bytes 1204232 | tf_op jit(solution)/shard_map/ppermute | solution.py:287
  93.7 8.2 %collective-permute-start.28 = (f32[392,256]{1,0:T(8,128)S(1)}, f32[392,256]{1,0:T(8,128)S(1)}, u32[]{:S(2)}, u32[]{:S(2)}) collective-permute-start(f32[392,256]{1,0:T(8,128)S(1)} %broadcast_select_fusion.refs_9_), channel_id=1, source_target_pairs={{0,1},{1,0},{2,3},{3,2},{4,5},{5,4},{6,7},{7,6},{8,9},{9,8},{10,11... | collective-permute-start | bytes 1204232 | tf_op jit(solution)/shard_map/ppermute | solution.py:287
  98.7 6.1 %collective-permute-start.24 = (f32[48,896]{1,0:T(8,128)S(1)}, f32[48,896]{1,0:T(8,128)S(1)}, u32[]{:S(2)}, u32[]{:S(2)}) collective-permute-start(f32[48,896]{1,0:T(8,128)S(1)} %get-tuple-element.145), channel_id=1, source_target_pairs={{0,8},{1,9},{2,10},{3,11},{4,12},{5,13},{6,14},{7,15},{8,0},{9,1},... | collective-permute-start | bytes 516104 | tf_op jit(solution)/shard_map/ppermute | solution.py:287
  100.2 5.4 %collective-permute-start.25 = (f32[48,896]{1,0:T(8,128)S(1)}, f32[48,896]{1,0:T(8,128)S(1)}, u32[]{:S(2)}, u32[]{:S(2)}) collective-permute-start(f32[48,896]{1,0:T(8,128)S(1)} %get-tuple-element.146), channel_id=1, source_target_pairs={{0,16},{1,17},{2,18},{3,19},{4,20},{5,21},{6,22},{7,23},{8,24},{9,... | collective-permute-start | bytes 516104 | tf_op jit(solution)/shard_map/ppermute | solution.py:287
  101.8 3.8 %collective-permute-start.27 = (f32[392,256]{1,0:T(8,128)S(1)}, f32[392,256]{1,0:T(8,128)S(1)}, u32[]{:S(2)}, u32[]{:S(2)}) collective-permute-start(f32[392,256]{1,0:T(8,128)S(1)} %broadcast_select_fusion.1.refs_8_), channel_id=1, source_target_pairs={{0,1},{1,0},{2,3},{3,2},{4,5},{5,4},{6,7},{7,6},{8,9},{9,8},{10,11... | collective-permute-start | bytes 1204232 | tf_op jit(solution)/shard_map/ppermute | solution.py:287
  103.2 8.2 %collective-permute-start.29 = (f32[8,384]{1,0:T(8,128)S(1)}, f32[8,384]{1,0:T(8,128)S(1)}, u32[]{:S(2)}, u32[]{:S(2)}) collective-permute-start(f32[8,384]{1,0:T(8,128)S(1)} %add.111), channel_id=1, source_target_pairs={{0,16},{1,17},{2,18},{3,19},{4,20},{5,21},{6,22},{7,23},{8,24},{9,... | collective-permute-start | bytes 36872 | tf_op jit(solution)/shard_map/ppermute | solution.py:287
  108.2 10.3 %all-to-all-start = ((f32[32,1,128]{2,1,0:T(1,128)}), f32[32,1,128]{2,1,0:T(1,128)S(1)}, u32[]{:S(2)}, u32[]{:S(2)}) async-start(f32[32,1,128]{2,1,0:T(1,128)} %bitcast.3), calls=%async_computation | async-start | bytes 32768 | tf_op jit(solution)/shard_map/all_to_all | solution.py:486

commit v6 on v5

--- a/solution.py
+++ b/solution.py
@@ -419,9 +419,11 @@
     )
     sent_4 = to_x
     x_4, y_4 = along_x(to_x), along_y(to_y)
+
+    mid_near, mid_own, out_own, partial_value = arrive(
+        mid_near, mid_own, out_own, partial_value, marked=(mid_near, to_x), flops=EARLY
+    )
     partial_value = partial_value + along_x(partial_value)
-
-    mid_near, mid_own, out_own = arrive(mid_near, mid_own, out_own, marked=(mid_near, to_x), flops=EARLY)
     out_near = outer_swap(mid_near)
     outer = (chip == 0) | (chip == chips - 1)
     factor_skip = jnp.where(outer, out_own, mid_near)

time: 119 us -> 119 us (level)
  no operation moved by 1% of the time
where the time goes in v6:
time: 119 us
  waiting for transfers between devices  49 us (41%)
  starting transfers between devices  37.9 us (32%)
  Pallas kernels  15.7 us (13%)
  local copies, waits for them, and re-layouts  10.1 us (8%)
  other arithmetic  5.33 us (4%)
    ppermute x30, waiting for transfers between devices, moved(): return lax.ppermute(value, ('blk', 'wide'), pairs)  44.8 us
    ppermute x30, starting transfers between devices, moved(): return lax.ppermute(value, ('blk', 'wide'), pairs)  34.8 us
    optimization_barrier x1, local copies, waits for them, and re-layouts, together(): return lax.optimization_barrier(values)  6.92 us
    pallas_call x5, Pallas kernels, add_products(): pl.pallas_call(kernel, out_shape=out_shape, in_specs=[pl.BlockSpec(memory...  6.45 us
    pallas_call x1, Pallas kernels, project(): pl.pallas_call(kernel, out_shape=jax.ShapeDtypeStruct((EXPERTS, rows, hid...  4.49 us
    all_to_all x1, waiting for transfers between devices, factors_body(): spread = lax.all_to_all(sums, ('blk', 'wide'), 0, 0, tiled=True)  4.16 us
    all_to_all x1, starting transfers between devices, factors_body(): spread = lax.all_to_all(sums, ('blk', 'wide'), 0, 0, tiled=True)  3.17 us
  transfers between devices with their start and end apart: 31, of which 15 were waited for; matrix products, arithmetic and copies ran while one was open for 10% of the time, Pallas kernels for 13%

profile of v6, /device:TPU:0, one launch (start us, length us, event | category | flops | bytes accessed | tf_op | source)
XLA Modules:
  0.0 119.1 jit_solution(11745842825620689912)
XLA Ops:
  0.7 2.2 %dynamic-slice_convert_fusion.2 = (f32[96,896]{1,0:T(8,128)}, f32[96,896]{1,0:T(8,128)S(1)}, f32[96,896]{1,0:T(8,128)S(1)}, f32[96,896]{1,0:T(8,128)}) fusion(bf16[384,7168]{1,0:T(8,128)(2,1)} %upstream_ref.1, s32[]{:T(128)S(6)} %select_n.77, s32[]{:T(128)S(6)} %select_n.83, s32[]{:T(128)S(6)} %select_n.82, s32[]{:T(128)S(6)} %select_n.81, s32[]{:T(128)S(6)} %select_n.80), kind=kLoop, calls=%fused_computation.7 | loop fusion | flops 344064 | bytes 2064404 | tf_op jit(solution)/shard_map/convert_element_type | solution.py:308
  2.9 3.0 %collective-permute-start.2 = (f32[96,896]{1,0:T(8,128)S(1)}, f32[96,896]{1,0:T(8,128)S(1)}, u32[]{:S(2)}, u32[]{:S(2)}) collective-permute-start(f32[96,896]{1,0:T(8,128)S(1)} %get-tuple-element.177), channel_id=1, source_target_pairs={{0,2},{1,3},{2,0},{3,1},{4,6},{5,7},{6,4},{7,5},{8,10},{9,11},{10,... | collective-permute-start | bytes 1032200 | tf_op jit(solution)/shard_map/ppermute | solution.py:287
  5.9 2.6 %collective-permute-start.3 = (f32[96,896]{1,0:T(8,128)S(1)}, f32[96,896]{1,0:T(8,128)S(1)}, u32[]{:S(2)}, u32[]{:S(2)}) collective-permute-start(f32[96,896]{1,0:T(8,128)S(1)} %get-tuple-element.176), channel_id=1, source_target_pairs={{0,4},{1,5},{2,6},{3,7},{4,0},{5,1},{6,2},{7,3},{8,12},{9,13},{10,... | collective-permute-start | bytes 1032200 | tf_op jit(solution)/shard_map/ppermute | solution.py:287
  8.5 2.3 %shard_map.110.refs_2_ = f32[392,256]{1,0:T(8,128)} custom-call(s32[3]{0:T(128)} %expert_ref.3, s32[1]{0:T(128)} %bitcast.index_ref, bf16[384,256]{1,0:T(8,128)(2,1)} %gate_ref.2, bf16[384,256]{1,0:T(8,128)(2,1)} %up_ref.3, f32[384]{0:T(512)} %prob_ref.3, s32[384]{0:T(512)} %token_ref.3), custom_call_target="tpu_custom_call" | custom-call | flops 75497472 | bytes 1179648 | tf_op jit(solution)/shard_map/pallas_call | solution.py:206
  10.8 0.5 collective-permute-start.1
  11.3 6.9 %copy.16 = bf16[7168,2,256]{2,0,1:T(8,128)(2,1)} copy(bf16[7168,2,256]{2,1,0:T(2,128)(2,1)} %param.10) | data formatting | bytes 14680064 | tf_op jit(solution)/shard_map/optimization_barrier | solution.py:263
  18.2 2.3 %collective-permute-done.2.refs_0_ = f32[96,896]{1,0:T(8,128)S(1)} collective-permute-done((f32[96,896]{1,0:T(8,128)S(1)}, f32[96,896]{1,0:T(8,128)S(1)}, u32[]{:S(2)}, u32[]{:S(2)}) %collective-permute-start.2) | collective-permute-done | bytes 344096 | tf_op jit(solution)/shard_map/ppermute | solution.py:287
  20.6 4.6 %collective-permute-done.3.refs_1_ = f32[96,896]{1,0:T(8,128)S(1)} collective-permute-done((f32[96,896]{1,0:T(8,128)S(1)}, f32[96,896]{1,0:T(8,128)S(1)}, u32[]{:S(2)}, u32[]{:S(2)}) %collective-permute-start.3) | collective-permute-done | bytes 344096 | tf_op jit(solution)/shard_map/ppermute | solution.py:287
  25.2 1.6 %collective-permute-start.5 = (f32[192,896]{1,0:T(8,128)S(1)}, f32[192,896]{1,0:T(8,128)S(1)}, u32[]{:S(2)}, u32[]{:S(2)}) collective-permute-start(f32[192,896]{1,0:T(8,128)S(1)} %shard_map.111.refs_1_.refs_0_), channel_id=1, source_target_pairs={{0,8},{1,9},{2,10},{3,11},{4,12},{5,13},{6,14},{7,15},{8,0},{9,1},... | collective-permute-start | bytes 2064392 | tf_op jit(solution)/shard_map/ppermute | solution.py:287
  26.8 1.5 %collective-permute-start.6 = (f32[192,896]{1,0:T(8,128)S(1)}, f32[192,896]{1,0:T(8,128)S(1)}, u32[]{:S(2)}, u32[]{:S(2)}) collective-permute-start(f32[192,896]{1,0:T(8,128)S(1)} %shard_map.111.refs_1_.refs_0_), channel_id=1, source_target_pairs={{0,16},{1,17},{2,18},{3,19},{4,20},{5,21},{6,22},{7,23},{8,24},{9,... | collective-permute-start | bytes 2064392 | tf_op jit(solution)/shard_map/ppermute | solution.py:287
  28.3 0.6 copy-done.6
  28.9 3.9 %collective-permute-start.4 = (f32[96,896]{1,0:T(8,128)}, f32[96,896]{1,0:T(8,128)S(1)}, u32[]{:S(2)}, u32[]{:S(2)}) collective-permute-start(f32[96,896]{1,0:T(8,128)} %get-tuple-element.90), channel_id=1, source_target_pairs={{0,5},{1,4},{2,7},{3,6},{4,1},{5,0},{6,3},{7,2},{8,13},{9,12},{10,... | collective-permute-start | bytes 1032200 | tf_op jit(solution)/shard_map/ppermute | solution.py:287
  32.8 1.7 %fusion.1 = (bf16[96,896]{1,0:T(8,128)(2,1)S(1)}, bf16[96,896]{1,0:T(8,128)(2,1)S(1)}, bf16[96,896]{1,0:T(8,128)(2,1)S(1)}, bf16[96,896]{1,0:T(8,128)(2,1)S(1)},...) fusion(bf16[384,7168]{1,0:T(8,128)(2,1)} %upstream_ref.1, ...), kind=kLoop, calls=%fused_computation.14 | loop fusion | flops 172032 | bytes 3784736 | tf_op jit(solution)/shard_map/dynamic_slice | solution.py:324
  34.7 6.0 %collective-permute-done.7.refs_0_ = f32[96,896]{1,0:T(8,128)S(1)} collective-permute-done((f32[96,896]{1,0:T(8,128)}, f32[96,896]{1,0:T(8,128)S(1)}, u32[]{:S(2)}, u32[]{:S(2)}) %collective-permute-start.7) | collective-permute-done | bytes 344096 | tf_op jit(solution)/shard_map/ppermute | solution.py:287
  41.0 6.0 %collective-permute-done.4.refs_0_ = f32[96,896]{1,0:T(8,128)S(1)} collective-permute-done((f32[96,896]{1,0:T(8,128)}, f32[96,896]{1,0:T(8,128)S(1)}, u32[]{:S(2)}, u32[]{:S(2)}) %collective-permute-start.4) | collective-permute-done | bytes 344096 | tf_op jit(solution)/shard_map/ppermute | solution.py:287
  47.0 1.4 %collective-permute-start.8 = (f32[96,896]{1,0:T(8,128)S(1)}, f32[96,896]{1,0:T(8,128)S(1)}, u32[]{:S(2)}, u32[]{:S(2)}) collective-permute-start(f32[96,896]{1,0:T(8,128)S(1)} %get-tuple-element.102), channel_id=1, source_target_pairs={{0,6},{1,7},{2,4},{3,5},{4,2},{5,3},{6,0},{7,1},{8,14},{9,15},{10,... | collective-permute-start | bytes 1032200 | tf_op jit(solution)/shard_map/ppermute | solution.py:287
  48.4 4.5 %shard_map.115.both_ref = f32[2,384,256]{2,1,0:T(8,128)S(1)} custom-call(bf16[384,7168]{1,0:T(8,128)(2,1)S(1)} %bitcast.11, bf16[2,7168,256]{2,1,0:T(8,128)(2,1)S(1)} %bitcast.9), custom_call_target="tpu_custom_call" | custom-call | flops 2818572288 | bytes 12845056 | tf_op jit(solution)/shard_map/pallas_call | solution.py:152
  52.9 3.6 %collective-permute-done.10.refs_1_.refs_3_.refs_6_ = f32[192,896]{1,0:T(8,128)S(1)} collective-permute-done((f32[192,896]{1,0:T(8,128)S(1)}, f32[192,896]{1,0:T(8,128)S(1)}, u32[]{:S(2)}, u32[]{:S(2)}) %collective-permute-start.10) | collective-permute-done | bytes 688160 | tf_op jit(solution)/shard_map/ppermute | solution.py:287
  57.0 1.7 %collective-permute-start.13 = (f32[144,896]{1,0:T(8,128)S(1)}, f32[144,896]{1,0:T(8,128)S(1)}, u32[]{:S(2)}, u32[]{:S(2)}) collective-permute-start(f32[144,896]{1,0:T(8,128)S(1)} %get-tuple-element.116), channel_id=1, source_target_pairs={{0,16},{1,17},{2,18},{3,19},{4,20},{5,21},{6,22},{7,23},{8,24},{9,... | collective-permute-start | bytes 1548296 | tf_op jit(solution)/shard_map/ppermute | solution.py:287
  58.7 1.5 %collective-permute-start.14 = (f32[392,256]{1,0:T(8,128)S(1)}, f32[392,256]{1,0:T(8,128)S(1)}, u32[]{:S(2)}, u32[]{:S(2)}) collective-permute-start(f32[392,256]{1,0:T(8,128)S(1)} %copy-done), channel_id=1, source_target_pairs={{0,2},{1,3},{2,0},{3,1},{4,6},{5,7},{6,4},{7,5},{8,10},{9,11},{10,... | collective-permute-start | bytes 1204232 | tf_op jit(solution)/shard_map/ppermute | solution.py:287
  60.2 2.3 %collective-permute-start.11 = (f32[96,896]{1,0:T(8,128)S(1)}, f32[96,896]{1,0:T(8,128)S(1)}, u32[]{:S(2)}, u32[]{:S(2)}) collective-permute-start(f32[96,896]{1,0:T(8,128)S(1)} %get-tuple-element.115), channel_id=1, source_target_pairs={{0,7},{1,6},{2,5},{3,4},{4,3},{5,2},{6,1},{7,0},{8,15},{9,14},{10,... | collective-permute-start | bytes 1032200 | tf_op jit(solution)/shard_map/ppermute | solution.py:287
  62.5 7.9 %collective-permute-done.14.refs_9_ = f32[392,256]{1,0:T(8,128)S(1)} collective-permute-done((f32[392,256]{1,0:T(8,128)S(1)}, f32[392,256]{1,0:T(8,128)S(1)}, u32[]{:S(2)}, u32[]{:S(2)}) %collective-permute-start.14) | collective-permute-done | bytes 401440 | tf_op jit(solution)/shard_map/ppermute | solution.py:287
  70.4 1.9 %collective-permute-start.22 = (f32[392,256]{1,0:T(8,128)S(1)}, f32[392,256]{1,0:T(8,128)S(1)}, u32[]{:S(2)}, u32[]{:S(2)}) collective-permute-start(f32[392,256]{1,0:T(8,128)S(1)} %collective-permute-done.refs_0_), channel_id=1, source_target_pairs={{0,2},{1,3},{2,0},{3,1},{4,6},{5,7},{6,4},{7,5},{8,10},{9,11},{10,... | collective-permute-start | bytes 1204232 | tf_op jit(solution)/shard_map/ppermute | solution.py:287
  72.4 1.8 %collective-permute-start.16 = (f32[144,896]{1,0:T(8,128)S(1)}, f32[144,896]{1,0:T(8,128)S(1)}, u32[]{:S(2)}, u32[]{:S(2)}) collective-permute-start(f32[144,896]{1,0:T(8,128)S(1)} %get-tuple-element.124.refs_1_.refs_0_), channel_id=1, source_target_pairs={{0,8},{1,9},{2,10},{3,11},{4,12},{5,13},{6,14},{7,15},{8,0},{9,1},... | collective-permute-start | bytes 1548296 | tf_op jit(solution)/shard_map/ppermute | solution.py:287
  74.2 0.4 collective-permute-start.17
  74.6 4.9 %collective-permute-done.11.refs_0_ = f32[96,896]{1,0:T(8,128)S(1)} collective-permute-done((f32[96,896]{1,0:T(8,128)S(1)}, f32[96,896]{1,0:T(8,128)S(1)}, u32[]{:S(2)}, u32[]{:S(2)}) %collective-permute-start.11) | collective-permute-done | bytes 344096 | tf_op jit(solution)/shard_map/ppermute | solution.py:287
  79.5 0.5 collective-permute-start.21
  80.0 2.1 %shard_map.120 = (bf16[384,256]{1,0:T(8,128)(2,1)}, bf16[384,256]{1,0:T(8,128)(2,1)}, f32[8,384]{1,0:T(8,128)S(1)}) custom-call(s32[3]{0:T(128)S(1)} %copy-done.5, f32[2,384,256]{2,1,0:T(8,128)S(1)} %shard_map.115.both_ref, bf16[384,256]{1,0:T(8,128)(2,1)S(1)} %copy-done.1, bf16[384,256]{1,0:T(8,128)(2,1)S(1)} %copy-done.2, f32[384]{0:T(512)S(1)} %copy-done.3, ...), custom_call_target="tpu_custom_call" | custom-call | flops 226492416 | bytes 1966080 | tf_op jit(solution)/shard_map/pallas_call | solution.py:248
  82.1 3.1 %collective-permute-done.16.refs_2_.refs_8_.refs_1_ = f32[144,896]{1,0:T(8,128)S(1)} collective-permute-done((f32[144,896]{1,0:T(8,128)S(1)}, f32[144,896]{1,0:T(8,128)S(1)}, u32[]{:S(2)}, u32[]{:S(2)}) %collective-permute-start.16) | collective-permute-done | bytes 516128 | tf_op jit(solution)/shard_map/ppermute | solution.py:287
  85.2 1.5 %collective-permute-done.17.refs_1_.refs_7_.refs_2_ = f32[144,896]{1,0:T(8,128)S(1)} collective-permute-done((f32[144,896]{1,0:T(8,128)S(1)}, f32[144,896]{1,0:T(8,128)S(1)}, u32[]{:S(2)}, u32[]{:S(2)}) %collective-permute-start.17) | collective-permute-done | bytes 516128 | tf_op jit(solution)/shard_map/ppermute | solution.py:287
  87.5 0.8 collective-permute-done.22
  88.3 1.7 %collective-permute-start.23 = (f32[8,384]{1,0:T(8,128)S(1)}, f32[8,384]{1,0:T(8,128)S(1)}, u32[]{:S(2)}, u32[]{:S(2)}) collective-permute-start(f32[8,384]{1,0:T(8,128)S(1)} %get-tuple-element.143), channel_id=1, source_target_pairs={{0,8},{1,9},{2,10},{3,11},{4,12},{5,13},{6,14},{7,15},{8,0},{9,1},... | collective-permute-start | bytes 36872 | tf_op jit(solution)/shard_map/ppermute | solution.py:287
  90.1 3.6 %collective-permute-start.26 = (f32[392,256]{1,0:T(8,128)S(1)}, f32[392,256]{1,0:T(8,128)S(1)}, u32[]{:S(2)}, u32[]{:S(2)}) collective-permute-start(f32[392,256]{1,0:T(8,128)S(1)} %collective-permute-done.21.refs_0_), channel_id=1, source_target_pairs={{0,2},{1,3},{2,0},{3,1},{4,6},{5,7},{6,4},{7,5},{8,10},{9,11},{10,... | collective-permute-start | bytes 1204232 | tf_op jit(solution)/shard_map/ppermute | solution.py:287
  94.0 1.3 %shard_map.125.refs_11_ = f32[896,512]{1,0:T(8,128)S(1)} custom-call(f32[384,896]{1,0:T(8,128)S(1)} %get-tuple-element.156.refs_0_, f32[384,896]{1,0:T(8,128)S(1)} %collective-permute-done.15.refs_1_, f32[392,256]{1,0:T(8,128)S(1)} %copy-done, f32[392,256]{1,0:T(8,128)S(1)} %collective-permute-done.1.refs_3_, f32[896,512]{1,0:T(8,128)S(1)} %broadcast_in_dim.3.refs_4_), custom_call_target="tpu_custom_call" | custom-call | flops 704643072 | bytes 7208960 | tf_op jit(solution)/shard_map/pallas_call | solution.py:72
  95.3 1.3 %shard_map.126.refs_11_ = f32[896,512]{1,0:T(8,128)S(1)} custom-call(f32[192,896]{1,0:T(8,128)S(1)} %shard_map.111.refs_1_.refs_0_, f32[192,896]{1,0:T(8,128)S(1)} %collective-permute-done.5.refs_2_.refs_1_, f32[192,896]{1,0:T(8,128)S(1)} %collective-permute-done.6.refs_1_.refs_2_, f32[192,896]{1,0:T(8,128)S(1)} %collective-permute-done.10.refs_1_.refs_3_.refs_6_, ...), custom_call_target="tpu_custom_call" | custom-call | flops 704643072 | bytes 7208960 | tf_op jit(solution)/shard_map/pallas_call | solution.py:72
  96.6 2.0 %collective-permute-done.23 = f32[8,384]{1,0:T(8,128)S(1)} collective-permute-done((f32[8,384]{1,0:T(8,128)S(1)}, f32[8,384]{1,0:T(8,128)S(1)}, u32[]{:S(2)}, u32[]{:S(2)}) %collective-permute-start.23) | collective-permute-done | bytes 12320 | tf_op jit(solution)/shard_map/ppermute | solution.py:287
  98.7 1.5 %collective-permute-start.24 = (f32[48,896]{1,0:T(8,128)S(1)}, f32[48,896]{1,0:T(8,128)S(1)}, u32[]{:S(2)}, u32[]{:S(2)}) collective-permute-start(f32[48,896]{1,0:T(8,128)S(1)} %get-tuple-element.147), channel_id=1, source_target_pairs={{0,8},{1,9},{2,10},{3,11},{4,12},{5,13},{6,14},{7,15},{8,0},{9,1},... | collective-permute-start | bytes 516104 | tf_op jit(solution)/shard_map/ppermute | solution.py:287
  100.6 1.2 %collective-permute-done.26 = f32[392,256]{1,0:T(8,128)S(1)} collective-permute-done((f32[392,256]{1,0:T(8,128)S(1)}, f32[392,256]{1,0:T(8,128)S(1)}, u32[]{:S(2)}, u32[]{:S(2)}) %collective-permute-start.26) | collective-permute-done | bytes 401440 | tf_op jit(solution)/shard_map/ppermute | solution.py:287
  101.9 1.3 %shard_map.127.refs_10_ = f32[896,512]{1,0:T(8,128)S(1)} custom-call(f32[192,896]{1,0:T(8,128)S(1)} %shard_map.111.refs_1_.refs_0_, f32[192,896]{1,0:T(8,128)S(1)} %collective-permute-done.5.refs_2_.refs_1_, f32[192,896]{1,0:T(8,128)S(1)} %collective-permute-done.6.refs_1_.refs_2_, f32[192,896]{1,0:T(8,128)S(1)} %collective-permute-done.9.refs_2_.refs_5_.refs_3_, ...), custom_call_target="tpu_custom_call" | custom-call | flops 704643072 | bytes 7208960 | tf_op jit(solution)/shard_map/pallas_call | solution.py:72
  103.2 1.6 %collective-permute-start.29 = (f32[8,384]{1,0:T(8,128)S(1)}, f32[8,384]{1,0:T(8,128)S(1)}, u32[]{:S(2)}, u32[]{:S(2)}) collective-permute-start(f32[8,384]{1,0:T(8,128)S(1)} %add.111), channel_id=1, source_target_pairs={{0,16},{1,17},{2,18},{3,19},{4,20},{5,21},{6,22},{7,23},{8,24},{9,... | collective-permute-start | bytes 36872 | tf_op jit(solution)/shard_map/ppermute | solution.py:287
  104.8 0.8 collective-permute-done.25.refs_1_.refs_0_
  105.6 1.3 %shard_map.128.refs_3_ = f32[896,512]{1,0:T(8,128)S(1)} custom-call(f32[144,896]{1,0:T(8,128)S(1)} %get-tuple-element.124.refs_1_.refs_0_, f32[144,896]{1,0:T(8,128)S(1)} %collective-permute-done.16.refs_2_.refs_8_.refs_1_, f32[144,896]{1,0:T(8,128)S(1)} %collective-permute-done.17.refs_1_.refs_7_.refs_2_, ...), custom_call_target="tpu_custom_call" | custom-call | flops 616562688 | bytes 6766592 | tf_op jit(solution)/shard_map/pallas_call | solution.py:72
  106.9 1.3 %shard_map.129 = (f32[896,512]{1,0:T(8,128)S(1)}, f32[32,128]{1,0:T(8,128)}) custom-call(f32[48,896]{1,0:T(8,128)S(1)} %collective-permute-done.25.refs_1_.refs_0_, f32[48,896]{1,0:T(8,128)S(1)} %collective-permute-done.24.refs_0_.refs_1_, f32[392,256]{1,0:T(8,128)S(1)} %collective-permute-done.27.refs_9_.refs_2_, f32[896,512]{1,0:T(8,128)S(1)} %shard_map.128.refs_3_, ...), custom_call_target="tpu_custom_call" | custom-call | flops 88080384 | bytes 4112384 | tf_op jit(solution)/shard_map/pallas_call | solution.py:72
  108.2 3.2 %all-to-all-start = ((f32[32,1,128]{2,1,0:T(1,128)}), f32[32,1,128]{2,1,0:T(1,128)S(1)}, u32[]{:S(2)}, u32[]{:S(2)}) async-start(f32[32,1,128]{2,1,0:T(1,128)} %bitcast.3), calls=%async_computation | async-start | bytes 32768 | tf_op jit(solution)/shard_map/all_to_all | solution.py:488
  111.4 0.6 fusion
  112.0 2.4 %reshape.19 = f32[896,2,256]{2,1,0:T(2,128)} reshape(f32[896,512]{1,0:T(8,128)S(1)} %get-tuple-element.160) | data formatting | bytes 3670016 | tf_op jit(solution)/shard_map/reshape | solution.py:487
  114.4 4.2 %all-to-all-done = f32[32,1,128]{2,1,0:T(1,128)S(1)} async-done(((f32[32,1,128]{2,1,0:T(1,128)}), f32[32,1,128]{2,1,0:T(1,128)S(1)}, u32[]{:S(2)}, u32[]{:S(2)}) %all-to-all-start) | async-done | bytes 16416 | tf_op jit(solution)/shard_map/all_to_all | solution.py:488
  118.6 0.5 multiply_sqrt_fusion
  (72 shorter events, 2.9 us)
Async XLA Ops:
  2.9 17.7 %collective-permute-start.2 = (f32[96,896]{1,0:T(8,128)S(1)}, f32[96,896]{1,0:T(8,128)S(1)}, u32[]{:S(2)}, u32[]{:S(2)}) collective-permute-start(f32[96,896]{1,0:T(8,128)S(1)} %get-tuple-element.177), channel_id=1, source_target_pairs={{0,2},{1,3},{2,0},{3,1},{4,6},{5,7},{6,4},{7,5},{8,10},{9,11},{10,... | collective-permute-start | bytes 1032200 | tf_op jit(solution)/shard_map/ppermute | solution.py:287
  5.9 19.3 %collective-permute-start.3 = (f32[96,896]{1,0:T(8,128)S(1)}, f32[96,896]{1,0:T(8,128)S(1)}, u32[]{:S(2)}, u32[]{:S(2)}) collective-permute-start(f32[96,896]{1,0:T(8,128)S(1)} %get-tuple-element.176), channel_id=1, source_target_pairs={{0,4},{1,5},{2,6},{3,7},{4,0},{5,1},{6,2},{7,3},{8,12},{9,13},{10,... | collective-permute-start | bytes 1032200 | tf_op jit(solution)/shard_map/ppermute | solution.py:287
  10.8 17.5 %collective-permute-start = (f32[392,256]{1,0:T(8,128)}, f32[392,256]{1,0:T(8,128)S(1)}, u32[]{:S(2)}, u32[]{:S(2)}) collective-permute-start(f32[392,256]{1,0:T(8,128)} %shard_map.110.refs_2_), channel_id=1, source_target_pairs={{0,1},{1,0},{2,4},{3,5},{4,2},{5,3},{6,7},{7,6},{8,9},{9,8},{10,12... | collective-permute-start | bytes 1204232 | tf_op jit(solution)/shard_map/ppermute | solution.py:287
  10.8 18.1 %collective-permute-start.1 = (f32[392,256]{1,0:T(8,128)}, f32[392,256]{1,0:T(8,128)S(1)}, u32[]{:S(2)}, u32[]{:S(2)}) collective-permute-start(f32[392,256]{1,0:T(8,128)} %shard_map.110.refs_2_), channel_id=1, source_target_pairs={{0,1},{1,0},{2,3},{3,2},{4,5},{5,4},{6,7},{7,6},{8,9},{9,8},{10,11... | collective-permute-start | bytes 1204232 | tf_op jit(solution)/shard_map/ppermute | solution.py:287
  25.2 15.5 %collective-permute-start.5 = (f32[192,896]{1,0:T(8,128)S(1)}, f32[192,896]{1,0:T(8,128)S(1)}, u32[]{:S(2)}, u32[]{:S(2)}) collective-permute-start(f32[192,896]{1,0:T(8,128)S(1)} %shard_map.111.refs_1_.refs_0_), channel_id=1, source_target_pairs={{0,8},{1,9},{2,10},{3,11},{4,12},{5,13},{6,14},{7,15},{8,0},{9,1},... | collective-permute-start | bytes 2064392 | tf_op jit(solution)/shard_map/ppermute | solution.py:287
  26.8 13.9 %collective-permute-start.6 = (f32[192,896]{1,0:T(8,128)S(1)}, f32[192,896]{1,0:T(8,128)S(1)}, u32[]{:S(2)}, u32[]{:S(2)}) collective-permute-start(f32[192,896]{1,0:T(8,128)S(1)} %shard_map.111.refs_1_.refs_0_), channel_id=1, source_target_pairs={{0,16},{1,17},{2,18},{3,19},{4,20},{5,21},{6,22},{7,23},{8,24},{9,... | collective-permute-start | bytes 2064392 | tf_op jit(solution)/shard_map/ppermute | solution.py:287
  28.3 12.4 %collective-permute-start.7 = (f32[96,896]{1,0:T(8,128)}, f32[96,896]{1,0:T(8,128)S(1)}, u32[]{:S(2)}, u32[]{:S(2)}) collective-permute-start(f32[96,896]{1,0:T(8,128)} %get-tuple-element.91), channel_id=1, source_target_pairs={{0,3},{1,2},{2,1},{3,0},{4,7},{5,6},{6,5},{7,4},{8,11},{9,10},{10,... | collective-permute-start | bytes 1032200 | tf_op jit(solution)/shard_map/ppermute | solution.py:287
  28.3 0.6 copy-start.6
  28.9 18.1 %collective-permute-start.4 = (f32[96,896]{1,0:T(8,128)}, f32[96,896]{1,0:T(8,128)S(1)}, u32[]{:S(2)}, u32[]{:S(2)}) collective-permute-start(f32[96,896]{1,0:T(8,128)} %get-tuple-element.90), channel_id=1, source_target_pairs={{0,5},{1,4},{2,7},{3,6},{4,1},{5,0},{6,3},{7,2},{8,13},{9,12},{10,... | collective-permute-start | bytes 1032200 | tf_op jit(solution)/shard_map/ppermute | solution.py:287
  40.7 6.3 %copy-start.7 = (f32[8,128]{1,0:T(8,128)S(1)}, f32[8,128]{1,0:T(8,128)}, u32[]{:S(2)}) copy-start(f32[8,128]{1,0:T(8,128)} %copy-done.6) | copy-start | bytes 12292
  40.7 7.7 %slice-start = ((s8[7340032]{0:T(1024)(128)(4,1)}), s8[4194304]{0:T(1024)(128)(4,1)S(1)}, s32[]{:S(2)}) async-start(s8[7340032]{0:T(1024)(128)(4,1)} %bitcast.7), calls=%async_computation.1 | async-start | bytes 8388608
  40.7 7.7 %slice-start.2 = ((s8[5505024]{0:T(1024)(128)(4,1)}), s8[4194304]{0:T(1024)(128)(4,1)S(1)}, s32[]{:S(2)}) async-start(s8[5505024]{0:T(1024)(128)(4,1)} %bitcast.10), calls=%async_computation.3 | async-start | bytes 8388608
  40.8 7.6 %slice-start.1 = ((s8[7340032]{0:T(1024)(128)(4,1)}), s8[3145728]{0:T(1024)(128)(4,1)S(1)}, s32[]{:S(2)}) async-start(s8[7340032]{0:T(1024)(128)(4,1)} %bitcast.7), calls=%async_computation.2 | async-start | bytes 6291456
  40.8 7.6 %slice-start.3 = ((s8[5505024]{0:T(1024)(128)(4,1)}), s8[1310720]{0:T(1024)(128)(4,1)S(1)}, s32[]{:S(2)}) async-start(s8[5505024]{0:T(1024)(128)(4,1)} %bitcast.10), calls=%async_computation.4 | async-start | bytes 2621440
  40.9 15.7 %collective-permute-start.10 = (f32[192,896]{1,0:T(8,128)S(1)}, f32[192,896]{1,0:T(8,128)S(1)}, u32[]{:S(2)}, u32[]{:S(2)}) collective-permute-start(f32[192,896]{1,0:T(8,128)S(1)} %get-tuple-element.106), channel_id=1, source_target_pairs={{0,16},{1,17},{2,18},{3,19},{4,20},{5,21},{6,22},{7,23},{8,24},{9,... | collective-permute-start | bytes 2064392 | tf_op jit(solution)/shard_map/ppermute | solution.py:287
  40.9 15.7 %collective-permute-start.9 = (f32[192,896]{1,0:T(8,128)S(1)}, f32[192,896]{1,0:T(8,128)S(1)}, u32[]{:S(2)}, u32[]{:S(2)}) collective-permute-start(f32[192,896]{1,0:T(8,128)S(1)} %get-tuple-element.100.refs_1_.refs_4_), channel_id=1, source_target_pairs={{0,8},{1,9},{2,10},{3,11},{4,12},{5,13},{6,14},{7,15},{8,0},{9,1},... | collective-permute-start | bytes 2064392 | tf_op jit(solution)/shard_map/ppermute | solution.py:287
  47.0 13.2 %collective-permute-start.8 = (f32[96,896]{1,0:T(8,128)S(1)}, f32[96,896]{1,0:T(8,128)S(1)}, u32[]{:S(2)}, u32[]{:S(2)}) collective-permute-start(f32[96,896]{1,0:T(8,128)S(1)} %get-tuple-element.102), channel_id=1, source_target_pairs={{0,6},{1,7},{2,4},{3,5},{4,2},{5,3},{6,0},{7,1},{8,14},{9,15},{10,... | collective-permute-start | bytes 1032200 | tf_op jit(solution)/shard_map/ppermute | solution.py:287
  52.9 5.8 %copy-start = (f32[392,256]{1,0:T(8,128)S(1)}, f32[392,256]{1,0:T(8,128)}, u32[]{:S(2)}) copy-start(f32[392,256]{1,0:T(8,128)} %shard_map.110.refs_2_) | copy-start | bytes 1204228
  56.7 15.6 %collective-permute-start.12 = (f32[144,896]{1,0:T(8,128)S(1)}, f32[144,896]{1,0:T(8,128)S(1)}, u32[]{:S(2)}, u32[]{:S(2)}) collective-permute-start(f32[144,896]{1,0:T(8,128)S(1)} %get-tuple-element.113.refs_1_.refs_4_), channel_id=1, source_target_pairs={{0,8},{1,9},{2,10},{3,11},{4,12},{5,13},{6,14},{7,15},{8,0},{9,1},... | collective-permute-start | bytes 1548296 | tf_op jit(solution)/shard_map/ppermute | solution.py:287
  57.0 15.3 %collective-permute-start.13 = (f32[144,896]{1,0:T(8,128)S(1)}, f32[144,896]{1,0:T(8,128)S(1)}, u32[]{:S(2)}, u32[]{:S(2)}) collective-permute-start(f32[144,896]{1,0:T(8,128)S(1)} %get-tuple-element.116), channel_id=1, source_target_pairs={{0,16},{1,17},{2,18},{3,19},{4,20},{5,21},{6,22},{7,23},{8,24},{9,... | collective-permute-start | bytes 1548296 | tf_op jit(solution)/shard_map/ppermute | solution.py:287
  58.7 13.6 %collective-permute-start.15 = (f32[384,896]{1,0:T(8,128)S(1)}, f32[384,896]{1,0:T(8,128)S(1)}, u32[]{:S(2)}, u32[]{:S(2)}) collective-permute-start(f32[384,896]{1,0:T(8,128)S(1)} %get-tuple-element.118), channel_id=1, source_target_pairs={{0,1},{1,0},{2,3},{3,2},{4,5},{5,4},{6,7},{7,6},{8,9},{9,8},{10,11... | collective-permute-start | bytes 4128776 | tf_op jit(solution)/shard_map/ppermute | solution.py:287
  58.7 11.7 %collective-permute-start.14 = (f32[392,256]{1,0:T(8,128)S(1)}, f32[392,256]{1,0:T(8,128)S(1)}, u32[]{:S(2)}, u32[]{:S(2)}) collective-permute-start(f32[392,256]{1,0:T(8,128)S(1)} %copy-done), channel_id=1, source_target_pairs={{0,2},{1,3},{2,0},{3,1},{4,6},{5,7},{6,4},{7,5},{8,10},{9,11},{10,... | collective-permute-start | bytes 1204232 | tf_op jit(solution)/shard_map/ppermute | solution.py:287
  60.2 19.3 %collective-permute-start.11 = (f32[96,896]{1,0:T(8,128)S(1)}, f32[96,896]{1,0:T(8,128)S(1)}, u32[]{:S(2)}, u32[]{:S(2)}) collective-permute-start(f32[96,896]{1,0:T(8,128)S(1)} %get-tuple-element.115), channel_id=1, source_target_pairs={{0,7},{1,6},{2,5},{3,4},{4,3},{5,2},{6,1},{7,0},{8,15},{9,14},{10,... | collective-permute-start | bytes 1032200 | tf_op jit(solution)/shard_map/ppermute | solution.py:287
  70.4 17.9 %collective-permute-start.22 = (f32[392,256]{1,0:T(8,128)S(1)}, f32[392,256]{1,0:T(8,128)S(1)}, u32[]{:S(2)}, u32[]{:S(2)}) collective-permute-start(f32[392,256]{1,0:T(8,128)S(1)} %collective-permute-done.refs_0_), channel_id=1, source_target_pairs={{0,2},{1,3},{2,0},{3,1},{4,6},{5,7},{6,4},{7,5},{8,10},{9,11},{10,... | collective-permute-start | bytes 1204232 | tf_op jit(solution)/shard_map/ppermute | solution.py:287
  72.4 12.8 %collective-permute-start.16 = (f32[144,896]{1,0:T(8,128)S(1)}, f32[144,896]{1,0:T(8,128)S(1)}, u32[]{:S(2)}, u32[]{:S(2)}) collective-permute-start(f32[144,896]{1,0:T(8,128)S(1)} %get-tuple-element.124.refs_1_.refs_0_), channel_id=1, source_target_pairs={{0,8},{1,9},{2,10},{3,11},{4,12},{5,13},{6,14},{7,15},{8,0},{9,1},... | collective-permute-start | bytes 1548296 | tf_op jit(solution)/shard_map/ppermute | solution.py:287
  74.2 5.8 %copy-start.1 = (bf16[384,256]{1,0:T(8,128)(2,1)S(1)}, bf16[384,256]{1,0:T(8,128)(2,1)}, u32[]{:S(2)}) copy-start(bf16[384,256]{1,0:T(8,128)(2,1)} %gate_ref.2) | copy-start | bytes 589828
  74.2 5.8 %copy-start.2 = (bf16[384,256]{1,0:T(8,128)(2,1)S(1)}, bf16[384,256]{1,0:T(8,128)(2,1)}, u32[]{:S(2)}) copy-start(bf16[384,256]{1,0:T(8,128)(2,1)} %up_ref.3) | copy-start | bytes 589828
  74.2 5.8 %copy-start.3 = (f32[384]{0:T(512)S(1)}, f32[384]{0:T(512)}, u32[]{:S(2)}) copy-start(f32[384]{0:T(512)} %prob_ref.3) | copy-start | bytes 4612
  74.2 5.8 %copy-start.4 = (s32[384]{0:T(512)S(1)}, s32[384]{0:T(512)}, u32[]{:S(2)}) copy-start(s32[384]{0:T(512)} %token_ref.3) | copy-start | bytes 4612
  74.2 5.8 %copy-start.5 = (s32[3]{0:T(128)S(1)}, s32[3]{0:T(128)}, u32[]{:S(2)}) copy-start(s32[3]{0:T(128)} %expert_ref.3) | copy-start | bytes 40
  74.2 12.5 %collective-permute-start.17 = (f32[144,896]{1,0:T(8,128)S(1)}, f32[144,896]{1,0:T(8,128)S(1)}, u32[]{:S(2)}, u32[]{:S(2)}) collective-permute-start(f32[144,896]{1,0:T(8,128)S(1)} %get-tuple-element.127), channel_id=1, source_target_pairs={{0,16},{1,17},{2,18},{3,19},{4,20},{5,21},{6,22},{7,23},{8,24},{9,... | collective-permute-start | bytes 1548296 | tf_op jit(solution)/shard_map/ppermute | solution.py:287
  74.6 7.5 %collective-permute-start.18 = (f32[392,256]{1,0:T(8,128)S(1)}, f32[392,256]{1,0:T(8,128)S(1)}, u32[]{:S(2)}, u32[]{:S(2)}) collective-permute-start(f32[392,256]{1,0:T(8,128)S(1)} %collective-permute-done.14.refs_9_), channel_id=1, source_target_pairs={{0,1},{1,0},{2,3},{3,2},{4,5},{5,4},{6,7},{7,6},{8,9},{9,8},{10,11... | collective-permute-start | bytes 1204232 | tf_op jit(solution)/shard_map/ppermute | solution.py:287
  79.5 8.0 %collective-permute-start.21 = (f32[392,256]{1,0:T(8,128)S(1)}, f32[392,256]{1,0:T(8,128)S(1)}, u32[]{:S(2)}, u32[]{:S(2)}) collective-permute-start(f32[392,256]{1,0:T(8,128)S(1)} %collective-permute-done.14.refs_9_), channel_id=1, source_target_pairs={{0,1},{1,0},{2,4},{3,5},{4,2},{5,3},{6,7},{7,6},{8,9},{9,8},{10,12... | collective-permute-start | bytes 1204232 | tf_op jit(solution)/shard_map/ppermute | solution.py:287
  86.8 11.8 %collective-permute-start.19 = (f32[144,896]{1,0:T(8,128)S(1)}, f32[144,896]{1,0:T(8,128)S(1)}, u32[]{:S(2)}, u32[]{:S(2)}) collective-permute-start(f32[144,896]{1,0:T(8,128)S(1)} %get-tuple-element.137.refs_1_.refs_5_), channel_id=1, source_target_pairs={{0,8},{1,9},{2,10},{3,11},{4,12},{5,13},{6,14},{7,15},{8,0},{9,1},... | collective-permute-start | bytes 1548296 | tf_op jit(solution)/shard_map/ppermute | solution.py:287
  87.2 11.5 %collective-permute-start.20 = (f32[144,896]{1,0:T(8,128)S(1)}, f32[144,896]{1,0:T(8,128)S(1)}, u32[]{:S(2)}, u32[]{:S(2)}) collective-permute-start(f32[144,896]{1,0:T(8,128)S(1)} %get-tuple-element.138), channel_id=1, source_target_pairs={{0,16},{1,17},{2,18},{3,19},{4,20},{5,21},{6,22},{7,23},{8,24},{9,... | collective-permute-start | bytes 1548296 | tf_op jit(solution)/shard_map/ppermute | solution.py:287
  88.3 10.3 %collective-permute-start.23 = (f32[8,384]{1,0:T(8,128)S(1)}, f32[8,384]{1,0:T(8,128)S(1)}, u32[]{:S(2)}, u32[]{:S(2)}) collective-permute-start(f32[8,384]{1,0:T(8,128)S(1)} %get-tuple-element.143), channel_id=1, source_target_pairs={{0,8},{1,9},{2,10},{3,11},{4,12},{5,13},{6,14},{7,15},{8,0},{9,1},... | collective-permute-start | bytes 36872 | tf_op jit(solution)/shard_map/ppermute | solution.py:287
  90.1 11.7 %collective-permute-start.26 = (f32[392,256]{1,0:T(8,128)S(1)}, f32[392,256]{1,0:T(8,128)S(1)}, u32[]{:S(2)}, u32[]{:S(2)}) collective-permute-start(f32[392,256]{1,0:T(8,128)S(1)} %collective-permute-done.21.refs_0_), channel_id=1, source_target_pairs={{0,2},{1,3},{2,0},{3,1},{4,6},{5,7},{6,4},{7,5},{8,10},{9,11},{10,... | collective-permute-start | bytes 1204232 | tf_op jit(solution)/shard_map/ppermute | solution.py:287
  93.7 8.2 %collective-permute-start.28 = (f32[392,256]{1,0:T(8,128)S(1)}, f32[392,256]{1,0:T(8,128)S(1)}, u32[]{:S(2)}, u32[]{:S(2)}) collective-permute-start(f32[392,256]{1,0:T(8,128)S(1)} %broadcast_select_fusion.refs_9_), channel_id=1, source_target_pairs={{0,1},{1,0},{2,3},{3,2},{4,5},{5,4},{6,7},{7,6},{8,9},{9,8},{10,11... | collective-permute-start | bytes 1204232 | tf_op jit(solution)/shard_map/ppermute | solution.py:287
  98.7 6.1 %collective-permute-start.24 = (f32[48,896]{1,0:T(8,128)S(1)}, f32[48,896]{1,0:T(8,128)S(1)}, u32[]{:S(2)}, u32[]{:S(2)}) collective-permute-start(f32[48,896]{1,0:T(8,128)S(1)} %get-tuple-element.147), channel_id=1, source_target_pairs={{0,8},{1,9},{2,10},{3,11},{4,12},{5,13},{6,14},{7,15},{8,0},{9,1},... | collective-permute-start | bytes 516104 | tf_op jit(solution)/shard_map/ppermute | solution.py:287
  100.2 5.4 %collective-permute-start.25 = (f32[48,896]{1,0:T(8,128)S(1)}, f32[48,896]{1,0:T(8,128)S(1)}, u32[]{:S(2)}, u32[]{:S(2)}) collective-permute-start(f32[48,896]{1,0:T(8,128)S(1)} %get-tuple-element.148), channel_id=1, source_target_pairs={{0,16},{1,17},{2,18},{3,19},{4,20},{5,21},{6,22},{7,23},{8,24},{9,... | collective-permute-start | bytes 516104 | tf_op jit(solution)/shard_map/ppermute | solution.py:287
  101.8 3.8 %collective-permute-start.27 = (f32[392,256]{1,0:T(8,128)S(1)}, f32[392,256]{1,0:T(8,128)S(1)}, u32[]{:S(2)}, u32[]{:S(2)}) collective-permute-start(f32[392,256]{1,0:T(8,128)S(1)} %broadcast_select_fusion.1.refs_8_), channel_id=1, source_target_pairs={{0,1},{1,0},{2,3},{3,2},{4,5},{5,4},{6,7},{7,6},{8,9},{9,8},{10,11... | collective-permute-start | bytes 1204232 | tf_op jit(solution)/shard_map/ppermute | solution.py:287
  103.2 8.2 %collective-permute-start.29 = (f32[8,384]{1,0:T(8,128)S(1)}, f32[8,384]{1,0:T(8,128)S(1)}, u32[]{:S(2)}, u32[]{:S(2)}) collective-permute-start(f32[8,384]{1,0:T(8,128)S(1)} %add.111), channel_id=1, source_target_pairs={{0,16},{1,17},{2,18},{3,19},{4,20},{5,21},{6,22},{7,23},{8,24},{9,... | collective-permute-start | bytes 36872 | tf_op jit(solution)/shard_map/ppermute | solution.py:287
  108.2 10.3 %all-to-all-start = ((f32[32,1,128]{2,1,0:T(1,128)}), f32[32,1,128]{2,1,0:T(1,128)S(1)}, u32[]{:S(2)}, u32[]{:S(2)}) async-start(f32[32,1,128]{2,1,0:T(1,128)} %bitcast.3), calls=%async_computation | async-start | bytes 32768 | tf_op jit(solution)/shard_map/all_to_all | solution.py:488
